TPU v7x, 512 devices: a whole 4x4x16 slice. The times are simulated.
512 devices in a mesh: lat: 16 (over y, x_lo, core), lon: 32 (over z, x_hi).
Axes of the slice: x: 4 (x_hi: 2, x_lo: 2; x = x_hi * 2 + x_lo), y: 4, z: 16, core: 2. Of those that a mesh axis runs over, the one named last changes fastest.
Arguments:
- field: float32 [69, 240, 1440], P(None, 'lat', 'lon'), may hold values from -6 to 6
- w_first: float32 [9, 128, 69], replicated, may hold values from -0.25 to 0.25
- b_first: float32 [128], replicated, may hold values from -3 to 3
- w_second: float32 [9, 128, 128], replicated, may hold values from -0.1875 to 0.1875
- b_second: float32 [128], replicated, may hold values from -3 to 3
- modes: float32 [512, 128], replicated, may hold values from -0.5 to 0.5
- cotangent: float32 [512], replicated, may hold values from -6 to 6
Outputs:
- grad_field: float32 [69, 240, 1440], P(None, 'lat', 'lon')
- grad_w_first: float32 [9, 128, 69], replicated
- grad_b_first: float32 [128], replicated
- grad_w_second: float32 [9, 128, 128], replicated
- grad_b_second: float32 [128], replicated
- grad_modes: float32 [512, 128], replicated
All inputs are finite; a program needn't handle non-finite values.
Results may differ from a plain program's by a relative error of at most 0.00014.
Values sent between devices are 32-bit elements; how exact they have to be, the bound alone decides.
No kernel may reach another device: no remote copies, remote signals or barrier semaphores. Data moves between devices by JAX's collectives and lax.ppermute only.
A program may use at most 64 MiB of HBM per device.

v0:
```python
import math

import jax
import jax.numpy as jnp
from jax import lax
from jax.sharding import PartitionSpec as P


def padded_2(cells, sides, width, closed):
    for axis, dim in sides:
        count = lax.axis_size(axis)
        ends = count if closed else count - 1
        head = lax.slice_in_dim(cells, 0, width, axis=dim)
        tail = lax.slice_in_dim(cells, cells.shape[dim] - width, cells.shape[dim], axis=dim)
        cells = jnp.concatenate(
            [
                lax.ppermute(tail, axis, [(i, (i + 1) % count) for i in range(ends)]),
                cells,
                lax.ppermute(head, axis, [((i + 1) % count, i) for i in range(ends)]),
            ],
            axis=dim,
        )
    return cells


def extend(values, width):
    rowed = padded_2(values, (("lat", 1),), width, False)
    return padded_2(rowed, (("lon", 2),), width, True)


def convolve(padded, weight, rows, cols):
    total = None
    for tap in range(9):
        shift_a, shift_b = (tap // 3, tap % 3)
        term = jnp.einsum(
            "oc,chw->ohw",
            weight[tap],
            padded[:, shift_a : shift_a + rows, shift_b : shift_b + cols],
            precision=lax.Precision.HIGHEST,
        )
        total = term if total is None else total + term
    return total


def transpose_conv(padded, weight, rows, cols):
    total = None
    for tap in range(9):
        shift_a, shift_b = (2 - tap // 3, 2 - tap % 3)
        term = jnp.einsum(
            "oc,ohw->chw",
            weight[tap],
            padded[:, shift_a : shift_a + rows, shift_b : shift_b + cols],
            precision=lax.Precision.HIGHEST,
        )
        total = term if total is None else total + term
    return total


def kernel_grad(grad, padded, rows, cols):
    pieces = []
    for tap in range(9):
        shift_a, shift_b = (tap // 3, tap % 3)
        pieces.append(
            jnp.einsum(
                "ohw,chw->oc",
                grad,
                padded[:, shift_a : shift_a + rows, shift_b : shift_b + cols],
                precision=lax.Precision.HIGHEST,
            )
        )
    return jnp.stack(pieces, axis=0)


def slope(pre):
    sigma = jax.nn.sigmoid(pre)
    return sigma * (1.0 + pre * (1.0 - sigma))


def row_weights(first, count, nlat, nlon):
    every = (jnp.arange(nlat, dtype=jnp.float32) + 0.5) * (math.pi / nlat) - math.pi / 2
    total = jnp.sum(jnp.cos(every)) * nlon
    global_rows = first + jnp.arange(count, dtype=jnp.int32)
    phi = (global_rows.astype(jnp.float32) + 0.5) * (math.pi / nlat) - math.pi / 2
    inside = (global_rows >= 0) & (global_rows < nlat)
    return (jnp.where(inside, jnp.cos(phi), 0.0) / total, inside)


def pool_modes(active_two, weights, modes, cotangent):
    local_sum = jnp.einsum("chw,h->c", active_two, weights, precision=lax.Precision.HIGHEST)
    pooled = lax.psum(local_sum, ("lat", "lon"))
    amplitude = jnp.dot(modes, pooled, precision=lax.Precision.HIGHEST)
    spread = jnp.sqrt(jnp.mean(amplitude * amplitude) + 1e-05)
    normal = amplitude / spread
    d_amplitude = (cotangent - normal * jnp.mean(cotangent * normal)) / spread
    d_modes = d_amplitude[:, None] * pooled[None, :]
    d_pooled = jnp.dot(d_amplitude, modes, precision=lax.Precision.HIGHEST)
    return (d_modes, d_pooled)


def body(field, w_first, b_first, w_second, b_second, modes, cotangent):
    channels, rows, cols = field.shape
    nlat = rows * lax.axis_size("lat")
    nlon = cols * lax.axis_size("lon")
    first_row = lax.axis_index("lat") * rows
    field_pad = extend(field, 1)
    hidden_one = convolve(field_pad, w_first, rows, cols) + b_first[:, None, None]
    active_pad = extend(jax.nn.silu(hidden_one), 1)
    hidden_two = convolve(active_pad, w_second, rows, cols) + b_second[:, None, None]
    weights, inside = row_weights(first_row, rows, nlat, nlon)
    d_modes, d_pooled = pool_modes(jax.nn.silu(hidden_two), weights, modes, cotangent)
    grad_two = d_pooled[:, None, None] * weights[None, :, None] * slope(hidden_two)
    grad_two_pad = extend(grad_two, 1)
    grad_w_second = kernel_grad(grad_two, active_pad, rows, cols)
    grad_b_second = jnp.sum(grad_two, axis=(1, 2))
    grad_one = transpose_conv(grad_two_pad, w_second, rows, cols) * slope(hidden_one)
    grad_w_first = kernel_grad(grad_one, field_pad, rows, cols)
    grad_b_first = jnp.sum(grad_one, axis=(1, 2))
    grad_one_pad = extend(grad_one, 1)
    grad_field = transpose_conv(grad_one_pad, w_first, rows, cols) * float(nlat * nlon)
    grad_w_first, grad_b_first, grad_w_second, grad_b_second = lax.psum(
        (grad_w_first, grad_b_first, grad_w_second, grad_b_second), ("lat", "lon")
    )
    return (grad_field, grad_w_first, grad_b_first, grad_w_second, grad_b_second, d_modes)


def solution(mesh):
    in_specs = (P(None, "lat", "lon"), P(), P(), P(), P(), P(), P())
    out_specs = (P(None, "lat", "lon"), P(), P(), P(), P(), P())
    return jax.shard_map(body, mesh=mesh, in_specs=in_specs, out_specs=out_specs, check_vma=False)
```

profile of v0, /device:TPU:1, one launch (start us, length us, event | category | flops | bytes accessed | tf_op | source)
XLA Modules:
  0.0 687.2 jit_solution(9247502093767110232)
XLA Ops:
  7.2 0.8 fusion.240
  8.0 4.5 collective-permute-start
  12.5 5.6 collective-permute-start.1
  19.5 1.1 constant_dynamic-update-slice_fusion.3
  20.7 10.3 %collective-permute-start.3 = (f32[69,17,1]{0,2,1:T(1,128)S(1)}, f32[69,17,1]{0,2,1:T(1,128)S(1)}, u32[]{:S(2)}, u32[]{:S(2)}) collective-permute-start(f32[69,17,1]{0,2,1:T(1,128)S(1)} %get-tuple-element.25), channel_id=1, source_target_pairs={{1,0},{2,1},{3,2},{4,3},{5,4},{6,5},{7,6},{8,7},{9,8},{10,9},{11,1... | collective-permute-start | bytes 14084 | tf_op jit(solution)/shard_map/ppermute | solution.py:19
  31.0 1.9 collective-permute-start.2
  34.3 4.7 collective-permute-done.2
  42.6 3.8 collective-permute-start.4
  46.4 1.9 collective-permute-start.5
  48.8 2.7 collective-permute-done.5
  51.5 1.9 collective-permute-start.6
  53.5 7.0 %collective-permute-start.7 = (f32[128,17,1]{0,2,1:T(1,128)S(1)}, f32[128,17,1]{0,2,1:T(1,128)S(1)}, u32[]{:S(2)}, u32[]{:S(2)}) collective-permute-start(f32[128,17,1]{0,2,1:T(1,128)S(1)} %get-tuple-element.23), channel_id=1, source_target_pairs={{1,0},{2,1},{3,2},{4,3},{5,4},{6,5},{7,6},{8,7},{9,8},{10,9},{11,1... | collective-permute-start | bytes 26120 | tf_op jit(solution)/shard_map/ppermute | solution.py:19
  64.0 1.3 multiply_reduce_fusion
  65.5 106.1 %psum.35 = f32[128]{0:T(128)S(1)} all-reduce(f32[128]{0:T(128)S(1)} %convolution_bitcast_fusion.23), channel_id=1, replica_groups=mesh['lat'=16,'lon'=32] {'lat','lon'}, use_global_device_ids=true, to_apply=%region_2.3 | all-reduce | flops 128 | bytes 1024 | tf_op jit(solution)/shard_map/psum | solution.py:90
  175.4 1.2 fusion.235
  176.6 0.8 fusion.40
  177.8 0.8 fusion.39
  178.7 0.8 fusion.38
  179.5 0.8 fusion.37
  180.5 0.8 fusion.36
  181.3 0.8 fusion.35
  182.1 0.8 fusion.34
  183.0 0.8 fusion.33
  183.8 0.8 fusion.32
  184.6 2.6 collective-permute-start.9
  187.2 3.0 collective-permute-start.8
  190.2 0.8 broadcast_multiply_fusion
  191.2 2.9 collective-permute-start.10
  194.1 4.1 collective-permute-start.11
  199.1 3.1 collective-permute-done.11
  206.0 0.8 fusion.49
  207.8 0.8 fusion.47
  208.6 0.8 fusion.46
  209.4 0.8 fusion.45
  210.1 0.8 fusion.44
  210.9 0.8 fusion.43
  211.7 0.8 fusion.42
  212.5 2.3 collective-permute-start.13
  214.8 4.6 collective-permute-start.12
  219.4 0.8 fusion.41
  221.0 100.6 %all-reduce = (f32[128]{0:T(128)}, f32[128]{0:T(128)}) all-reduce(f32[128]{0:T(128)S(1)} %get-tuple-element.45, f32[128]{0:T(128)S(1)} %get-tuple-element.10), channel_id=1, replica_groups=mesh['lat'=16,'lon'=32] {'lat','lon'}, use_global_device_ids=true, to_apply=%region_7.8 | all-reduce | flops 256 | bytes 2048 | tf_op jit(solution)/shard_map/psum | solution.py:120
  321.6 4.5 collective-permute-start.14
  326.1 2.6 collective-permute-start.15
  329.6 4.5 collective-permute-done.15
  336.5 1.2 fusion.9
  337.7 340.1 %all-reduce.4.cloned.1.call-done = (f32[9,128,69]{1,2,0:T(8,128)}, f32[9,128,128]{2,1,0:T(8,128)}) async-done(((f32[9,128,69]{1,2,0:T(8,128)}, f32[9,128,128]{2,1,0:T(8,128)}), (f32[9,128,69]{1,2,0:T(8,128)}, f32[9,128,128]{2,1,0:T(8,128)})) %all-reduce.4.cloned.1.call-update) | async-done | bytes 907792 | tf_op jit(solution)/shard_map/psum | solution.py:120
  677.8 1.8 copy.35
  679.6 0.8 copy.36
  (100 shorter events, 22.5 us)
Async XLA Ops:
  7.2 164.4 %copy-start = (f32[512,128]{1,0:T(8,128)S(1)}, f32[512,128]{1,0:T(8,128)}, u32[]{:S(2)}) copy-start(f32[512,128]{1,0:T(8,128)} %param.12) | copy-start | bytes 786436
  7.2 670.6 %all-reduce.4.cloned.1.call-start = ((), (), s32[]{:S(2)}) async-start(), calls=%async_computation | async-start | bytes 1843200 | tf_op jit(solution)/shard_map/psum | solution.py:120
  8.0 11.4 %collective-permute-start = (f32[69,1,45]{0,2,1:T(8,128)S(1)}, f32[69,1,45]{0,2,1:T(8,128)S(1)}, u32[]{:S(2)}, u32[]{:S(2)}) collective-permute-start(f32[69,1,45]{0,2,1:T(8,128)S(1)} %get-tuple-element.36), channel_id=1, source_target_pairs={{0,32},{32,64},{64,96},{96,128},{128,160},{160,192},{192,224},{224... | collective-permute-start | bytes 37268 | tf_op jit(solution)/shard_map/ppermute | solution.py:17
  12.5 8.1 %collective-permute-start.1 = (f32[69,1,45]{0,2,1:T(8,128)S(1)}, f32[69,1,45]{0,2,1:T(8,128)S(1)}, u32[]{:S(2)}, u32[]{:S(2)}) collective-permute-start(f32[69,1,45]{0,2,1:T(8,128)S(1)} %get-tuple-element.35), channel_id=1, source_target_pairs={{32,0},{64,32},{96,64},{128,96},{160,128},{192,160},{224,192},{256... | collective-permute-start | bytes 37268 | tf_op jit(solution)/shard_map/ppermute | solution.py:19
  19.5 13.4 %copy-start.7 = (f32[9,128,69]{1,2,0:T(8,128)S(1)}, f32[9,128,69]{1,2,0:T(8,128)}, u32[]{:S(2)}) copy-start(f32[9,128,69]{1,2,0:T(8,128)} %param.8) | copy-start | bytes 953860
  20.6 12.8 %copy-start.3 = (f32[69,16,45]{0,2,1:T(8,128)}, f32[69,16,45]{0,2,1:T(8,128)S(1)}, u32[]{:S(2)}) copy-start(f32[69,16,45]{0,2,1:T(8,128)S(1)} %get-tuple-element.32) | copy-start | bytes 596164
  20.7 13.2 %collective-permute-start.3 = (f32[69,17,1]{0,2,1:T(1,128)S(1)}, f32[69,17,1]{0,2,1:T(1,128)S(1)}, u32[]{:S(2)}, u32[]{:S(2)}) collective-permute-start(f32[69,17,1]{0,2,1:T(1,128)S(1)} %get-tuple-element.25), channel_id=1, source_target_pairs={{1,0},{2,1},{3,2},{4,3},{5,4},{6,5},{7,6},{8,7},{9,8},{10,9},{11,1... | collective-permute-start | bytes 14084 | tf_op jit(solution)/shard_map/ppermute | solution.py:19
  31.0 8.0 %collective-permute-start.2 = (f32[69,17,1]{0,2,1:T(1,128)S(1)}, f32[69,17,1]{0,2,1:T(1,128)S(1)}, u32[]{:S(2)}, u32[]{:S(2)}) collective-permute-start(f32[69,17,1]{0,2,1:T(1,128)S(1)} %get-tuple-element.24), channel_id=1, source_target_pairs={{0,1},{1,2},{2,3},{3,4},{4,5},{5,6},{6,7},{7,8},{8,9},{9,10},{10,1... | collective-permute-start | bytes 14084 | tf_op jit(solution)/shard_map/ppermute | solution.py:17
  39.5 1.0 copy-start.1
  41.4 0.7 copy-start.14
  42.0 6.3 copy-start.2
  42.6 6.3 copy-start.5
  42.6 6.2 collective-permute-start.4
  46.4 5.1 collective-permute-start.5
  51.5 9.8 %collective-permute-start.6 = (f32[128,17,1]{0,2,1:T(1,128)S(1)}, f32[128,17,1]{0,2,1:T(1,128)S(1)}, u32[]{:S(2)}, u32[]{:S(2)}) collective-permute-start(f32[128,17,1]{0,2,1:T(1,128)S(1)} %get-tuple-element.22), channel_id=1, source_target_pairs={{0,1},{1,2},{2,3},{3,4},{4,5},{5,6},{6,7},{7,8},{8,9},{9,10},{10,1... | collective-permute-start | bytes 26120 | tf_op jit(solution)/shard_map/ppermute | solution.py:17
  53.5 7.9 %collective-permute-start.7 = (f32[128,17,1]{0,2,1:T(1,128)S(1)}, f32[128,17,1]{0,2,1:T(1,128)S(1)}, u32[]{:S(2)}, u32[]{:S(2)}) collective-permute-start(f32[128,17,1]{0,2,1:T(1,128)S(1)} %get-tuple-element.23), channel_id=1, source_target_pairs={{1,0},{2,1},{3,2},{4,3},{5,4},{6,5},{7,6},{8,7},{9,8},{10,9},{11,1... | collective-permute-start | bytes 26120 | tf_op jit(solution)/shard_map/ppermute | solution.py:19
  63.4 0.7 copy-start.13
  173.1 0.7 copy-start.12
  179.5 1.0 copy-start.6
  184.6 14.0 %copy-start.9 = (f32[9,128,128]{2,1,0:T(8,128)}, f32[9,128,128]{2,1,0:T(8,128)S(1)}, u32[]{:S(2)}) copy-start(f32[9,128,128]{2,1,0:T(8,128)S(1)} %fusion.32) | copy-start | bytes 1769476
  184.6 6.4 collective-permute-start.9
  187.2 3.9 collective-permute-start.8
  191.2 7.9 %collective-permute-start.10 = (f32[128,17,1]{0,2,1:T(1,128)S(1)}, f32[128,17,1]{0,2,1:T(1,128)S(1)}, u32[]{:S(2)}, u32[]{:S(2)}) collective-permute-start(f32[128,17,1]{0,2,1:T(1,128)S(1)} %get-tuple-element.18), channel_id=1, source_target_pairs={{1,0},{2,1},{3,2},{4,3},{5,4},{6,5},{7,6},{8,7},{9,8},{10,9},{11,1... | collective-permute-start | bytes 26120 | tf_op jit(solution)/shard_map/ppermute | solution.py:19
  194.1 8.1 %collective-permute-start.11 = (f32[128,17,1]{0,2,1:T(1,128)S(1)}, f32[128,17,1]{0,2,1:T(1,128)S(1)}, u32[]{:S(2)}, u32[]{:S(2)}) collective-permute-start(f32[128,17,1]{0,2,1:T(1,128)S(1)} %get-tuple-element.19), channel_id=1, source_target_pairs={{0,1},{1,2},{2,3},{3,4},{4,5},{5,6},{6,7},{7,8},{8,9},{9,10},{10,1... | collective-permute-start | bytes 26120 | tf_op jit(solution)/shard_map/ppermute | solution.py:17
  204.6 1.0 copy-start.8
  206.0 1.0 copy-start.4
  212.5 109.1 %collective-permute-start.13 = (f32[128,1,45]{0,2,1:T(8,128)S(1)}, f32[128,1,45]{0,2,1:T(8,128)S(1)}, u32[]{:S(2)}, u32[]{:S(2)}) collective-permute-start(f32[128,1,45]{0,2,1:T(8,128)S(1)} %get-tuple-element.27), channel_id=1, source_target_pairs={{32,0},{64,32},{96,64},{128,96},{160,128},{192,160},{224,192},{256... | collective-permute-start | bytes 69128 | tf_op jit(solution)/shard_map/ppermute | solution.py:19
  214.8 106.8 %collective-permute-start.12 = (f32[128,1,45]{0,2,1:T(8,128)S(1)}, f32[128,1,45]{0,2,1:T(8,128)S(1)}, u32[]{:S(2)}, u32[]{:S(2)}) collective-permute-start(f32[128,1,45]{0,2,1:T(8,128)S(1)} %get-tuple-element.26), channel_id=1, source_target_pairs={{0,32},{32,64},{64,96},{96,128},{128,160},{160,192},{192,224},{224... | collective-permute-start | bytes 69128 | tf_op jit(solution)/shard_map/ppermute | solution.py:17
  220.2 0.7 copy-start.11
  321.6 8.0 %collective-permute-start.14 = (f32[128,17,1]{0,2,1:T(1,128)S(1)}, f32[128,17,1]{0,2,1:T(1,128)S(1)}, u32[]{:S(2)}, u32[]{:S(2)}) collective-permute-start(f32[128,17,1]{0,2,1:T(1,128)S(1)} %get-tuple-element.14), channel_id=1, source_target_pairs={{1,0},{2,1},{3,2},{4,3},{5,4},{6,5},{7,6},{8,7},{9,8},{10,9},{11,1... | collective-permute-start | bytes 26120 | tf_op jit(solution)/shard_map/ppermute | solution.py:19
  326.1 8.0 %collective-permute-start.15 = (f32[128,17,1]{0,2,1:T(1,128)S(1)}, f32[128,17,1]{0,2,1:T(1,128)S(1)}, u32[]{:S(2)}, u32[]{:S(2)}) collective-permute-start(f32[128,17,1]{0,2,1:T(1,128)S(1)} %get-tuple-element.15), channel_id=1, source_target_pairs={{0,1},{1,2},{2,3},{3,4},{4,5},{5,6},{6,7},{7,8},{8,9},{9,10},{10,1... | collective-permute-start | bytes 26120 | tf_op jit(solution)/shard_map/ppermute | solution.py:17
  677.8 1.8 copy-start.10
Sparse Core Ops, SparseCore 0:
  221.1 456.6 all-reduce.3
where the time goes:
time: 688 us; the launch traced here: 687 us
  waiting for transfers between devices  355 us (52%)
  blocking collectives  207 us (30%)
  starting transfers between devices  63.5 us (9%)
  matrix products  33.3 us (5%)
  between operations  16.8 us (2%)
  local copies, waits for them, and re-layouts  7.53 us (1%)
    psum x1, waiting for transfers between devices, body(): lax.psum((grad_w_first, grad_b_first, grad_w_second, grad_b_second), ('la...  340 us
    psum x1, blocking collectives, pool_modes(): pooled = lax.psum(local_sum, ('lat', 'lon'))  106 us
    psum x1, blocking collectives, body(): lax.psum((grad_w_first, grad_b_first, grad_w_second, grad_b_second), ('la...  101 us
    ppermute x8, starting transfers between devices, padded_2(): lax.ppermute(head, axis, [((i + 1) % count, i) for i in range(ends)])  37.1 us
    ppermute x8, starting transfers between devices, padded_2(): lax.ppermute(tail, axis, [(i, (i + 1) % count) for i in range(ends)])  26.4 us
    dot_general x18, matrix products, kernel_grad(): jnp.einsum('ohw,chw->oc', grad, padded[:, shift_a:shift_a + rows, shift_b...  14.4 us
  transfers between devices with their start and end apart: 17, of which 6 were waited for; matrix products, arithmetic and copies ran while one was open for 2% of the time, Pallas kernels for 0%

commit v1 on v0

v1 whole, which is shorter than its diff:
```python
import math

import jax
import jax.numpy as jnp
from jax import lax
from jax.sharding import Mesh, PartitionSpec as P

LAT = ("y", "xl", "c")
LON = ("z", "xh")
PLANE = ("y", "xl", "xh", "c")
RING = ("z",)
HIGH = lax.Precision.HIGH


def grow(cells, axes, dim, width, closed):
    count = lax.axis_size(axes)
    ends = count if closed else count - 1
    head = lax.slice_in_dim(cells, 0, width, axis=dim)
    tail = lax.slice_in_dim(cells, cells.shape[dim] - width, cells.shape[dim], axis=dim)
    return jnp.concatenate(
        [
            lax.ppermute(tail, axes, [(i, (i + 1) % count) for i in range(ends)]),
            cells,
            lax.ppermute(head, axes, [((i + 1) % count, i) for i in range(ends)]),
        ],
        axis=dim,
    )


def convolve(padded, weight, rows, cols):
    total = None
    for tap in range(9):
        a, b = tap // 3, tap % 3
        term = jnp.einsum("oc,chw->ohw", weight[tap], padded[:, a : a + rows, b : b + cols], precision=HIGH)
        total = term if total is None else total + term
    return total


def transpose_conv(padded, weight, rows, cols):
    total = None
    for tap in range(9):
        a, b = 2 - tap // 3, 2 - tap % 3
        term = jnp.einsum("oc,ohw->chw", weight[tap], padded[:, a : a + rows, b : b + cols], precision=HIGH)
        total = term if total is None else total + term
    return total


def kernel_grad(grad, padded, rows, cols, spec):
    return jnp.stack(
        [
            jnp.einsum(spec, grad, padded[:, t // 3 : t // 3 + rows, t % 3 : t % 3 + cols], precision=HIGH)
            for t in range(9)
        ]
    )


def slope(pre):
    sigma = jax.nn.sigmoid(pre)
    return sigma * (1.0 + pre * (1.0 - sigma))


def row_weights(first, count, nlat, nlon):
    every = (jnp.arange(nlat, dtype=jnp.float32) + 0.5) * (math.pi / nlat) - math.pi / 2
    total = jnp.sum(jnp.cos(every)) * nlon
    global_rows = first + jnp.arange(count, dtype=jnp.int32)
    phi = (global_rows.astype(jnp.float32) + 0.5) * (math.pi / nlat) - math.pi / 2
    inside = (global_rows >= 0) & (global_rows < nlat)
    return jnp.where(inside, jnp.cos(phi), 0.0) / total, inside


def swap(pieces, axes):
    return lax.all_to_all(pieces, axes, 0, 0, tiled=True)


def to_all(piece, axes):
    return swap(jnp.broadcast_to(piece[None], (lax.axis_size(axes),) + piece.shape), axes)


def fill(rows, count):
    return jnp.pad(rows, ((0, count - rows.shape[0]), (0, 0)))


def body(field, w_first, b_first, w_second, b_second, modes, cotangent):
    cin, rows, cols = field.shape
    ch = w_first.shape[1]
    n_lat, n_lon = lax.axis_size(LAT), lax.axis_size(LON)
    n_pl, n_z = lax.axis_size(PLANE), lax.axis_size(RING)
    nlat, nlon = rows * n_lat, cols * n_lon
    first = lax.axis_index(LAT) * rows

    fext = grow(grow(field, LAT, 1, 4, False), LON, 2, 4, True)
    weights, inside = row_weights(first - 3, rows + 6, nlat, nlon)
    inside = inside[None, :, None]
    h1 = convolve(fext, w_first, rows + 6, cols + 6) + b_first[:, None, None]
    a1 = jnp.where(inside, jax.nn.silu(h1), 0.0)
    s1 = jnp.where(inside, slope(h1), 0.0)[:, 2 : rows + 4, 2 : cols + 4]
    h2 = convolve(a1, w_second, rows + 4, cols + 4) + b_second[:, None, None]
    s2 = weights[None, 1 : rows + 5, None] * slope(h2)
    own_h2 = h2[:, 2 : rows + 2, 2 : cols + 2]
    own_s2 = s2[:, 2 : rows + 2, 2 : cols + 2]
    own_weights = weights[3 : rows + 3][None, :, None]
    pooled = jnp.sum(jax.nn.silu(own_h2) * own_weights, axis=(1, 2))
    bias2 = jnp.sum(own_s2, axis=(1, 2))
    g2 = kernel_grad(own_s2, a1[:, 2 : rows + 4, 2 : cols + 4], rows, cols, "ohw,chw->oc")

    share2 = 9 * ch // n_pl
    small = jnp.stack([pooled, bias2])
    part = jnp.concatenate(
        [g2.reshape(n_pl, share2, ch), jnp.broadcast_to(small[None], (n_pl, 2, ch))], axis=1
    )
    part = jnp.sum(swap(part, PLANE), axis=0)
    bit2 = -(-share2 // n_z)
    mine = fill(part[:share2], bit2 * n_z).reshape(n_z, bit2, ch)
    mine = jnp.concatenate([mine, jnp.broadcast_to(part[None, share2:], (n_z, 2, ch))], axis=1)
    mine = jnp.sum(swap(mine, RING), axis=0)
    piece2, pooled, bias2 = mine[:bit2], mine[bit2], mine[bit2 + 1]

    amplitude = jnp.dot(modes, pooled, precision=lax.Precision.HIGHEST)
    spread = jnp.sqrt(jnp.mean(amplitude * amplitude) + 1e-05)
    normal = amplitude / spread
    d_amplitude = (cotangent - normal * jnp.mean(cotangent * normal)) / spread
    d_modes = d_amplitude[:, None] * pooled[None, :]
    d_pooled = jnp.dot(d_amplitude, modes, precision=lax.Precision.HIGHEST)

    grad_two = d_pooled[:, None, None] * s2
    grad_one = transpose_conv(grad_two, w_second, rows + 2, cols + 2) * s1
    own_one = grad_one[:, 1 : rows + 1, 1 : cols + 1]
    g1 = kernel_grad(own_one, fext[:, 3 : rows + 5, 3 : cols + 5], rows, cols, "ohw,chw->co")
    bias1 = jnp.sum(own_one, axis=(1, 2))
    grad_field = transpose_conv(grad_one, w_first, rows, cols) * float(nlat * nlon)

    share1 = -(-(9 * cin + 1) // n_pl)
    part = fill(jnp.concatenate([g1.reshape(9 * cin, ch), bias1[None]]), share1 * n_pl)
    part = jnp.sum(swap(part.reshape(n_pl, share1, ch), PLANE), axis=0)
    both = to_all(jnp.concatenate([part, piece2]), RING)
    part = jnp.sum(both[:, :share1], axis=0)
    piece2 = both[:, share1:].reshape(n_z * bit2, ch)[:share2]
    whole = to_all(jnp.concatenate([piece2, part]), PLANE)
    grad_w_second = whole[:, :share2].reshape(9, ch, ch) * d_pooled[None, :, None]
    first_rows = whole[:, share2:].reshape(n_pl * share1, ch)
    grad_w_first = first_rows[: 9 * cin].reshape(9, cin, ch).transpose(0, 2, 1)
    return (grad_field, grad_w_first, first_rows[9 * cin], grad_w_second, bias2 * d_pooled, d_modes)


def solution(mesh):
    fine = Mesh(mesh.devices.reshape(4, 2, 2, 16, 2), ("y", "xl", "c", "z", "xh"))
    in_specs = (P(None, LAT, LON), P(), P(), P(), P(), P(), P())
    out_specs = (P(None, LAT, LON), P(), P(), P(), P(), P())
    return jax.shard_map(body, mesh=fine, in_specs=in_specs, out_specs=out_specs, check_vma=False)
```

time: 688 us -> 174 us (0.25)
  waiting for transfers between devices: 355 us -> 52.9 us
  blocking collectives: 207 us -> 18.7 us
  starting transfers between devices: 63.5 us -> 45.4 us
  between operations: 16.8 us -> 3.34 us
    psum x1 -> x0, waiting for transfers between devices: 340 us -> none  [body(): lax.psum((grad_w_first, grad_b_first, grad_w_second, grad_b_second), ('la...]
    psum x2 -> x0, blocking collectives: 207 us -> none  [the longest x1 106 us: pool_modes(): pooled = lax.psum(local_sum, ('lat', 'lon'))]
    all_to_all x0 -> x4, waiting for transfers between devices: none -> 46.6 us  [swap(): return lax.all_to_all(pieces, axes, 0, 0, tiled=True)]
    ppermute x16 -> x4, starting transfers between devices: 63.5 us -> 23.6 us  [the longest x2 17.2 us: grow(): lax.ppermute(head, axes, [((i + 1) % count, i) for i in range(ends)])]
    all_to_all x0 -> x4, starting transfers between devices: none -> 21.8 us  [swap(): return lax.all_to_all(pieces, axes, 0, 0, tiled=True)]
    all_to_all x0 -> x1, blocking collectives: none -> 18.7 us  [swap(): return lax.all_to_all(pieces, axes, 0, 0, tiled=True)]
    ppermute x16 -> x4, waiting for transfers between devices: 15.1 us -> 6.3 us  [the longest x2 6.29 us: grow(): lax.ppermute(tail, axes, [(i, (i + 1) % count) for i in range(ends)])]
    dot_general x57 -> x56, matrix products: 33.3 us -> 35.5 us  [the longest x18 15 us: kernel_grad(): jnp.einsum(spec, grad, padded[:, t // 3:t // 3 + rows, t % 3:t % 3 + cols...]
  transfers between devices with their start and end apart: 17 -> 8, of which waited for: 6 -> 5; matrix products, arithmetic and copies ran while one was open for 2% -> 3% of each run, Pallas kernels for 0% -> 0%
where the time goes in v1:
time: 174 us; the launch traced here: 173 us
  waiting for transfers between devices  52.9 us (30%)
  starting transfers between devices  45.4 us (26%)
  matrix products  35.5 us (20%)
  blocking collectives  18.7 us (11%)
  local copies, waits for them, and re-layouts  10.7 us (6%)
  other arithmetic  6.08 us (3%)
  between operations  3.34 us (2%)
    all_to_all x4, waiting for transfers between devices, swap(): return lax.all_to_all(pieces, axes, 0, 0, tiled=True)  46.6 us
    all_to_all x4, starting transfers between devices, swap(): return lax.all_to_all(pieces, axes, 0, 0, tiled=True)  21.8 us
    all_to_all x1, blocking collectives, swap(): return lax.all_to_all(pieces, axes, 0, 0, tiled=True)  18.7 us
    ppermute x2, starting transfers between devices, grow(): lax.ppermute(head, axes, [((i + 1) % count, i) for i in range(ends)])  17.2 us
    dot_general x18, matrix products, kernel_grad(): jnp.einsum(spec, grad, padded[:, t // 3:t // 3 + rows, t % 3:t % 3 + cols...  15 us
    dot_general x18, matrix products, convolve(): jnp.einsum('oc,chw->ohw', weight[tap], padded[:, a:a + rows, b:b + cols],...  13 us
    dot_general x18, matrix products, transpose_conv(): jnp.einsum('oc,ohw->chw', weight[tap], padded[:, a:a + rows, b:b + cols],...  6.49 us
    ppermute x2, starting transfers between devices, grow(): lax.ppermute(tail, axes, [(i, (i + 1) % count) for i in range(ends)])  6.43 us
  transfers between devices with their start and end apart: 8, of which 5 were waited for; matrix products, arithmetic and copies ran while one was open for 3% of the time, Pallas kernels for 0%

profile of v1, /device:TPU:1, one launch (start us, length us, event | category | flops | bytes accessed | tf_op | source)
XLA Modules:
  0.0 172.7 jit_solution(1970053912209786241)
XLA Ops:
  0.7 1.0 fusion.210
  1.7 4.5 %collective-permute-start = (f32[69,4,45]{0,2,1:T(8,128)S(1)}, f32[69,4,45]{0,2,1:T(8,128)S(1)}, u32[]{:S(2)}, u32[]{:S(2)}) collective-permute-start(f32[69,4,45]{0,2,1:T(8,128)S(1)} %get-tuple-element.11), channel_id=1, source_target_pairs={{0,32},{32,64},{64,96},{96,128},{128,160},{160,192},{192,224},{224... | collective-permute-start | bytes 149048 | tf_op jit(solution)/shard_map/ppermute | solution.py:22
  6.2 5.6 %collective-permute-start.1 = (f32[69,4,45]{0,2,1:T(8,128)S(1)}, f32[69,4,45]{0,2,1:T(8,128)S(1)}, u32[]{:S(2)}, u32[]{:S(2)}) collective-permute-start(f32[69,4,45]{0,2,1:T(8,128)S(1)} %get-tuple-element.10), channel_id=1, source_target_pairs={{32,0},{64,32},{96,64},{128,96},{160,128},{192,160},{224,192},{256... | collective-permute-start | bytes 149048 | tf_op jit(solution)/shard_map/ppermute | solution.py:24
  11.8 0.7 cosine_reduce_fusion
  13.1 0.6 copy-done.9
  14.5 11.6 %collective-permute-start.3 = (f32[69,23,4]{0,2,1:T(4,128)S(1)}, f32[69,23,4]{0,2,1:T(4,128)S(1)}, u32[]{:S(2)}, u32[]{:S(2)}) collective-permute-start(f32[69,23,4]{0,2,1:T(4,128)S(1)} %get-tuple-element.9), channel_id=1, source_target_pairs={{1,0},{2,1},{3,2},{4,3},{5,4},{6,5},{7,6},{8,7},{9,8},{10,9},{11,1... | collective-permute-start | bytes 76184 | tf_op jit(solution)/shard_map/ppermute | solution.py:24
  26.1 1.9 %collective-permute-start.2 = (f32[69,23,4]{0,2,1:T(4,128)S(1)}, f32[69,23,4]{0,2,1:T(4,128)S(1)}, u32[]{:S(2)}, u32[]{:S(2)}) collective-permute-start(f32[69,23,4]{0,2,1:T(4,128)S(1)} %get-tuple-element.8), channel_id=1, source_target_pairs={{0,1},{1,2},{2,3},{3,4},{4,5},{5,6},{6,7},{7,8},{8,9},{9,10},{10,1... | collective-permute-start | bytes 76184 | tf_op jit(solution)/shard_map/ppermute | solution.py:22
  28.2 6.3 %collective-permute-done.2 = f32[69,23,4]{0,2,1:T(4,128)S(1)} collective-permute-done((f32[69,23,4]{0,2,1:T(4,128)S(1)}, f32[69,23,4]{0,2,1:T(4,128)S(1)}, u32[]{:S(2)}, u32[]{:S(2)}) %collective-permute-start.2) | collective-permute-done | bytes 25424 | tf_op jit(solution)/shard_map/ppermute | solution.py:22
  34.6 0.6 fusion.33
  35.3 0.6 fusion.35
  35.9 0.6 fusion.37
  37.1 0.6 fusion.41
  38.4 0.6 fusion.45
  39.0 0.6 fusion.47
  39.6 1.8 %add_divide_fusion = (f32[128,21,51]{0,2,1:T(8,128)}, f32[128,21,51]{0,2,1:T(8,128)S(1)}, f32[128,21,51]{0,2,1:T(8,128)}) fusion(pred[21]{0:T(512)(128)(4,1)S(1)} %compare_and_fusion, f32[128]{0:T(128)S(1)} %copy-done.14, f32[21,51,128]{2,1,0:T(8,128)S(1)} %fusion.33, f32[21,51,128]{2,1,0:T(8,128)S(1)} %fusion.35, f32[21,51,128]{2,1,0:T(8,128)S(1)} %fusion.37, ...), kind=kOutput, calls=%fused_computation.105 | convolution fusion | flops 58673664 | bytes 7101952 | tf_op jit(solution)/shard_map/oc,chw->ohw/dot_general | solution.py:34
  46.4 1.4 multiply_multiply_fusion
  47.8 1.2 fusion.23
  49.0 1.2 fusion.22
  50.2 1.2 fusion.21
  51.3 1.2 fusion.20
  52.5 1.2 fusion.19
  53.7 1.2 fusion.18
  54.9 1.2 fusion.17
  56.0 1.2 fusion.16
  57.2 1.2 fusion.15
  58.4 1.1 reshape.53
  59.5 1.2 multiply_reduce_fusion
  60.8 18.7 %all_to_all.25 = f32[32,38,128]{2,1,0:T(8,128)S(1)} all-to-all(f32[32,38,128]{2,1,0:T(8,128)S(1)} %pad_maximum_fusion.1), channel_id=1, replica_groups=mesh['y'=4,'xl'=2,'c'=2,'z'=16,'xh'=2] {'y','xl','xh','c'}, dimensions={0} | all-to-all | bytes 1245184 | tf_op jit(solution)/shard_map/all_to_all | solution.py:72
  79.6 0.6 pad_maximum_fusion.6
  80.3 5.5 %all-to-all-start.1 = ((f32[16,5,128]{2,1,0:T(8,128)}), f32[16,5,128]{2,1,0:T(8,128)S(1)}, u32[]{:S(2)}, u32[]{:S(2)}) async-start(f32[16,5,128]{2,1,0:T(8,128)} %pad_maximum_fusion.6), calls=%async_computation.1 | async-start | bytes 131072 | tf_op jit(solution)/shard_map/all_to_all | solution.py:72
  85.9 11.5 %all-to-all-done.1 = f32[16,5,128]{2,1,0:T(8,128)S(1)} async-done(((f32[16,5,128]{2,1,0:T(8,128)}), f32[16,5,128]{2,1,0:T(8,128)S(1)}, u32[]{:S(2)}, u32[]{:S(2)}) %all-to-all-start.1) | async-done | bytes 40992 | tf_op jit(solution)/shard_map/all_to_all | solution.py:72
  97.7 0.6 multiply_reduce_fusion.2
  99.1 0.6 copy-done.13
  101.0 0.8 bitcast_multiply_fusion
  104.5 0.7 copy-done.3
  112.4 0.8 reshape.56
  113.2 5.5 %all-to-all-start.2 = ((f32[32,20,128]{2,1,0:T(8,128)}), f32[32,20,128]{2,1,0:T(8,128)S(1)}, u32[]{:S(2)}, u32[]{:S(2)}) async-start(f32[32,20,128]{2,1,0:T(8,128)} %reshape.56), calls=%async_computation.2 | async-start | bytes 786432 | tf_op jit(solution)/shard_map/all_to_all | solution.py:72
  119.3 9.4 %all-to-all-done.2 = f32[32,20,128]{2,1,0:T(8,128)S(1)} async-done(((f32[32,20,128]{2,1,0:T(8,128)}), f32[32,20,128]{2,1,0:T(8,128)S(1)}, u32[]{:S(2)}, u32[]{:S(2)}) %all-to-all-start.2) | async-done | bytes 327712 | tf_op jit(solution)/shard_map/all_to_all | solution.py:72
  128.8 0.7 broadcast_in_dim.61
  129.5 3.7 %all-to-all-start.3 = ((f32[16,23,128]{2,1,0:T(8,128)}), f32[16,23,128]{2,1,0:T(8,128)S(1)}, u32[]{:S(2)}, u32[]{:S(2)}) async-start(f32[16,23,128]{2,1,0:T(8,128)} %broadcast_in_dim.61), calls=%async_computation.3 | async-start | bytes 393216 | tf_op jit(solution)/shard_map/all_to_all | solution.py:72
  133.8 12.6 %all-to-all-done.3 = f32[16,23,128]{2,1,0:T(8,128)S(1)} async-done(((f32[16,23,128]{2,1,0:T(8,128)}), f32[16,23,128]{2,1,0:T(8,128)S(1)}, u32[]{:S(2)}, u32[]{:S(2)}) %all-to-all-start.3) | async-done | bytes 188448 | tf_op jit(solution)/shard_map/all_to_all | solution.py:72
  146.4 1.0 broadcast_in_dim.62
  147.4 7.1 %all-to-all-start.4 = ((f32[32,56,128]{2,1,0:T(8,128)}), f32[32,56,128]{2,1,0:T(8,128)S(1)}, u32[]{:S(2)}, u32[]{:S(2)}) async-start(f32[32,56,128]{2,1,0:T(8,128)} %broadcast_in_dim.62), calls=%async_computation.4 | async-start | bytes 1835008 | tf_op jit(solution)/shard_map/all_to_all | solution.py:72
  154.6 0.8 broadcast_multiply_fusion.2
  156.1 1.1 fusion.14
  157.1 13.1 %all-to-all-done.4 = f32[32,56,128]{2,1,0:T(8,128)S(1)} async-done(((f32[32,56,128]{2,1,0:T(8,128)}), f32[32,56,128]{2,1,0:T(8,128)S(1)}, u32[]{:S(2)}, u32[]{:S(2)}) %all-to-all-start.4) | async-done | bytes 917536 | tf_op jit(solution)/shard_map/all_to_all | solution.py:72
  170.9 0.7 reshape.58
  171.7 0.9 broadcast_multiply_fusion
  (109 shorter events, 20.8 us)
Async XLA Ops:
  0.6 96.8 %copy-start = (f32[512,128]{1,0:T(8,128)S(1)}, f32[512,128]{1,0:T(8,128)}, u32[]{:S(2)}) copy-start(f32[512,128]{1,0:T(8,128)} %param.12) | copy-start | bytes 786436
  0.6 13.1 %copy-start.1 = (f32[69,15,45]{0,2,1:T(8,128)S(1)}, f32[69,15,45]{0,2,1:T(8,128)}, u32[]{:S(2)}) copy-start(f32[69,15,45]{0,2,1:T(8,128)} %param.7) | copy-start | bytes 558904
  1.7 11.4 %collective-permute-start = (f32[69,4,45]{0,2,1:T(8,128)S(1)}, f32[69,4,45]{0,2,1:T(8,128)S(1)}, u32[]{:S(2)}, u32[]{:S(2)}) collective-permute-start(f32[69,4,45]{0,2,1:T(8,128)S(1)} %get-tuple-element.11), channel_id=1, source_target_pairs={{0,32},{32,64},{64,96},{96,128},{128,160},{160,192},{192,224},{224... | collective-permute-start | bytes 149048 | tf_op jit(solution)/shard_map/ppermute | solution.py:22
  6.2 7.6 %collective-permute-start.1 = (f32[69,4,45]{0,2,1:T(8,128)S(1)}, f32[69,4,45]{0,2,1:T(8,128)S(1)}, u32[]{:S(2)}, u32[]{:S(2)}) collective-permute-start(f32[69,4,45]{0,2,1:T(8,128)S(1)} %get-tuple-element.10), channel_id=1, source_target_pairs={{32,0},{64,32},{96,64},{128,96},{160,128},{192,160},{224,192},{256... | collective-permute-start | bytes 149048 | tf_op jit(solution)/shard_map/ppermute | solution.py:24
  13.1 0.6 copy-start.9
  13.8 0.6 copy-start.7
  14.5 13.8 %collective-permute-start.3 = (f32[69,23,4]{0,2,1:T(4,128)S(1)}, f32[69,23,4]{0,2,1:T(4,128)S(1)}, u32[]{:S(2)}, u32[]{:S(2)}) collective-permute-start(f32[69,23,4]{0,2,1:T(4,128)S(1)} %get-tuple-element.9), channel_id=1, source_target_pairs={{1,0},{2,1},{3,2},{4,3},{5,4},{6,5},{7,6},{8,7},{9,8},{10,9},{11,1... | collective-permute-start | bytes 76184 | tf_op jit(solution)/shard_map/ppermute | solution.py:24
  26.1 8.4 %collective-permute-start.2 = (f32[69,23,4]{0,2,1:T(4,128)S(1)}, f32[69,23,4]{0,2,1:T(4,128)S(1)}, u32[]{:S(2)}, u32[]{:S(2)}) collective-permute-start(f32[69,23,4]{0,2,1:T(4,128)S(1)} %get-tuple-element.8), channel_id=1, source_target_pairs={{0,1},{1,2},{2,3},{3,4},{4,5},{5,6},{6,7},{7,8},{8,9},{9,10},{10,1... | collective-permute-start | bytes 76184 | tf_op jit(solution)/shard_map/ppermute | solution.py:22
  28.2 6.4 %copy-start.5 = (f32[9,128,69]{1,2,0:T(8,128)S(1)}, f32[9,128,69]{1,2,0:T(8,128)}, u32[]{:S(2)}) copy-start(f32[9,128,69]{1,2,0:T(8,128)} %param.8) | copy-start | bytes 953860
  39.0 0.7 copy-start.14
  39.6 1.8 %copy-start.2 = (f32[9,128,128]{2,1,0:T(8,128)S(1)}, f32[9,128,128]{2,1,0:T(8,128)}, u32[]{:S(2)}) copy-start(f32[9,128,128]{2,1,0:T(8,128)} %param.10) | copy-start | bytes 1769476
  45.7 0.7 copy-start.15
  80.3 17.1 %all-to-all-start.1 = ((f32[16,5,128]{2,1,0:T(8,128)}), f32[16,5,128]{2,1,0:T(8,128)S(1)}, u32[]{:S(2)}, u32[]{:S(2)}) async-start(f32[16,5,128]{2,1,0:T(8,128)} %pad_maximum_fusion.6), calls=%async_computation.1 | async-start | bytes 131072 | tf_op jit(solution)/shard_map/all_to_all | solution.py:72
  97.4 21.6 %copy-start.11 = (f32[5,128]{1,0:T(8,128)}, f32[5,128]{1,0:T(8,128)S(1)}, u32[]{:S(2)}) copy-start(f32[5,128]{1,0:T(8,128)S(1)} %reduce_sum.94) | copy-start | bytes 7684
  99.0 0.7 copy-start.13
  104.1 1.1 copy-start.3
  104.1 1.2 copy-start.4
  105.4 1.0 copy-start.6
  107.1 0.9 copy-start.10
  110.5 0.9 copy-start.8
  113.2 15.5 %all-to-all-start.2 = ((f32[32,20,128]{2,1,0:T(8,128)}), f32[32,20,128]{2,1,0:T(8,128)S(1)}, u32[]{:S(2)}, u32[]{:S(2)}) async-start(f32[32,20,128]{2,1,0:T(8,128)} %reshape.56), calls=%async_computation.2 | async-start | bytes 786432 | tf_op jit(solution)/shard_map/all_to_all | solution.py:72
  119.3 9.4 %slice-start = ((f32[5,128]{1,0:T(8,128)}), f32[3,128]{1,0:T(4,128)S(1)}, s32[]{:S(2)}) async-start(f32[5,128]{1,0:T(8,128)} %copy-done.11), calls=%async_computation.5 | async-start | bytes 4096 | tf_op jit(solution)/shard_map/slice | solution.py:116
  129.5 3.7 %copy-start.12 = (f32[5,128]{1,0:T(8,128)S(1)}, f32[5,128]{1,0:T(8,128)}, u32[]{:S(2)}) copy-start(f32[5,128]{1,0:T(8,128)} %copy-done.11) | copy-start | bytes 7684
  129.5 16.9 %all-to-all-start.3 = ((f32[16,23,128]{2,1,0:T(8,128)}), f32[16,23,128]{2,1,0:T(8,128)S(1)}, u32[]{:S(2)}, u32[]{:S(2)}) async-start(f32[16,23,128]{2,1,0:T(8,128)} %broadcast_in_dim.61), calls=%async_computation.3 | async-start | bytes 393216 | tf_op jit(solution)/shard_map/all_to_all | solution.py:72
  147.4 22.8 %all-to-all-start.4 = ((f32[32,56,128]{2,1,0:T(8,128)}), f32[32,56,128]{2,1,0:T(8,128)S(1)}, u32[]{:S(2)}, u32[]{:S(2)}) async-start(f32[32,56,128]{2,1,0:T(8,128)} %broadcast_in_dim.62), calls=%async_computation.4 | async-start | bytes 1835008 | tf_op jit(solution)/shard_map/all_to_all | solution.py:72

commit v2 on v1

v2 whole, which is shorter than its diff:
```python
import math

import jax
import jax.numpy as jnp
from jax import lax
from jax.experimental import pallas as pl
from jax.experimental.pallas import tpu as pltpu
from jax.sharding import Mesh, PartitionSpec as P

LAT = ("y", "xl", "c")
LON = ("z", "xh")
PLANE = ("y", "xl", "xh", "c")
RING = ("z",)
F32 = jnp.float32
BF16 = jnp.bfloat16

PITCH = 64
LANES = 128
ROWS, COLS, CIN = 15, 45, 69
WINDOW = 16 * PITCH
NX, N1, N2, N3 = 23 * PITCH, 21 * PITCH, 19 * PITCH, 17 * PITCH


def split(x):
    hi = x.astype(BF16)
    return hi, (x - hi.astype(F32)).astype(BF16)


def spread(src, high, low, start, stop):
    for r in range(start, stop, PITCH):
        for b in range(3):
            hi, lo = split(src[r + b : r + b + PITCH, :])
            high[r : r + PITCH, b * LANES : (b + 1) * LANES] = hi
            low[r : r + PITCH, b * LANES : (b + 1) * LANES] = lo


def dot(a, b):
    return jnp.dot(a, b, preferred_element_type=F32)


def convolve(high, low, weight, start, count):
    total = None
    for a in range(3):
        r = start + a * PITCH
        w = weight[a]
        both = dot(high[r : r + count, :], w)
        term = both[:, :LANES] + both[:, LANES:] + dot(low[r : r + count, :], w[:, :LANES])
        total = term if total is None else total + term
    return total


def correlate(grad, high, low, start):
    hi, lo = split(grad.T)
    both = jnp.concatenate([hi, lo], axis=0)
    blocks = []
    for a in range(3):
        r = start + a * PITCH
        x = high[r : r + WINDOW, :]
        out = dot(both, x)
        blocks.append(out[:LANES] + out[LANES:] + dot(hi, low[r : r + WINDOW, :]))
    return blocks


def chunks(rows, parts):
    size = -(-rows // parts)
    return [(s, min(size, rows - s)) for s in range(0, rows, size)]


def column_mask(first, shape):
    col = lax.broadcasted_iota(jnp.int32, shape, 0)
    return ((col >= first) & (col < first + COLS)).astype(F32)


def forward_kernel(weights, own, north, south, west, east, w1, b1, w2, b2, x, a1, s1, s2, small, high, low):
    x[...] = jnp.zeros_like(x)
    for i in range(ROWS + 8):
        r = i * PITCH
        row = north[i] if i < 4 else own[i - 4] if i < ROWS + 4 else south[i - ROWS - 4]
        x[r + 8 : r + 8 + COLS, :CIN] = row
        x[r + 4 : r + 8, :CIN] = west[i]
        x[r + 8 + COLS : r + 12 + COLS, :CIN] = east[i]
    spread(x, high, low, 0, NX)
    for first, rows in chunks(ROWS + 6, 3):
        acc = convolve(high, low, w1, first * PITCH, rows * PITCH)
        for k in range(rows):
            r = (first + k) * PITCH
            h = acc[k * PITCH : (k + 1) * PITCH] + b1[...]
            sigma = jax.nn.sigmoid(h)
            inside = jnp.where(weights[first + k] > 0.0, 1.0, 0.0)
            a1[r : r + PITCH, :] = h * sigma * inside
            s1[r : r + PITCH, :] = sigma * (1.0 + h * (1.0 - sigma)) * inside
    a1[N1:, :] = jnp.zeros((8, LANES), F32)
    s1[N1:, :] = jnp.zeros((8, LANES), F32)
    spread(a1, high, low, 0, N1)
    mask = column_mask(6, (PITCH, LANES))
    pooled = jnp.zeros((PITCH, LANES), F32)
    bias = jnp.zeros((PITCH, LANES), F32)
    for first, rows in chunks(ROWS + 4, 2):
        acc = convolve(high, low, w2, first * PITCH, rows * PITCH)
        for k in range(rows):
            i = first + k
            r = i * PITCH
            h = acc[k * PITCH : (k + 1) * PITCH] + b2[...]
            sigma = jax.nn.sigmoid(h)
            weight = weights[i + 1]
            slope = sigma * (1.0 + h * (1.0 - sigma)) * weight
            s2[r : r + PITCH, :] = slope
            if 2 <= i < ROWS + 2:
                pooled = pooled + h * sigma * weight
                bias = bias + slope
    s2[N2:, :] = jnp.zeros((8, LANES), F32)
    small[0:1, :] = jnp.sum(pooled * mask, axis=0, keepdims=True)
    small[1:2, :] = jnp.sum(bias * mask, axis=0, keepdims=True)


def second_kernel(a1, s2, out, high, low, rows):
    spread(a1, high, low, 2 * PITCH, 20 * PITCH)
    mask = column_mask(6, (PITCH, LANES))
    own = [s2[(i + 2) * PITCH : (i + 3) * PITCH, :] * mask for i in range(ROWS)]
    grad = jnp.concatenate(own + [jnp.zeros((PITCH, LANES), F32)], axis=0)
    for a, block in enumerate(correlate(grad, high, low, 2 * PITCH)):
        for b in range(3):
            t = 3 * a + b
            rows[t * LANES : (t + 1) * LANES, :] = block[:, b * LANES : (b + 1) * LANES]
    size = out.shape[1]
    for p in range(out.shape[0]):
        out[p] = rows[p * size : (p + 1) * size, :]


def backward_kernel(sums, modes, cot, s2, s1, x, w2, out, d_modes, spread_d, bias2, g1, g2, high, low, rows):
    total = jnp.sum(sums[...], axis=0)
    pooled = total[0:1]
    amplitude = jnp.sum(modes[...] * pooled, axis=1, keepdims=True)
    count = amplitude.shape[0]
    width = jnp.sqrt(jnp.sum(amplitude * amplitude, axis=0, keepdims=True) / count + 1e-05)
    normal = amplitude / width
    along = jnp.sum(cot[...] * normal, axis=0, keepdims=True) / count
    d_amplitude = (cot[...] - normal * along) / width
    d_modes[...] = d_amplitude * pooled
    d_pooled = jnp.sum(d_amplitude * modes[...], axis=0, keepdims=True)
    spread_d[...] = jnp.broadcast_to(d_pooled, (LANES, LANES)).T
    bias2[...] = total[1:2] * d_pooled

    for i in range(ROWS + 4):
        r = i * PITCH
        g2[r : r + PITCH, :] = s2[r : r + PITCH, :] * d_pooled
    g2[N2:, :] = jnp.zeros((8, LANES), F32)
    spread(g2, high, low, 0, N2)
    for first, count in chunks(ROWS + 2, 2):
        r, n = first * PITCH, count * PITCH
        g1[r : r + n, :] = convolve(high, low, w2, r, n) * s1[r + 2 * PITCH + 2 : r + 2 * PITCH + 2 + n, :]
    g1[N3:, :] = jnp.zeros((8, LANES), F32)

    mask = column_mask(7, (PITCH, LANES))
    own = [g1[(i + 1) * PITCH - 2 : (i + 2) * PITCH - 2, :] * mask for i in range(ROWS)]
    bias1 = own[0]
    for row in own[1:]:
        bias1 = bias1 + row
    grad = jnp.concatenate(own + [jnp.zeros((PITCH, LANES), F32)], axis=0)
    spread(x, high, low, 3 * PITCH, 21 * PITCH)
    for a, block in enumerate(correlate(grad, high, low, 3 * PITCH)):
        for b in range(3):
            t = 3 * a + b
            rows[t * CIN : (t + 1) * CIN, :] = block[:, b * LANES : (b + 1) * LANES].T[:CIN]
    rows[9 * CIN : 9 * CIN + 1, :] = jnp.sum(bias1, axis=0, keepdims=True)
    rows[9 * CIN + 1 :, :] = jnp.zeros((rows.shape[0] - 9 * CIN - 1, LANES), F32)
    size = out.shape[1]
    for p in range(out.shape[0]):
        out[p] = rows[p * size : (p + 1) * size, :]


def field_kernel(scale, g1, w1, out, high, low):
    spread(g1, high, low, 0, N3)
    for first, count in chunks(ROWS, 2):
        acc = convolve(high, low, w1, first * PITCH, count * PITCH) * scale
        for k in range(count):
            out[first + k] = acc[k * PITCH + 4 : k * PITCH + 4 + COLS, :CIN]


def finish_kernel(whole, spread_d, w_second, w_first, b_first, rows):
    pieces, size = whole.shape[0], 9 * LANES // whole.shape[0]
    rest = whole.shape[1] - size
    for p in range(pieces):
        rows[p * size : (p + 1) * size, :] = whole[p, :size, :]
    for t in range(9):
        w_second[t] = rows[t * LANES : (t + 1) * LANES, :] * spread_d[...]
    for p in range(pieces):
        rows[p * rest : (p + 1) * rest, :] = whole[p, size:, :]
    for t in range(9):
        w_first[t] = rows[t * CIN : t * CIN + LANES, :].T[:, :CIN]
    b_first[...] = rows[9 * CIN : 9 * CIN + 1, :]


def call(kernel, outs, scratch, flops, smem=()):
    def run(*args):
        ins = [pl.BlockSpec(memory_space=pltpu.SMEM if i in smem else pltpu.VMEM) for i in range(len(args))]
        return pl.pallas_call(
            kernel,
            out_shape=[jax.ShapeDtypeStruct(s, F32) for s in outs],
            in_specs=ins,
            out_specs=[pl.BlockSpec(memory_space=pltpu.VMEM) for _ in outs],
            scratch_shapes=[pltpu.VMEM(s, d) for s, d in scratch],
            compiler_params=pltpu.CompilerParams(vmem_limit_bytes=32 << 20),
            cost_estimate=pl.CostEstimate(flops=flops, bytes_accessed=4 << 20, transcendentals=0),
        )(*args)

    return run


def stacked(weight, flip):
    weight = weight[::-1] if flip else weight
    weight = jnp.pad(weight, ((0, 0), (0, LANES - weight.shape[1]), (0, LANES - weight.shape[2])))
    weight = weight.reshape(3, 3 * LANES, LANES)
    high = lax.reduce_precision(weight, 8, 7)
    return jnp.concatenate([high.astype(BF16), (weight - high).astype(BF16)], axis=2)


def edges(cells, axes, dim, width, closed):
    count = lax.axis_size(axes)
    ends = count if closed else count - 1
    head = lax.slice_in_dim(cells, 0, width, axis=dim)
    tail = lax.slice_in_dim(cells, cells.shape[dim] - width, cells.shape[dim], axis=dim)
    before = lax.ppermute(tail, axes, [(i, (i + 1) % count) for i in range(ends)])
    after = lax.ppermute(head, axes, [((i + 1) % count, i) for i in range(ends)])
    return before, after


def row_weights(first, count, nlat, nlon):
    every = (jnp.arange(nlat, dtype=F32) + 0.5) * (math.pi / nlat) - math.pi / 2
    total = jnp.sum(jnp.cos(every)) * nlon
    global_rows = first + jnp.arange(count, dtype=jnp.int32)
    phi = (global_rows.astype(F32) + 0.5) * (math.pi / nlat) - math.pi / 2
    inside = (global_rows >= 0) & (global_rows < nlat)
    return jnp.where(inside, jnp.cos(phi), 0.0) / total


def swap(pieces, axes):
    return lax.all_to_all(pieces, axes, 0, 0, tiled=True)


def to_all(piece, axes):
    return swap(jnp.broadcast_to(piece[None], (lax.axis_size(axes),) + piece.shape), axes)


def fill(rows, count):
    return jnp.pad(rows, ((0, count - rows.shape[0]), (0, 0)))


def body(field, w_first, b_first, w_second, b_second, modes, cotangent):
    cin, rows, cols = field.shape
    ch = w_first.shape[1]
    n_lat, n_lon = lax.axis_size(LAT), lax.axis_size(LON)
    n_pl, n_z = lax.axis_size(PLANE), lax.axis_size(RING)
    nlat, nlon = rows * n_lat, cols * n_lon
    weights = row_weights(lax.axis_index(LAT) * rows - 3, 24, nlat, nlon)

    own = field.transpose(1, 2, 0)
    north, south = edges(own, LAT, 0, 4, False)
    left = jnp.concatenate([north[:, :4], own[:, :4], south[:, :4]], axis=0)
    right = jnp.concatenate([north[:, cols - 4 :], own[:, cols - 4 :], south[:, cols - 4 :]], axis=0)
    west, east = edges(jnp.concatenate([left, right], axis=1), LON, 1, 4, True)

    w1 = stacked(w_first.transpose(0, 2, 1), False)
    w2 = stacked(w_second.transpose(0, 2, 1), False)
    w2_back = stacked(w_second, True)
    w1_back = stacked(w_first, True)

    three = (3 * LANES,)
    pair = lambda n: [((n,) + three, BF16), ((n,) + three, BF16)]
    x, a1, s1, s2, small = call(
        forward_kernel,
        [(NX + 8, LANES), (N1 + 8, LANES), (N1 + 8, LANES), (N2 + 8, LANES), (2, LANES)],
        pair(NX),
        10**9,
        (0,),
    )(weights, own, north, south, west, east, w1, b_first[None], w2, b_second[None])

    share2 = 9 * ch // n_pl
    (g2,) = call(second_kernel, [(n_pl, share2, ch)], pair(20 * PITCH) + [((9 * ch, LANES), F32)], 10**9)(a1, s2)

    part = jnp.concatenate([g2, jnp.broadcast_to(small[None], (n_pl, 2, ch))], axis=1)
    part = jnp.sum(swap(part, PLANE), axis=0)
    bit2 = -(-share2 // n_z)
    mine = fill(part[:share2], bit2 * n_z).reshape(n_z, bit2, ch)
    mine = jnp.concatenate([jnp.broadcast_to(part[None, share2:], (n_z, 2, ch)), mine], axis=1)
    mine = swap(mine, RING)
    piece2 = jnp.sum(mine[:, 2:], axis=0)

    share1 = -(-(9 * cin + 1) // n_pl)
    g1rows, d_modes, spread_d, bias2, g1 = call(
        backward_kernel,
        [(n_pl, share1, ch), modes.shape, (LANES, LANES), (1, LANES), (N3 + 8, LANES)],
        [((N2 + 8, LANES), F32)] + pair(21 * PITCH) + [((n_pl * share1, LANES), F32)],
        10**9,
    )(mine, modes, cotangent[:, None], s2, s1, x, w2_back)

    part = jnp.sum(swap(g1rows, PLANE), axis=0)
    (grad_field,) = call(lambda *r: field_kernel(float(nlat * nlon), *r), [(rows, cols, cin)], pair(N3), 10**9)(g1, w1_back)

    both = to_all(jnp.concatenate([part, piece2]), RING)
    part = jnp.sum(both[:, :share1], axis=0)
    piece2 = both[:, share1:].reshape(n_z * bit2, ch)[:share2]
    whole = to_all(jnp.concatenate([piece2, part]), PLANE)
    grad_w_second, grad_w_first, grad_b_first = call(
        finish_kernel,
        [(9, ch, ch), (9, ch, cin), (1, ch)],
        [((9 * ch, LANES), F32)],
        10**6,
    )(whole, spread_d)
    return (grad_field.transpose(2, 0, 1), grad_w_first, grad_b_first[0], grad_w_second, bias2[0], d_modes)


def solution(mesh):
    fine = Mesh(mesh.devices.reshape(4, 2, 2, 16, 2), ("y", "xl", "c", "z", "xh"))
    in_specs = (P(None, LAT, LON), P(), P(), P(), P(), P(), P())
    out_specs = (P(None, LAT, LON), P(), P(), P(), P(), P())
    return jax.shard_map(body, mesh=fine, in_specs=in_specs, out_specs=out_specs, check_vma=False)
```

time: 174 us -> 146 us (0.84)
  matrix products: 35.5 us -> 0 us
  Pallas kernels: 0 us -> 14.4 us
  starting transfers between devices: 45.4 us -> 48.6 us
  waiting for transfers between devices: 52.9 us -> 50 us
  blocking collectives: 18.7 us -> 15.9 us
    dot_general x56 -> x0, matrix products: 35.5 us -> none  [the longest x18 15 us: kernel_grad(): jnp.einsum(spec, grad, padded[:, t // 3:t // 3 + rows, t % 3:t % 3 + cols...]
    pallas_call x0 -> x5, Pallas kernels: none -> 14.4 us  [run(): pl.pallas_call(kernel, out_shape=[jax.ShapeDtypeStruct(s, F32) for s in o...]
    all_to_all x4, starting transfers between devices: 21.8 us -> 27 us  [swap(): return lax.all_to_all(pieces, axes, 0, 0, tiled=True)]
    all_to_all x4, waiting for transfers between devices: 46.6 us -> 43.5 us  [swap(): return lax.all_to_all(pieces, axes, 0, 0, tiled=True)]
    all_to_all x1, blocking collectives: 18.7 us -> 15.9 us  [swap(): return lax.all_to_all(pieces, axes, 0, 0, tiled=True)]
    reshape x6 -> x0, local copies, waits for them, and re-layouts: 2.72 us -> none  [the longest x1 1.11 us: body(): g2.reshape(n_pl, share2, ch)]
    reduce_sum x6 -> x2, other arithmetic: 2.62 us -> 0.07 us  [the longest x1 0.04 us: body(): part = jnp.sum(swap(g1rows, PLANE), axis=0)]
    concatenate x4 -> x7, other arithmetic: 0.82 us -> 2.84 us  [the longest x3 1.26 us: stacked(): jnp.concatenate([high.astype(BF16), (weight - high).astype(BF16)], axis=2)]
  transfers between devices with their start and end apart: 8 -> 8, of which waited for: 5 -> 5; matrix products, arithmetic and copies ran while one was open for 3% -> 5% of each run, Pallas kernels for 0% -> 2%
where the time goes in v2:
time: 146 us; the launch traced here: 145 us
  waiting for transfers between devices  50 us (34%)
  starting transfers between devices  48.6 us (33%)
  blocking collectives  15.9 us (11%)
  Pallas kernels  14.4 us (10%)
  local copies, waits for them, and re-layouts  9.37 us (6%)
  other arithmetic  4.8 us (3%)
  between operations  1.69 us (1%)
    all_to_all x4, waiting for transfers between devices, swap(): return lax.all_to_all(pieces, axes, 0, 0, tiled=True)  43.5 us
    all_to_all x4, starting transfers between devices, swap(): return lax.all_to_all(pieces, axes, 0, 0, tiled=True)  27 us
    all_to_all x1, blocking collectives, swap(): return lax.all_to_all(pieces, axes, 0, 0, tiled=True)  15.9 us
    ppermute x2, starting transfers between devices, edges(): lax.ppermute(head, axes, [((i + 1) % count, i) for i in range(ends)])  15.2 us
    pallas_call x5, Pallas kernels, run(): pl.pallas_call(kernel, out_shape=[jax.ShapeDtypeStruct(s, F32) for s in o...  14.4 us
    ppermute x2, waiting for transfers between devices, edges(): lax.ppermute(tail, axes, [(i, (i + 1) % count) for i in range(ends)])  6.44 us
    ppermute x2, starting transfers between devices, edges(): lax.ppermute(tail, axes, [(i, (i + 1) % count) for i in range(ends)])  6.43 us
    unnamed x26, local copies, waits for them, and re-layouts  4 us
  transfers between devices with their start and end apart: 8, of which 5 were waited for; matrix products, arithmetic and copies ran while one was open for 5% of the time, Pallas kernels for 2%

profile of v2, /device:TPU:1, one launch (start us, length us, event | category | flops | bytes accessed | tf_op | source)
XLA Modules:
  0.0 144.8 jit_solution(17693392851661585881)
XLA Ops:
  0.6 1.0 fusion.6
  1.6 4.5 %collective-permute-start = (f32[4,45,69]{2,1,0:T(8,128)S(1)}, f32[4,45,69]{2,1,0:T(8,128)S(1)}, u32[]{:S(2)}, u32[]{:S(2)}) collective-permute-start(f32[4,45,69]{2,1,0:T(8,128)S(1)} %get-tuple-element.55), channel_id=1, source_target_pairs={{0,32},{32,64},{64,96},{96,128},{128,160},{160,192},{192,224},{224... | collective-permute-start | bytes 149048 | tf_op jit(solution)/shard_map/ppermute | solution.py:223
  6.1 5.6 %collective-permute-start.1 = (f32[4,45,69]{2,1,0:T(8,128)S(1)}, f32[4,45,69]{2,1,0:T(8,128)S(1)}, u32[]{:S(2)}, u32[]{:S(2)}) collective-permute-start(f32[4,45,69]{2,1,0:T(8,128)S(1)} %get-tuple-element.54), channel_id=1, source_target_pairs={{32,0},{64,32},{96,64},{128,96},{160,128},{192,160},{224,192},{256... | collective-permute-start | bytes 149048 | tf_op jit(solution)/shard_map/ppermute | solution.py:224
  11.7 0.9 fusion.5
  12.6 0.0 copy-start.10
  12.6 1.3 copy.16
  13.9 0.1 reduce-precision_convert_fusion.2
  14.1 0.1 reduce-precision_convert_fusion.3
  14.2 0.0 copy-start
  14.2 0.0 copy-start.2
  14.2 0.0 copy-start.3
  14.2 0.1 pad_maximum_fusion.1
  14.4 0.7 cosine_reduce_fusion
  15.8 9.6 %collective-permute-start.3 = (f32[23,4,69]{2,1,0:T(4,128)S(1)}, f32[23,4,69]{2,1,0:T(4,128)S(1)}, u32[]{:S(2)}, u32[]{:S(2)}) collective-permute-start(f32[23,4,69]{2,1,0:T(4,128)S(1)} %pad_maximum_fusion.7), channel_id=1, source_target_pairs={{1,0},{2,1},{3,2},{4,3},{5,4},{6,5},{7,6},{8,7},{9,8},{10,9},{11,1... | collective-permute-start | bytes 76184 | tf_op jit(solution)/shard_map/ppermute | solution.py:224
  25.4 1.9 %collective-permute-start.2 = (f32[23,4,69]{2,1,0:T(4,128)S(1)}, f32[23,4,69]{2,1,0:T(4,128)S(1)}, u32[]{:S(2)}, u32[]{:S(2)}) collective-permute-start(f32[23,4,69]{2,1,0:T(4,128)S(1)} %pad_maximum_fusion.6), channel_id=1, source_target_pairs={{0,1},{1,2},{2,3},{3,4},{4,5},{5,6},{6,7},{7,8},{8,9},{9,10},{10,1... | collective-permute-start | bytes 76184 | tf_op jit(solution)/shard_map/ppermute | solution.py:223
  27.3 0.1 fusion.4.weights
  27.4 6.4 %collective-permute-done.2.west = f32[23,4,69]{2,1,0:T(4,128)S(1)} collective-permute-done((f32[23,4,69]{2,1,0:T(4,128)S(1)}, f32[23,4,69]{2,1,0:T(4,128)S(1)}, u32[]{:S(2)}, u32[]{:S(2)}) %collective-permute-start.2) | collective-permute-done | bytes 25424 | tf_op jit(solution)/shard_map/ppermute | solution.py:223
  33.9 4.9 %shard_map.118 = (f32[1480,128]{1,0:T(8,128)S(1)}, f32[1352,128]{1,0:T(8,128)S(1)}, f32[1352,128]{1,0:T(8,128)S(1)}, f32[1224,128]{1,0:T(8,128)S(1)}, f32[2,128]{1,0:T(2,128)S(1)}) custom-call(f32[24]{0:T(128)S(1)} %fusion.4.weights, f32[15,45,69]{2,1,0:T(8,128)S(1)} %bitcast.28, f32[4,45,69]{2,1,0:T(8,128)S(1)} %collective-permute-done.north, ...), custom_call_target="tpu_custom_call" | custom-call | flops 1000000000 | bytes 4194304 | tf_op jit(solution)/shard_map/pallas_call | solution.py:197
  38.8 1.6 %shard_map.119 = f32[32,36,128]{2,1,0:T(8,128)S(1)} custom-call(f32[1352,128]{1,0:T(8,128)S(1)} %get-tuple-element.19.a1, f32[1224,128]{1,0:T(8,128)S(1)} %get-tuple-element.20.s2), custom_call_target="tpu_custom_call" | custom-call | flops 1000000000 | bytes 4194304 | tf_op jit(solution)/shard_map/pallas_call | solution.py:197
  40.4 0.9 pad_maximum_fusion
  41.4 8.0 %all-to-all-start = ((f32[32,38,128]{2,1,0:T(8,128)}), f32[32,38,128]{2,1,0:T(8,128)S(1)}, u32[]{:S(2)}, u32[]{:S(2)}) async-start(f32[32,38,128]{2,1,0:T(8,128)} %pad_maximum_fusion), calls=%async_computation | async-start | bytes 1310720 | tf_op jit(solution)/shard_map/all_to_all | solution.py:238
  49.4 0.9 rev.6
  50.2 12.0 %all-to-all-done = f32[32,38,128]{2,1,0:T(8,128)S(1)} async-done(((f32[32,38,128]{2,1,0:T(8,128)}), f32[32,38,128]{2,1,0:T(8,128)S(1)}, u32[]{:S(2)}, u32[]{:S(2)}) %all-to-all-start) | async-done | bytes 622624 | tf_op jit(solution)/shard_map/all_to_all | solution.py:238
  62.2 0.1 reduce_sum.46
  62.3 0.0 copy-start.11
  62.4 0.6 pad_maximum_fusion.5
  63.0 5.5 %all-to-all-start.1 = ((f32[16,5,128]{2,1,0:T(8,128)}), f32[16,5,128]{2,1,0:T(8,128)S(1)}, u32[]{:S(2)}, u32[]{:S(2)}) async-start(f32[16,5,128]{2,1,0:T(8,128)} %pad_maximum_fusion.5), calls=%async_computation.1 | async-start | bytes 131072 | tf_op jit(solution)/shard_map/all_to_all | solution.py:238
  68.6 0.8 reduce-precision_convert_fusion.1
  69.4 0.1 copy.17.cot
  69.5 1.0 pad_maximum_fusion.3.w2
  70.6 9.6 %all-to-all-done.1.sums = f32[16,5,128]{2,1,0:T(8,128)S(1)} async-done(((f32[16,5,128]{2,1,0:T(8,128)}), f32[16,5,128]{2,1,0:T(8,128)S(1)}, u32[]{:S(2)}, u32[]{:S(2)}) %all-to-all-start.1) | async-done | bytes 40992 | tf_op jit(solution)/shard_map/all_to_all | solution.py:238
  80.1 1.1 copy-done.5
  81.2 4.5 %shard_map.120 = (f32[32,20,128]{2,1,0:T(8,128)}, f32[512,128]{1,0:T(8,128)}, f32[128,128]{1,0:T(8,128)S(1)}, f32[1,128]{1,0:T(1,128)}, f32[1096,128]{1,0:T(8,128)S(1)}) custom-call(f32[16,5,128]{2,1,0:T(8,128)S(1)} %all-to-all-done.1.sums, f32[512,128]{1,0:T(8,128)S(1)} %copy-done.1, f32[512,1]{1,0:T(8,128)S(1)} %copy.17.cot, f32[1224,128]{1,0:T(8,128)S(1)} %copy-done.5, ...), custom_call_target="tpu_custom_call" | custom-call | flops 1000000000 | bytes 4194304 | tf_op jit(solution)/shard_map/pallas_call | solution.py:197
  85.7 0.8 copy-done.6
  86.5 5.5 %all-to-all-start.2 = ((f32[32,20,128]{2,1,0:T(8,128)}), f32[32,20,128]{2,1,0:T(8,128)S(1)}, u32[]{:S(2)}, u32[]{:S(2)}) async-start(f32[32,20,128]{2,1,0:T(8,128)} %get-tuple-element.25), calls=%async_computation.2 | async-start | bytes 786432 | tf_op jit(solution)/shard_map/all_to_all | solution.py:238
  92.0 10.0 %all-to-all-done.2 = f32[32,20,128]{2,1,0:T(8,128)S(1)} async-done(((f32[32,20,128]{2,1,0:T(8,128)}), f32[32,20,128]{2,1,0:T(8,128)S(1)}, u32[]{:S(2)}, u32[]{:S(2)}) %all-to-all-start.2) | async-done | bytes 327712 | tf_op jit(solution)/shard_map/all_to_all | solution.py:238
  102.1 15.9 %all_to_all.25 = f32[16,23,128]{2,1,0:T(8,128)S(1)} all-to-all(f32[16,23,128]{2,1,0:T(8,128)S(1)} %broadcast_in_dim.43), channel_id=1, replica_groups=mesh['y'=4,'xl'=2,'c'=2,'z'=16,'xh'=2] {'z'}, dimensions={0} | all-to-all | bytes 376832 | tf_op jit(solution)/shard_map/all_to_all | solution.py:238
  118.1 1.0 broadcast_in_dim.44
  119.1 8.0 %all-to-all-start.4 = ((f32[32,56,128]{2,1,0:T(8,128)}), f32[32,56,128]{2,1,0:T(8,128)S(1)}, u32[]{:S(2)}, u32[]{:S(2)}) async-start(f32[32,56,128]{2,1,0:T(8,128)} %broadcast_in_dim.44), calls=%async_computation.4 | async-start | bytes 1835008 | tf_op jit(solution)/shard_map/all_to_all | solution.py:238
  127.1 0.2 copy.20
  127.5 0.0 copy-start.7
  127.5 0.1 reduce-precision_convert_fusion
  127.6 0.1 pad_maximum_fusion.4.r_1_
  127.7 0.9 copy-done.7
  128.5 2.3 %shard_map.121 = f32[15,45,69]{2,1,0:T(8,128)} custom-call(f32[1096,128]{1,0:T(8,128)S(1)} %copy-done.7, bf16[3,384,256]{2,1,0:T(8,128)(2,1)S(1)} %pad_maximum_fusion.4.r_1_), custom_call_target="tpu_custom_call" | custom-call | flops 1000000000 | bytes 4194304 | tf_op jit(solution)/shard_map/pallas_call | solution.py:197
  130.8 12.0 %all-to-all-done.4.whole = f32[32,56,128]{2,1,0:T(8,128)S(1)} async-done(((f32[32,56,128]{2,1,0:T(8,128)}), f32[32,56,128]{2,1,0:T(8,128)S(1)}, u32[]{:S(2)}, u32[]{:S(2)}) %all-to-all-start.4) | async-done | bytes 917536 | tf_op jit(solution)/shard_map/all_to_all | solution.py:238
  142.8 1.0 shard_map.122
  143.8 1.0 copy.19
  (38 shorter events, 0.4 us)
Async XLA Ops:
  1.6 14.1 %collective-permute-start = (f32[4,45,69]{2,1,0:T(8,128)S(1)}, f32[4,45,69]{2,1,0:T(8,128)S(1)}, u32[]{:S(2)}, u32[]{:S(2)}) collective-permute-start(f32[4,45,69]{2,1,0:T(8,128)S(1)} %get-tuple-element.55), channel_id=1, source_target_pairs={{0,32},{32,64},{64,96},{96,128},{128,160},{160,192},{192,224},{224... | collective-permute-start | bytes 149048 | tf_op jit(solution)/shard_map/ppermute | solution.py:223
  6.1 9.6 %collective-permute-start.1 = (f32[4,45,69]{2,1,0:T(8,128)S(1)}, f32[4,45,69]{2,1,0:T(8,128)S(1)}, u32[]{:S(2)}, u32[]{:S(2)}) collective-permute-start(f32[4,45,69]{2,1,0:T(8,128)S(1)} %get-tuple-element.54), channel_id=1, source_target_pairs={{32,0},{64,32},{96,64},{128,96},{160,128},{192,160},{224,192},{256... | collective-permute-start | bytes 149048 | tf_op jit(solution)/shard_map/ppermute | solution.py:224
  12.6 1.5 %copy-start.10 = (f32[9,128,69]{1,2,0:T(8,128)S(1)}, f32[9,128,69]{1,2,0:T(8,128)}, u32[]{:S(2)}) copy-start(f32[9,128,69]{1,2,0:T(8,128)} %param.8) | copy-start | bytes 953860
  14.2 19.7 %copy-start = (f32[69,15,45]{0,2,1:T(8,128)S(1)}, f32[69,15,45]{0,2,1:T(8,128)}, u32[]{:S(2)}) copy-start(f32[69,15,45]{0,2,1:T(8,128)} %param.7) | copy-start | bytes 558904
  14.2 19.7 %copy-start.2 = (f32[128]{0:T(128)S(1)}, f32[128]{0:T(128)}, u32[]{:S(2)}) copy-start(f32[128]{0:T(128)} %param.9) | copy-start | bytes 1540
  14.2 19.6 %copy-start.3 = (f32[128]{0:T(128)S(1)}, f32[128]{0:T(128)}, u32[]{:S(2)}) copy-start(f32[128]{0:T(128)} %param.11) | copy-start | bytes 1540
  15.8 11.7 %collective-permute-start.3 = (f32[23,4,69]{2,1,0:T(4,128)S(1)}, f32[23,4,69]{2,1,0:T(4,128)S(1)}, u32[]{:S(2)}, u32[]{:S(2)}) collective-permute-start(f32[23,4,69]{2,1,0:T(4,128)S(1)} %pad_maximum_fusion.7), channel_id=1, source_target_pairs={{1,0},{2,1},{3,2},{4,3},{5,4},{6,5},{7,6},{8,7},{9,8},{10,9},{11,1... | collective-permute-start | bytes 76184 | tf_op jit(solution)/shard_map/ppermute | solution.py:224
  25.4 8.4 %collective-permute-start.2 = (f32[23,4,69]{2,1,0:T(4,128)S(1)}, f32[23,4,69]{2,1,0:T(4,128)S(1)}, u32[]{:S(2)}, u32[]{:S(2)}) collective-permute-start(f32[23,4,69]{2,1,0:T(4,128)S(1)} %pad_maximum_fusion.6), channel_id=1, source_target_pairs={{0,1},{1,2},{2,3},{3,4},{4,5},{5,6},{6,7},{7,8},{8,9},{9,10},{10,1... | collective-permute-start | bytes 76184 | tf_op jit(solution)/shard_map/ppermute | solution.py:223
  38.8 1.6 %copy-start.4 = (f32[1224,128]{1,0:T(8,128)}, f32[1224,128]{1,0:T(8,128)S(1)}, u32[]{:S(2)}) copy-start(f32[1224,128]{1,0:T(8,128)S(1)} %get-tuple-element.20.s2) | copy-start | bytes 1880068
  41.4 8.0 %copy-start.8 = (f32[9,128,128]{2,1,0:T(8,128)S(1)}, f32[9,128,128]{2,1,0:T(8,128)}, u32[]{:S(2)}) copy-start(f32[9,128,128]{2,1,0:T(8,128)} %param.10) | copy-start | bytes 1769476
  41.4 20.9 %all-to-all-start = ((f32[32,38,128]{2,1,0:T(8,128)}), f32[32,38,128]{2,1,0:T(8,128)S(1)}, u32[]{:S(2)}, u32[]{:S(2)}) async-start(f32[32,38,128]{2,1,0:T(8,128)} %pad_maximum_fusion), calls=%async_computation | async-start | bytes 1310720 | tf_op jit(solution)/shard_map/all_to_all | solution.py:238
  50.2 18.3 %copy-start.9 = (f32[9,128,128]{2,1,0:T(8,128)S(1)}, f32[9,128,128]{2,1,0:T(8,128)}, u32[]{:S(2)}) copy-start(f32[9,128,128]{2,1,0:T(8,128)} %rev.6) | copy-start | bytes 1769476
  62.3 7.1 %copy-start.11 = (f32[512]{0:T(512)S(1)}, f32[512]{0:T(512)}, u32[]{:S(2)}) copy-start(f32[512]{0:T(512)} %param.13) | copy-start | bytes 6148
  63.0 17.1 %all-to-all-start.1 = ((f32[16,5,128]{2,1,0:T(8,128)}), f32[16,5,128]{2,1,0:T(8,128)S(1)}, u32[]{:S(2)}, u32[]{:S(2)}) async-start(f32[16,5,128]{2,1,0:T(8,128)} %pad_maximum_fusion.5), calls=%async_computation.1 | async-start | bytes 131072 | tf_op jit(solution)/shard_map/all_to_all | solution.py:238
  69.4 10.8 %copy-start.1 = (f32[512,128]{1,0:T(8,128)S(1)}, f32[512,128]{1,0:T(8,128)}, u32[]{:S(2)}) copy-start(f32[512,128]{1,0:T(8,128)} %modes.1) | copy-start | bytes 786436
  80.1 1.1 copy-start.5
  85.7 0.8 copy-start.6
  86.5 15.5 %all-to-all-start.2 = ((f32[32,20,128]{2,1,0:T(8,128)}), f32[32,20,128]{2,1,0:T(8,128)S(1)}, u32[]{:S(2)}, u32[]{:S(2)}) async-start(f32[32,20,128]{2,1,0:T(8,128)} %get-tuple-element.25), calls=%async_computation.2 | async-start | bytes 786432 | tf_op jit(solution)/shard_map/all_to_all | solution.py:238
  119.1 23.6 %all-to-all-start.4 = ((f32[32,56,128]{2,1,0:T(8,128)}), f32[32,56,128]{2,1,0:T(8,128)S(1)}, u32[]{:S(2)}, u32[]{:S(2)}) async-start(f32[32,56,128]{2,1,0:T(8,128)} %broadcast_in_dim.44), calls=%async_computation.4 | async-start | bytes 1835008 | tf_op jit(solution)/shard_map/all_to_all | solution.py:238
  127.5 1.1 copy-start.7

commit v3 on v2

v3 whole, which is shorter than its diff:
```python
import math

import jax
import jax.numpy as jnp
import numpy as np
from jax import lax
from jax.experimental import pallas as pl
from jax.experimental.pallas import tpu as pltpu
from jax.sharding import Mesh, PartitionSpec as P

LAT = ("y", "xl", "c")
LON = ("z", "xh")
CHIPS = ("y", "xl", "xh")
PLANE = ("y", "xl", "xh", "c")
RING = ("z",)
F32 = jnp.float32
BF16 = jnp.bfloat16

PITCH = 64
LANES = 128
ROWS, COLS, CIN = 15, 45, 69
WINDOW = 16 * PITCH
NX, N1, N2, N3 = 23 * PITCH, 21 * PITCH, 19 * PITCH, 17 * PITCH


def split(x):
    hi = x.astype(BF16)
    return hi, (x - hi.astype(F32)).astype(BF16)


def spread(src, high, low, start, stop):
    for r in range(start, stop, PITCH):
        for b in range(3):
            hi, lo = split(src[r + b : r + b + PITCH, :])
            high[r : r + PITCH, b * LANES : (b + 1) * LANES] = hi
            low[r : r + PITCH, b * LANES : (b + 1) * LANES] = lo


def dot(a, b):
    return jnp.dot(a, b, preferred_element_type=F32)


def convolve(high, low, weight, start, count):
    total = None
    for a in range(3):
        r = start + a * PITCH
        w = weight[a]
        both = dot(high[r : r + count, :], w)
        term = both[:, :LANES] + both[:, LANES:] + dot(low[r : r + count, :], w[:, :LANES])
        total = term if total is None else total + term
    return total


def correlate(grad, high, low, start):
    hi, lo = split(grad.T)
    both = jnp.concatenate([hi, lo], axis=0)
    blocks = []
    for a in range(3):
        r = start + a * PITCH
        x = high[r : r + WINDOW, :]
        out = dot(both, x)
        blocks.append(out[:LANES] + out[LANES:] + dot(hi, low[r : r + WINDOW, :]))
    return blocks


def chunks(rows, parts):
    size = -(-rows // parts)
    return [(s, min(size, rows - s)) for s in range(0, rows, size)]


def column_mask(first, shape):
    col = lax.broadcasted_iota(jnp.int32, shape, 0)
    return ((col >= first) & (col < first + COLS)).astype(F32)


def padded_rows(pad, block):
    pad[:CIN, :] = block
    return pad[...]


def store_weight(weight, t, block):
    a, b = t // 3, t % 3
    hi, lo = split(block)
    weight[a, b * LANES : (b + 1) * LANES, :LANES] = hi
    weight[a, b * LANES : (b + 1) * LANES, LANES:] = lo


def prepare_kernel(own, north, south, w_first, w_second, x, w1, w2, pad):
    x[...] = jnp.zeros_like(x)
    for i in range(ROWS + 8):
        r = i * PITCH
        row = north[i] if i < 4 else own[i - 4] if i < ROWS + 4 else south[i - ROWS - 4]
        x[r + 8 : r + 8 + COLS, :CIN] = row
    pad[...] = jnp.zeros_like(pad)
    for t in range(9):
        store_weight(w1, t, padded_rows(pad, w_first[t]))
        store_weight(w2, t, w_second[t].T)


def forward_kernel(weights, centre, west, east, w1, b1, w2, b2, cells, a1, s1, s2, small, x, slopes, high, low):
    x[...] = centre[...]
    for i in range(ROWS + 8):
        r = i * PITCH
        x[r + 4 : r + 8, :CIN] = west[i]
        x[r + 8 + COLS : r + 12 + COLS, :CIN] = east[i]
    spread(x, high, low, 0, NX)
    cells[...] = x[3 * PITCH : 21 * PITCH + 8, :]
    for first, rows in chunks(ROWS + 6, 3):
        acc = convolve(high, low, w1, first * PITCH, rows * PITCH)
        for k in range(rows):
            r = (first + k) * PITCH
            h = acc[k * PITCH : (k + 1) * PITCH] + b1[...]
            sigma = jax.nn.sigmoid(h)
            inside = jnp.where(weights[first + k] > 0.0, 1.0, 0.0)
            a1[r : r + PITCH, :] = h * sigma * inside
            slopes[r : r + PITCH, :] = sigma * (1.0 + h * (1.0 - sigma)) * inside
    a1[N1:, :] = jnp.zeros((8, LANES), F32)
    s1[...] = slopes[2 * PITCH + 2 : 2 * PITCH + 2 + N3, :]
    spread(a1, high, low, 0, N1)
    mask = column_mask(6, (PITCH, LANES))
    pooled = jnp.zeros((PITCH, LANES), F32)
    bias = jnp.zeros((PITCH, LANES), F32)
    for first, rows in chunks(ROWS + 4, 2):
        acc = convolve(high, low, w2, first * PITCH, rows * PITCH)
        for k in range(rows):
            i = first + k
            r = i * PITCH
            h = acc[k * PITCH : (k + 1) * PITCH] + b2[...]
            sigma = jax.nn.sigmoid(h)
            weight = weights[i + 1]
            slope = sigma * (1.0 + h * (1.0 - sigma)) * weight
            s2[r : r + PITCH, :] = slope
            if 2 <= i < ROWS + 2:
                pooled = pooled + h * sigma * weight
                bias = bias + slope
    s2[N2:, :] = jnp.zeros((8, LANES), F32)
    small[0:1, :] = jnp.sum(pooled * mask, axis=0, keepdims=True)
    small[1:2, :] = jnp.sum(bias * mask, axis=0, keepdims=True)


def write_pieces(out, rows, extra=None):
    count, size = out.shape[0], out.shape[1] - (0 if extra is None else extra.shape[0])
    for p in range(count):
        q = (p % 2) * (count // 2) + p // 2
        out[p, :size] = rows[q * size : (q + 1) * size, :]
        if extra is not None:
            out[p, size:] = extra[...]


def second_kernel(a1, s2, small, out, high, low, rows):
    spread(a1, high, low, 2 * PITCH, 20 * PITCH)
    mask = column_mask(6, (PITCH, LANES))
    own = [s2[(i + 2) * PITCH : (i + 3) * PITCH, :] * mask for i in range(ROWS)]
    grad = jnp.concatenate(own + [jnp.zeros((PITCH, LANES), F32)], axis=0)
    for a, block in enumerate(correlate(grad, high, low, 2 * PITCH)):
        for b in range(3):
            t = 3 * a + b
            rows[t * LANES : (t + 1) * LANES, :] = block[:, b * LANES : (b + 1) * LANES]
    write_pieces(out, rows, small)


def mode_gradients(sums, modes, cot):
    total = jnp.sum(sums[...], axis=0)
    pooled = total[0:1]
    amplitude = jnp.sum(modes[...] * pooled, axis=1, keepdims=True)
    count = amplitude.shape[0]
    column = jnp.concatenate(
        [jnp.broadcast_to(cot[k : k + 1, :], (LANES, LANES)).T[:, :1] for k in range(count // LANES)], axis=0
    )
    width = jnp.sqrt(jnp.sum(amplitude * amplitude, axis=0, keepdims=True) / count + 1e-05)
    normal = amplitude / width
    along = jnp.sum(column * normal, axis=0, keepdims=True) / count
    d_amplitude = (column - normal * along) / width
    d_pooled = jnp.sum(d_amplitude * modes[...], axis=0, keepdims=True)
    return total, pooled, d_amplitude, d_pooled


def backward_kernel(sums, modes, cot, s1, s2, x, w_second, out, g1, weight, rows, high, low):
    spread(s2, high, low, 0, N2)
    d_pooled = mode_gradients(sums, modes, cot)[3]
    column = jnp.broadcast_to(d_pooled, (LANES, LANES)).T
    for t in range(9):
        store_weight(weight, t, w_second[8 - t] * column)
    for first, count in chunks(ROWS + 2, 2):
        r, n = first * PITCH, count * PITCH
        g1[r : r + n, :] = convolve(high, low, weight, r, n) * s1[r : r + n, :]
    g1[N3:, :] = jnp.zeros((8, LANES), F32)

    mask = column_mask(7, (PITCH, LANES))
    own = [g1[(i + 1) * PITCH - 2 : (i + 2) * PITCH - 2, :] * mask for i in range(ROWS)]
    bias1 = own[0]
    for row in own[1:]:
        bias1 = bias1 + row
    grad = jnp.concatenate(own + [jnp.zeros((PITCH, LANES), F32)], axis=0)
    spread(x, high, low, 0, 18 * PITCH)
    for a, block in enumerate(correlate(grad, high, low, 0)):
        for b in range(3):
            t = 3 * a + b
            rows[t * CIN : (t + 1) * CIN, :] = block[:, b * LANES : (b + 1) * LANES].T[:CIN]
    rows[9 * CIN : 9 * CIN + 1, :] = jnp.sum(bias1, axis=0, keepdims=True)
    rows[9 * CIN + 1 :, :] = jnp.zeros((rows.shape[0] - 9 * CIN - 1, LANES), F32)
    write_pieces(out, rows)


def field_kernel(scale, g1, w_first, sums, modes, cot, out, d_modes, spread_d, bias2, weight, pad, high, low):
    total, pooled, d_amplitude, d_pooled = mode_gradients(sums, modes, cot)
    d_modes[...] = d_amplitude * pooled
    spread_d[...] = jnp.broadcast_to(d_pooled, (LANES, LANES)).T
    bias2[...] = total[1:2] * d_pooled
    pad[...] = jnp.zeros_like(pad)
    for t in range(9):
        store_weight(weight, t, padded_rows(pad, w_first[8 - t]).T)
    spread(g1, high, low, 0, N3)
    for first, count in chunks(ROWS, 2):
        acc = convolve(high, low, weight, first * PITCH, count * PITCH) * scale
        for k in range(count):
            out[first + k] = acc[k * PITCH + 4 : k * PITCH + 4 + COLS, :CIN]


def finish_kernel(core, mine, other, spread_d, w_second, w_first, b_first, rows):
    chips = mine.shape[0]
    size = 9 * LANES // (2 * chips)
    rest = mine.shape[1] - size
    even = core[0] == 0

    def gather(start, count):
        for p in range(chips):
            m, o = mine[p, start : start + count, :], other[p, start : start + count, :]
            rows[p * count : (p + 1) * count, :] = jnp.where(even, m, o)
            rows[(chips + p) * count : (chips + p + 1) * count, :] = jnp.where(even, o, m)

    gather(0, size)
    for t in range(9):
        w_second[t] = rows[t * LANES : (t + 1) * LANES, :] * spread_d[...]
    gather(size, rest)
    for t in range(9):
        w_first[t] = rows[t * CIN : (t + 1) * CIN, :]
    b_first[...] = rows[9 * CIN : 9 * CIN + 1, :]


def call(kernel, outs, scratch, flops, smem=()):
    outs = [o if isinstance(o[0], tuple) else (o, F32) for o in outs]

    def run(*args):
        ins = [pl.BlockSpec(memory_space=pltpu.SMEM if i in smem else pltpu.VMEM) for i in range(len(args))]
        return pl.pallas_call(
            kernel,
            out_shape=[jax.ShapeDtypeStruct(s, d) for s, d in outs],
            in_specs=ins,
            out_specs=[pl.BlockSpec(memory_space=pltpu.VMEM) for _ in outs],
            scratch_shapes=[pltpu.VMEM(s, d) for s, d in scratch],
            compiler_params=pltpu.CompilerParams(vmem_limit_bytes=12 << 20),
            cost_estimate=pl.CostEstimate(flops=flops, bytes_accessed=4 << 20, transcendentals=0),
        )(*args)

    return run


def edges(cells, axes, dim, width, closed):
    count = lax.axis_size(axes)
    ends = count if closed else count - 1
    head = lax.slice_in_dim(cells, 0, width, axis=dim)
    tail = lax.slice_in_dim(cells, cells.shape[dim] - width, cells.shape[dim], axis=dim)
    before = lax.ppermute(tail, axes, [(i, (i + 1) % count) for i in range(ends)])
    after = lax.ppermute(head, axes, [((i + 1) % count, i) for i in range(ends)])
    return before, after


def row_weights(first, count, nlat, nlon):
    phi = (np.arange(nlat) + 0.5) * (math.pi / nlat) - math.pi / 2
    area = np.cos(phi) / (np.cos(phi).sum() * nlon)
    table = np.zeros(nlat + 2 * count, np.float32)
    table[count : count + nlat] = area
    return lax.dynamic_slice(jnp.asarray(table), (first + count,), (count,))


def swap(pieces, axes):
    return lax.all_to_all(pieces, axes, 0, 0, tiled=True)


def to_all(piece, axes):
    return swap(jnp.broadcast_to(piece[None], (lax.axis_size(axes),) + piece.shape), axes)


def fill(rows, count):
    return jnp.pad(rows, ((0, count - rows.shape[0]), (0, 0)))


def body(field, w_first, b_first, w_second, b_second, modes, cotangent):
    cin, rows, cols = field.shape
    ch = w_first.shape[1]
    n_lat, n_lon = lax.axis_size(LAT), lax.axis_size(LON)
    n_pl, n_z = lax.axis_size(PLANE), lax.axis_size(RING)
    nlat, nlon = rows * n_lat, cols * n_lon
    weights = row_weights(lax.axis_index(LAT) * rows - 3, 24, nlat, nlon)

    own = field.transpose(1, 2, 0)
    north, south = edges(own, LAT, 0, 4, False)
    left = jnp.concatenate([north[:, :4], own[:, :4], south[:, :4]], axis=0)
    right = jnp.concatenate([north[:, cols - 4 :], own[:, cols - 4 :], south[:, cols - 4 :]], axis=0)
    west, east = edges(jnp.concatenate([left, right], axis=1), LON, 1, 4, True)
    w_first = w_first.transpose(0, 2, 1)
    weight = ((3, 3 * LANES, 2 * LANES), BF16)
    pad = ((LANES, LANES), F32)
    pair = lambda n: [((n, 3 * LANES), BF16), ((n, 3 * LANES), BF16)]
    centre, w1, w2 = call(prepare_kernel, [(NX + 8, LANES), weight, weight], [pad], 10**9)(own, north, south, w_first, w_second)
    x, a1, s1, s2, small = call(
        forward_kernel,
        [(18 * PITCH + 8, LANES), (N1 + 8, LANES), (N3, LANES), (N2 + 8, LANES), (2, LANES)],
        [((NX + 8, LANES), F32), ((N1, LANES), F32)] + pair(NX),
        10**9,
        (0,),
    )(weights, centre, west, east, w1, b_first[None], w2, b_second[None])

    share2 = 9 * ch // n_pl
    (part,) = call(second_kernel, [(n_pl, share2 + 2, ch)], pair(20 * PITCH) + [((9 * ch, LANES), F32)], 10**9)(a1, s2, small)

    part = jnp.sum(swap(part, PLANE), axis=0)
    bit2 = -(-share2 // n_z)
    mine = fill(part[:share2], bit2 * n_z).reshape(n_z, bit2, ch)
    mine = jnp.concatenate([jnp.broadcast_to(part[None, share2:], (n_z, 2, ch)), mine], axis=1)
    mine = swap(mine, RING)
    piece2 = jnp.sum(mine[:, 2:], axis=0)

    share1 = -(-(9 * cin + 1) // n_pl)
    cot = cotangent.reshape(-1, LANES)
    g1rows, g1 = call(
        backward_kernel,
        [(n_pl, share1, ch), (N3 + 8, LANES)],
        [weight, ((n_pl * share1, LANES), F32)] + pair(N2),
        10**9,
    )(mine, modes, cot, s1, s2, x, w_second)

    part = jnp.sum(swap(g1rows, PLANE), axis=0)
    grad_field, d_modes, spread_d, bias2 = call(
        lambda *r: field_kernel(float(nlat * nlon), *r),
        [(rows, cols, cin), modes.shape, (LANES, LANES), (1, LANES)],
        [weight, pad] + pair(N3),
        10**9,
    )(g1, w_first, mine, modes, cot)
    part, grad_field = lax.optimization_barrier((part, grad_field))

    both = to_all(jnp.concatenate([part, piece2]), RING)
    part = jnp.sum(both[:, :share1], axis=0)
    piece2 = both[:, share1:].reshape(n_z * bit2, ch)[:share2]
    whole = to_all(jnp.concatenate([piece2, part]), CHIPS)
    other = lax.ppermute(whole, "c", [(0, 1), (1, 0)])
    core = lax.axis_index("c").astype(jnp.int32).reshape(1)
    grad_w_second, grad_w_first, grad_b_first = call(
        finish_kernel,
        [(9, ch, ch), (9, cin, ch), (1, ch)],
        [((9 * ch, LANES), F32)],
        10**6,
        (0,),
    )(core, whole, other, spread_d)
    return (grad_field.transpose(2, 0, 1), grad_w_first.transpose(0, 2, 1), grad_b_first[0], grad_w_second, bias2[0], d_modes)


def solution(mesh):
    fine = Mesh(mesh.devices.reshape(4, 2, 2, 16, 2), ("y", "xl", "c", "z", "xh"))
    in_specs = (P(None, LAT, LON), P(), P(), P(), P(), P(), P())
    out_specs = (P(None, LAT, LON), P(), P(), P(), P(), P())
    return jax.shard_map(body, mesh=fine, in_specs=in_specs, out_specs=out_specs, check_vma=False)
```

time: 146 us -> 139 us (0.952)
  blocking collectives: 15.9 us -> 71.8 us
  waiting for transfers between devices: 50 us -> 9.82 us
  starting transfers between devices: 48.6 us -> 34.5 us
  other arithmetic: 4.8 us -> 0.21 us
  local copies, waits for them, and re-layouts: 9.37 us -> 6.17 us
    all_to_all x1 -> x4, blocking collectives: 15.9 us -> 71.8 us  [swap(): return lax.all_to_all(pieces, axes, 0, 0, tiled=True)]
    all_to_all x4 -> x1, waiting for transfers between devices: 43.5 us -> 7.58 us  [swap(): return lax.all_to_all(pieces, axes, 0, 0, tiled=True)]
    all_to_all x4 -> x1, starting transfers between devices: 27 us -> 5.5 us  [swap(): return lax.all_to_all(pieces, axes, 0, 0, tiled=True)]
    ppermute x0 -> x1, starting transfers between devices: none -> 7.13 us  [body(): other = lax.ppermute(whole, 'c', [(0, 1), (1, 0)])]
    ppermute x2, waiting for transfers between devices: 6.44 us -> 0.8 us  [edges(): lax.ppermute(tail, axes, [(i, (i + 1) % count) for i in range(ends)])]
    ppermute x2, starting transfers between devices: 15.2 us -> 18.1 us  [edges(): lax.ppermute(head, axes, [((i + 1) % count, i) for i in range(ends)])]
    ppermute x2, starting transfers between devices: 6.43 us -> 3.84 us  [edges(): lax.ppermute(tail, axes, [(i, (i + 1) % count) for i in range(ends)])]
    concatenate x5 -> x1, other arithmetic: 2.17 us -> 0.01 us  [body(): whole = to_all(jnp.concatenate([piece2, part]), CHIPS)]
  transfers between devices with their start and end apart: 8 -> 6, of which waited for: 5 -> 3; matrix products, arithmetic and copies ran while one was open for 5% -> 1% of each run, Pallas kernels for 2% -> 2%
where the time goes in v3:
time: 139 us; the launch traced here: 138 us
  blocking collectives  71.8 us (52%)
  starting transfers between devices  34.5 us (25%)
  Pallas kernels  14.9 us (11%)
  waiting for transfers between devices  9.82 us (7%)
  local copies, waits for them, and re-layouts  6.17 us (4%)
    all_to_all x4, blocking collectives, swap(): return lax.all_to_all(pieces, axes, 0, 0, tiled=True)  71.8 us
    ppermute x2, starting transfers between devices, edges(): lax.ppermute(head, axes, [((i + 1) % count, i) for i in range(ends)])  18.1 us
    pallas_call x6, Pallas kernels, run(): pl.pallas_call(kernel, out_shape=[jax.ShapeDtypeStruct(s, d) for s, d in...  14.9 us
    all_to_all x1, waiting for transfers between devices, swap(): return lax.all_to_all(pieces, axes, 0, 0, tiled=True)  7.58 us
    ppermute x1, starting transfers between devices, body(): other = lax.ppermute(whole, 'c', [(0, 1), (1, 0)])  7.13 us
    all_to_all x1, starting transfers between devices, swap(): return lax.all_to_all(pieces, axes, 0, 0, tiled=True)  5.5 us
    unnamed x20, local copies, waits for them, and re-layouts  4.26 us
    ppermute x2, starting transfers between devices, edges(): lax.ppermute(tail, axes, [(i, (i + 1) % count) for i in range(ends)])  3.84 us
  transfers between devices with their start and end apart: 6, of which 3 were waited for; matrix products, arithmetic and copies ran while one was open for 1% of the time, Pallas kernels for 2%

profile of v3, /device:TPU:1, one launch (start us, length us, event | category | flops | bytes accessed | tf_op | source)
XLA Modules:
  0.0 138.3 jit_solution(9490106485793120892)
XLA Ops:
  0.6 0.0 copy-start
  0.6 0.0 copy-start.3
  0.7 1.0 fusion.1
  1.7 8.8 %collective-permute-start.1 = (f32[4,45,69]{2,1,0:T(8,128)S(1)}, f32[4,45,69]{2,1,0:T(8,128)S(1)}, u32[]{:S(2)}, u32[]{:S(2)}) collective-permute-start(f32[4,45,69]{2,1,0:T(8,128)S(1)} %get-tuple-element.46), channel_id=1, source_target_pairs={{32,0},{64,32},{96,64},{128,96},{160,128},{192,160},{224,192},{256... | collective-permute-start | bytes 149048 | tf_op jit(solution)/shard_map/ppermute | solution.py:265
  10.5 1.9 %collective-permute-start = (f32[4,45,69]{2,1,0:T(8,128)S(1)}, f32[4,45,69]{2,1,0:T(8,128)S(1)}, u32[]{:S(2)}, u32[]{:S(2)}) collective-permute-start(f32[4,45,69]{2,1,0:T(8,128)S(1)} %get-tuple-element.47), channel_id=1, source_target_pairs={{0,32},{32,64},{64,96},{96,128},{128,160},{160,192},{192,224},{224... | collective-permute-start | bytes 149048 | tf_op jit(solution)/shard_map/ppermute | solution.py:264
  12.4 0.0 copy-done
  12.4 0.8 dynamic_slice.3.weights
  13.2 0.0 collective-permute-done.1.south
  13.2 0.8 collective-permute-done.north
  14.0 1.9 %collective-permute-start.2 = (f32[23,4,69]{2,1,0:T(4,128)S(1)}, f32[23,4,69]{2,1,0:T(4,128)S(1)}, u32[]{:S(2)}, u32[]{:S(2)}) collective-permute-start(f32[23,4,69]{2,1,0:T(4,128)S(1)} %pad_maximum_fusion.1), channel_id=1, source_target_pairs={{0,1},{1,2},{2,3},{3,4},{4,5},{5,6},{6,7},{7,8},{8,9},{9,10},{10,1... | collective-permute-start | bytes 76184 | tf_op jit(solution)/shard_map/ppermute | solution.py:264
  16.0 9.3 %collective-permute-start.3 = (f32[23,4,69]{2,1,0:T(4,128)S(1)}, f32[23,4,69]{2,1,0:T(4,128)S(1)}, u32[]{:S(2)}, u32[]{:S(2)}) collective-permute-start(f32[23,4,69]{2,1,0:T(4,128)S(1)} %pad_maximum_fusion.2), channel_id=1, source_target_pairs={{1,0},{2,1},{3,2},{4,3},{5,4},{6,5},{7,6},{8,7},{9,8},{10,9},{11,1... | collective-permute-start | bytes 76184 | tf_op jit(solution)/shard_map/ppermute | solution.py:265
  25.3 0.0 copy-done.3
  25.3 0.0 copy-start.1
  25.3 1.1 copy-done.1
  26.3 0.3 shard_map.127
  26.7 0.0 collective-permute-done.2.west
  26.7 0.0 collective-permute-done.3.east
  26.7 0.0 copy-start.6
  26.7 0.0 copy-start.7
  26.7 0.6 copy-done.6
  27.4 0.0 copy-done.7
  27.4 4.9 %shard_map.128 = (f32[1160,128]{1,0:T(8,128)S(1)}, f32[1352,128]{1,0:T(8,128)S(1)}, f32[1088,128]{1,0:T(8,128)S(1)}, f32[1224,128]{1,0:T(8,128)S(1)}, f32[2,128]{1,0:T(2,128)S(1)}) custom-call(f32[24]{0:T(128)S(1)} %dynamic_slice.3.weights, f32[1480,128]{1,0:T(8,128)S(1)} %get-tuple-element.25.centre, f32[23,4,69]{2,1,0:T(4,128)S(1)} %collective-permute-done.2.west, ...), custom_call_target="tpu_custom_call" | custom-call | flops 1000000000 | bytes 4194304 | tf_op jit(solution)/shard_map/pallas_call | solution.py:246
  32.3 0.0 copy-start.8
  32.3 0.8 copy-done.8
  33.1 1.6 %shard_map.129 = f32[32,38,128]{2,1,0:T(8,128)S(1)} custom-call(f32[1352,128]{1,0:T(8,128)S(1)} %get-tuple-element.28.a1, f32[1224,128]{1,0:T(8,128)S(1)} %get-tuple-element.29.s2, f32[2,128]{1,0:T(2,128)S(1)} %get-tuple-element.30.small), custom_call_target="tpu_custom_call" | custom-call | flops 1000000000 | bytes 4194304 | tf_op jit(solution)/shard_map/pallas_call | solution.py:246
  34.7 20.7 %all_to_all.25 = f32[32,38,128]{2,1,0:T(8,128)S(1)} all-to-all(f32[32,38,128]{2,1,0:T(8,128)S(1)} %shard_map.129), channel_id=1, replica_groups=mesh['y'=4,'xl'=2,'c'=2,'z'=16,'xh'=2] {'y','xl','xh','c'}, dimensions={0} | all-to-all | bytes 1245184 | tf_op jit(solution)/shard_map/all_to_all | solution.py:278
  55.4 0.0 copy-start.2
  55.4 0.1 reduce_sum.36
  55.4 0.0 copy-start.4
  55.5 23.7 %all_to_all.26.sums.r_2_ = f32[16,5,128]{2,1,0:T(8,128)S(1)} all-to-all(f32[16,5,128]{2,1,0:T(8,128)S(1)} %pad_maximum_fusion), channel_id=1, replica_groups=mesh['y'=4,'xl'=2,'c'=2,'z'=16,'xh'=2] {'z'}, dimensions={0} | all-to-all | bytes 81920 | tf_op jit(solution)/shard_map/all_to_all | solution.py:278
  79.2 0.0 copy-start.5
  79.2 0.0 copy-done.2
  79.2 0.0 copy-done.4
  79.2 0.7 copy-done.5
  79.9 0.0 copy-start.9
  79.9 1.1 copy-done.9
  80.9 4.6 %shard_map.130 = (f32[32,20,128]{2,1,0:T(8,128)}, f32[1096,128]{1,0:T(8,128)S(1)}) custom-call(f32[16,5,128]{2,1,0:T(8,128)S(1)} %all_to_all.26.sums.r_2_, f32[512,128]{1,0:T(8,128)S(1)} %copy-done.4, f32[4,128]{1,0:T(4,128)S(1)} %bitcast.16, f32[1088,128]{1,0:T(8,128)S(1)} %copy-done.9, f32[1224,128]{1,0:T(8,128)S(1)} %get-tuple-element.29.s2, ...), custom_call_target="tpu_custom_call" | custom-call | flops 1000000000 | bytes 4194304 | tf_op jit(solution)/shard_map/pallas_call | solution.py:246
  85.5 5.5 %all-to-all-start.2 = ((f32[32,20,128]{2,1,0:T(8,128)}), f32[32,20,128]{2,1,0:T(8,128)S(1)}, u32[]{:S(2)}, u32[]{:S(2)}) async-start(f32[32,20,128]{2,1,0:T(8,128)} %get-tuple-element.33), calls=%async_computation.2 | async-start | bytes 786432 | tf_op jit(solution)/shard_map/all_to_all | solution.py:278
  91.0 2.4 %shard_map.131 = (f32[15,45,69]{2,1,0:T(8,128)}, f32[512,128]{1,0:T(8,128)}, f32[128,128]{1,0:T(8,128)S(1)}, f32[1,128]{1,0:T(1,128)}) custom-call(f32[1096,128]{1,0:T(8,128)S(1)} %get-tuple-element.34.r_0_, f32[9,69,128]{2,1,0:T(8,128)S(1)} %bitcast.15, f32[16,5,128]{2,1,0:T(8,128)S(1)} %all_to_all.26.sums.r_2_, f32[512,128]{1,0:T(8,128)S(1)} %copy-done.4, ...), custom_call_target="tpu_custom_call" | custom-call | flops 1000000000 | bytes 4194304 | tf_op jit(solution)/shard_map/pallas_call | solution.py:246
  93.5 7.6 %all-to-all-done.2 = f32[32,20,128]{2,1,0:T(8,128)S(1)} async-done(((f32[32,20,128]{2,1,0:T(8,128)}), f32[32,20,128]{2,1,0:T(8,128)S(1)}, u32[]{:S(2)}, u32[]{:S(2)}) %all-to-all-start.2) | async-done | bytes 327712 | tf_op jit(solution)/shard_map/all_to_all | solution.py:278
  101.2 15.8 %all_to_all.27 = f32[16,23,128]{2,1,0:T(8,128)S(1)} all-to-all(f32[16,23,128]{2,1,0:T(8,128)S(1)} %broadcast_in_dim.13), channel_id=1, replica_groups=mesh['y'=4,'xl'=2,'c'=2,'z'=16,'xh'=2] {'z'}, dimensions={0} | all-to-all | bytes 376832 | tf_op jit(solution)/shard_map/all_to_all | solution.py:278
  117.0 11.6 %all_to_all.28.mine = f32[16,56,128]{2,1,0:T(8,128)S(1)} all-to-all(f32[16,56,128]{2,1,0:T(8,128)S(1)} %broadcast_in_dim.28), channel_id=1, replica_groups=mesh['y'=4,'xl'=2,'c'=2,'z'=16,'xh'=2] {'y','xl','xh'}, dimensions={0} | all-to-all | bytes 917504 | tf_op jit(solution)/shard_map/all_to_all | solution.py:278
  128.7 7.1 %collective-permute-start.4 = (f32[16,56,128]{2,1,0:T(8,128)S(1)}, f32[16,56,128]{2,1,0:T(8,128)S(1)}, u32[]{:S(2)}, u32[]{:S(2)}) collective-permute-start(f32[16,56,128]{2,1,0:T(8,128)S(1)} %all_to_all.28.mine), channel_id=1, source_target_pairs={{0,32},{32,0},{1,33},{33,1},{2,34},{34,2},{3,35},{35,3},{4,36},{36... | collective-permute-start | bytes 1376264 | tf_op jit(solution)/shard_map/ppermute | solution.py:347
  135.8 1.4 %collective-permute-done.4.other = f32[16,56,128]{2,1,0:T(8,128)S(1)} collective-permute-done((f32[16,56,128]{2,1,0:T(8,128)S(1)}, f32[16,56,128]{2,1,0:T(8,128)S(1)}, u32[]{:S(2)}, u32[]{:S(2)}) %collective-permute-start.4) | collective-permute-done | bytes 458784 | tf_op jit(solution)/shard_map/ppermute | solution.py:347
  137.2 1.0 shard_map.132
  (19 shorter events, 0.3 us)
Async XLA Ops:
  0.6 11.8 %copy-start = (f32[69,15,45]{0,2,1:T(8,128)S(1)}, f32[69,15,45]{0,2,1:T(8,128)}, u32[]{:S(2)}) copy-start(f32[69,15,45]{0,2,1:T(8,128)} %param.8) | copy-start | bytes 558904
  0.6 24.6 %copy-start.3 = (f32[9,128,69]{1,2,0:T(8,128)S(1)}, f32[9,128,69]{1,2,0:T(8,128)}, u32[]{:S(2)}) copy-start(f32[9,128,69]{1,2,0:T(8,128)} %param.9) | copy-start | bytes 953860
  1.7 11.5 %collective-permute-start.1 = (f32[4,45,69]{2,1,0:T(8,128)S(1)}, f32[4,45,69]{2,1,0:T(8,128)S(1)}, u32[]{:S(2)}, u32[]{:S(2)}) collective-permute-start(f32[4,45,69]{2,1,0:T(8,128)S(1)} %get-tuple-element.46), channel_id=1, source_target_pairs={{32,0},{64,32},{96,64},{128,96},{160,128},{192,160},{224,192},{256... | collective-permute-start | bytes 149048 | tf_op jit(solution)/shard_map/ppermute | solution.py:265
  10.5 3.5 %collective-permute-start = (f32[4,45,69]{2,1,0:T(8,128)S(1)}, f32[4,45,69]{2,1,0:T(8,128)S(1)}, u32[]{:S(2)}, u32[]{:S(2)}) collective-permute-start(f32[4,45,69]{2,1,0:T(8,128)S(1)} %get-tuple-element.47), channel_id=1, source_target_pairs={{0,32},{32,64},{64,96},{96,128},{128,160},{160,192},{192,224},{224... | collective-permute-start | bytes 149048 | tf_op jit(solution)/shard_map/ppermute | solution.py:264
  14.0 12.7 %collective-permute-start.2 = (f32[23,4,69]{2,1,0:T(4,128)S(1)}, f32[23,4,69]{2,1,0:T(4,128)S(1)}, u32[]{:S(2)}, u32[]{:S(2)}) collective-permute-start(f32[23,4,69]{2,1,0:T(4,128)S(1)} %pad_maximum_fusion.1), channel_id=1, source_target_pairs={{0,1},{1,2},{2,3},{3,4},{4,5},{5,6},{6,7},{7,8},{8,9},{9,10},{10,1... | collective-permute-start | bytes 76184 | tf_op jit(solution)/shard_map/ppermute | solution.py:264
  16.0 10.7 %collective-permute-start.3 = (f32[23,4,69]{2,1,0:T(4,128)S(1)}, f32[23,4,69]{2,1,0:T(4,128)S(1)}, u32[]{:S(2)}, u32[]{:S(2)}) collective-permute-start(f32[23,4,69]{2,1,0:T(4,128)S(1)} %pad_maximum_fusion.2), channel_id=1, source_target_pairs={{1,0},{2,1},{3,2},{4,3},{5,4},{6,5},{7,6},{8,7},{9,8},{10,9},{11,1... | collective-permute-start | bytes 76184 | tf_op jit(solution)/shard_map/ppermute | solution.py:265
  25.3 1.1 copy-start.1
  26.7 0.7 copy-start.6
  26.7 0.7 copy-start.7
  32.3 0.8 copy-start.8
  55.4 23.8 %copy-start.2 = (f32[9,128,128]{2,1,0:T(8,128)S(1)}, f32[9,128,128]{2,1,0:T(8,128)}, u32[]{:S(2)}) copy-start(f32[9,128,128]{2,1,0:T(8,128)} %w_second.3) | copy-start | bytes 1769476
  55.4 23.8 %copy-start.4 = (f32[512,128]{1,0:T(8,128)S(1)}, f32[512,128]{1,0:T(8,128)}, u32[]{:S(2)}) copy-start(f32[512,128]{1,0:T(8,128)} %r_3_.1) | copy-start | bytes 786436
  79.2 0.7 copy-start.5
  79.9 1.1 copy-start.9
  85.5 15.5 %all-to-all-start.2 = ((f32[32,20,128]{2,1,0:T(8,128)}), f32[32,20,128]{2,1,0:T(8,128)S(1)}, u32[]{:S(2)}, u32[]{:S(2)}) async-start(f32[32,20,128]{2,1,0:T(8,128)} %get-tuple-element.33), calls=%async_computation.2 | async-start | bytes 786432 | tf_op jit(solution)/shard_map/all_to_all | solution.py:278
  128.7 8.6 %collective-permute-start.4 = (f32[16,56,128]{2,1,0:T(8,128)S(1)}, f32[16,56,128]{2,1,0:T(8,128)S(1)}, u32[]{:S(2)}, u32[]{:S(2)}) collective-permute-start(f32[16,56,128]{2,1,0:T(8,128)S(1)} %all_to_all.28.mine), channel_id=1, source_target_pairs={{0,32},{32,0},{1,33},{33,1},{2,34},{34,2},{3,35},{35,3},{4,36},{36... | collective-permute-start | bytes 1376264 | tf_op jit(solution)/shard_map/ppermute | solution.py:347

commit v4 on v3

--- a/solution.py
+++ b/solution.py
@@ -36,19 +36,30 @@
             low[r : r + PITCH, b * LANES : (b + 1) * LANES] = lo
 
 
+def spread_packed(src, high, low, start, stop):
+    lane = lax.broadcasted_iota(jnp.int32, (PITCH, LANES), 1)
+    for r in range(start, stop, PITCH):
+        second = pltpu.roll(src[r + 1 : r + 1 + PITCH, :], CIN, 1)
+        third = pltpu.roll(src[r + 2 : r + 2 + PITCH, :], 2 * CIN - LANES, 1)
+        for k, x in enumerate(
+            (jnp.where(lane < CIN, src[r : r + PITCH, :], second), jnp.where(lane < 2 * CIN - LANES, second, third))
+        ):
+            hi, lo = split(x)
+            high[r : r + PITCH, k * LANES : (k + 1) * LANES] = hi
+            low[r : r + PITCH, k * LANES : (k + 1) * LANES] = lo
+
+
 def dot(a, b):
     return jnp.dot(a, b, preferred_element_type=F32)
 
 
 def convolve(high, low, weight, start, count):
-    total = None
-    for a in range(3):
-        r = start + a * PITCH
-        w = weight[a]
-        both = dot(high[r : r + count, :], w)
-        term = both[:, :LANES] + both[:, LANES:] + dot(low[r : r + count, :], w[:, :LANES])
-        total = term if total is None else total + term
-    return total
+    def taps(src):
+        return jnp.concatenate([src[start + a * PITCH : start + a * PITCH + count, :] for a in range(3)], axis=1)
+
+    w = jnp.concatenate([weight[a] for a in range(3)], axis=0)
+    both = dot(taps(high), w)
+    return both[:, :LANES] + both[:, LANES:] + dot(taps(low), w[:, :LANES])
 
 
 def correlate(grad, high, low, start):
@@ -92,24 +103,31 @@
         row = north[i] if i < 4 else own[i - 4] if i < ROWS + 4 else south[i - ROWS - 4]
         x[r + 8 : r + 8 + COLS, :CIN] = row
     pad[...] = jnp.zeros_like(pad)
+    for a in range(3):
+        for b in range(3):
+            pad[b * CIN : (b + 1) * CIN, :] = w_first[3 * a + b]
+        hi, lo = split(pad[...])
+        w1[a, :, :LANES] = hi
+        w1[a, :, LANES:] = lo
     for t in range(9):
-        store_weight(w1, t, padded_rows(pad, w_first[t]))
         store_weight(w2, t, w_second[t].T)
 
 
-def forward_kernel(weights, centre, west, east, w1, b1, w2, b2, cells, a1, s1, s2, small, x, slopes, high, low):
+def forward_kernel(consts, centre, west, east, w1, w2, cells, a1, s1, s2, small, x, slopes, high, low, high1, low1):
+    b1, b2 = consts[0:1, :], consts[1:2, :]
+    weights = [consts[6:7, i : i + 1] for i in range(ROWS + 6)]
     x[...] = centre[...]
     for i in range(ROWS + 8):
         r = i * PITCH
         x[r + 4 : r + 8, :CIN] = west[i]
         x[r + 8 + COLS : r + 12 + COLS, :CIN] = east[i]
-    spread(x, high, low, 0, NX)
     cells[...] = x[3 * PITCH : 21 * PITCH + 8, :]
-    for first, rows in chunks(ROWS + 6, 3):
-        acc = convolve(high, low, w1, first * PITCH, rows * PITCH)
+    spread_packed(x, high1, low1, 0, NX)
+    for first, rows in chunks(ROWS + 6, 2):
+        acc = convolve(high1, low1, w1, first * PITCH, rows * PITCH)
         for k in range(rows):
             r = (first + k) * PITCH
-            h = acc[k * PITCH : (k + 1) * PITCH] + b1[...]
+            h = acc[k * PITCH : (k + 1) * PITCH] + b1
             sigma = jax.nn.sigmoid(h)
             inside = jnp.where(weights[first + k] > 0.0, 1.0, 0.0)
             a1[r : r + PITCH, :] = h * sigma * inside
@@ -125,7 +143,7 @@
         for k in range(rows):
             i = first + k
             r = i * PITCH
-            h = acc[k * PITCH : (k + 1) * PITCH] + b2[...]
+            h = acc[k * PITCH : (k + 1) * PITCH] + b2
             sigma = jax.nn.sigmoid(h)
             weight = weights[i + 1]
             slope = sigma * (1.0 + h * (1.0 - sigma)) * weight
@@ -159,29 +177,61 @@
     write_pieces(out, rows, small)
 
 
-def mode_gradients(sums, modes, cot):
+def mode_gradients(sums, modes, consts):
     total = jnp.sum(sums[...], axis=0)
     pooled = total[0:1]
     amplitude = jnp.sum(modes[...] * pooled, axis=1, keepdims=True)
     count = amplitude.shape[0]
-    column = jnp.concatenate(
-        [jnp.broadcast_to(cot[k : k + 1, :], (LANES, LANES)).T[:, :1] for k in range(count // LANES)], axis=0
+    cotangent = jnp.concatenate(
+        [jnp.broadcast_to(consts[k : k + 1, :], (LANES, LANES)).T[:, :1] for k in range(2, 2 + count // LANES)], axis=0
     )
     width = jnp.sqrt(jnp.sum(amplitude * amplitude, axis=0, keepdims=True) / count + 1e-05)
     normal = amplitude / width
-    along = jnp.sum(column * normal, axis=0, keepdims=True) / count
-    d_amplitude = (column - normal * along) / width
+    along = jnp.sum(cotangent * normal, axis=0, keepdims=True) / count
+    d_amplitude = (cotangent - normal * along) / width
     d_pooled = jnp.sum(d_amplitude * modes[...], axis=0, keepdims=True)
     return total, pooled, d_amplitude, d_pooled
 
 
-def backward_kernel(sums, modes, cot, s1, s2, x, w_second, out, g1, weight, rows, high, low):
+def share_kernel(parts, out):
+    total = jnp.sum(parts[...], axis=0)
+    bit, size = out.shape[1] - 2, total.shape[0] - 2
+    for z in range(out.shape[0]):
+        out[z] = jnp.zeros_like(out[z])
+        out[z, :2] = total[size:]
+        count = min(bit, size - z * bit)
+        if count > 0:
+            out[z, 2 : 2 + count] = total[z * bit : z * bit + count]
+
+
+def ring_kernel(parts, sums, out):
+    part = jnp.sum(parts[...], axis=0)
+    bit = jnp.sum(sums[...], axis=0)[2:]
+    for z in range(out.shape[0]):
+        out[z, : part.shape[0]] = part
+        out[z, part.shape[0] :] = bit
+
+
+def plane_kernel(size, both, out, rows):
+    first = out.shape[1] - size
+    part = jnp.sum(both[...], axis=0)[:first]
+    bit = both.shape[1] - first
+    for z in range(-(-size // bit)):
+        count = min(bit, size - z * bit)
+        rows[z * bit : z * bit + count, :] = both[z, first : first + count]
+    second = rows[...]
+    for p in range(out.shape[0]):
+        out[p, :size] = second
+        out[p, size:] = part
+
+
+def backward_kernel(sums, modes, consts, s1, s2, x, w_second, out, g1, weight, rows, high, low, high1, low1):
     spread(s2, high, low, 0, N2)
-    d_pooled = mode_gradients(sums, modes, cot)[3]
+    d_pooled = mode_gradients(sums, modes, consts)[3]
     column = jnp.broadcast_to(d_pooled, (LANES, LANES)).T
     for t in range(9):
         store_weight(weight, t, w_second[8 - t] * column)
-    for first, count in chunks(ROWS + 2, 2):
+    for first, count in chunks(ROWS + 2, 6):
         r, n = first * PITCH, count * PITCH
         g1[r : r + n, :] = convolve(high, low, weight, r, n) * s1[r : r + n, :]
     g1[N3:, :] = jnp.zeros((8, LANES), F32)
@@ -192,18 +242,16 @@
     for row in own[1:]:
         bias1 = bias1 + row
     grad = jnp.concatenate(own + [jnp.zeros((PITCH, LANES), F32)], axis=0)
-    spread(x, high, low, 0, 18 * PITCH)
-    for a, block in enumerate(correlate(grad, high, low, 0)):
-        for b in range(3):
-            t = 3 * a + b
-            rows[t * CIN : (t + 1) * CIN, :] = block[:, b * LANES : (b + 1) * LANES].T[:CIN]
+    spread_packed(x, high1, low1, 0, 18 * PITCH)
+    for a, block in enumerate(correlate(grad, high1, low1, 0)):
+        rows[3 * a * CIN : 3 * (a + 1) * CIN, :] = block.T[: 3 * CIN]
     rows[9 * CIN : 9 * CIN + 1, :] = jnp.sum(bias1, axis=0, keepdims=True)
     rows[9 * CIN + 1 :, :] = jnp.zeros((rows.shape[0] - 9 * CIN - 1, LANES), F32)
     write_pieces(out, rows)
 
 
-def field_kernel(scale, g1, w_first, sums, modes, cot, out, d_modes, spread_d, bias2, weight, pad, high, low):
-    total, pooled, d_amplitude, d_pooled = mode_gradients(sums, modes, cot)
+def field_kernel(scale, g1, w_first, sums, modes, consts, out, d_modes, spread_d, bias2, weight, pad, high, low):
+    total, pooled, d_amplitude, d_pooled = mode_gradients(sums, modes, consts)
     d_modes[...] = d_amplitude * pooled
     spread_d[...] = jnp.broadcast_to(d_pooled, (LANES, LANES)).T
     bias2[...] = total[1:2] * d_pooled
@@ -242,11 +290,10 @@
     outs = [o if isinstance(o[0], tuple) else (o, F32) for o in outs]
 
     def run(*args):
-        ins = [pl.BlockSpec(memory_space=pltpu.SMEM if i in smem else pltpu.VMEM) for i in range(len(args))]
         return pl.pallas_call(
             kernel,
             out_shape=[jax.ShapeDtypeStruct(s, d) for s, d in outs],
-            in_specs=ins,
+            in_specs=[pl.BlockSpec(memory_space=pltpu.SMEM if i in smem else pltpu.VMEM) for i in range(len(args))],
             out_specs=[pl.BlockSpec(memory_space=pltpu.VMEM) for _ in outs],
             scratch_shapes=[pltpu.VMEM(s, d) for s, d in scratch],
             compiler_params=pltpu.CompilerParams(vmem_limit_bytes=12 << 20),
@@ -268,22 +315,13 @@
 
 def row_weights(first, count, nlat, nlon):
     phi = (np.arange(nlat) + 0.5) * (math.pi / nlat) - math.pi / 2
-    area = np.cos(phi) / (np.cos(phi).sum() * nlon)
     table = np.zeros(nlat + 2 * count, np.float32)
-    table[count : count + nlat] = area
+    table[count : count + nlat] = np.cos(phi) / (np.cos(phi).sum() * nlon)
     return lax.dynamic_slice(jnp.asarray(table), (first + count,), (count,))
 
 
 def swap(pieces, axes):
     return lax.all_to_all(pieces, axes, 0, 0, tiled=True)
-
-
-def to_all(piece, axes):
-    return swap(jnp.broadcast_to(piece[None], (lax.axis_size(axes),) + piece.shape), axes)
-
-
-def fill(rows, count):
-    return jnp.pad(rows, ((0, count - rows.shape[0]), (0, 0)))
 
 
 def body(field, w_first, b_first, w_second, b_second, modes, cotangent):
@@ -292,7 +330,8 @@
     n_lat, n_lon = lax.axis_size(LAT), lax.axis_size(LON)
     n_pl, n_z = lax.axis_size(PLANE), lax.axis_size(RING)
     nlat, nlon = rows * n_lat, cols * n_lon
-    weights = row_weights(lax.axis_index(LAT) * rows - 3, 24, nlat, nlon)
+    weights = row_weights(lax.axis_index(LAT) * rows - 3, rows + 6, nlat, nlon)
+    consts = jnp.concatenate([b_first, b_second, cotangent, weights, jnp.zeros(LANES - rows - 6, F32)]).reshape(-1, LANES)
 
     own = field.transpose(1, 2, 0)
     north, south = edges(own, LAT, 0, 4, False)
@@ -301,49 +340,47 @@
     west, east = edges(jnp.concatenate([left, right], axis=1), LON, 1, 4, True)
     w_first = w_first.transpose(0, 2, 1)
     weight = ((3, 3 * LANES, 2 * LANES), BF16)
+    packed = ((3, 2 * LANES, 2 * LANES), BF16)
     pad = ((LANES, LANES), F32)
-    pair = lambda n: [((n, 3 * LANES), BF16), ((n, 3 * LANES), BF16)]
-    centre, w1, w2 = call(prepare_kernel, [(NX + 8, LANES), weight, weight], [pad], 10**9)(own, north, south, w_first, w_second)
+    pair = lambda n, width=3 * LANES: [((n, width), BF16), ((n, width), BF16)]
+    centre, w1, w2 = call(prepare_kernel, [(NX + 8, LANES), packed, weight], [((2 * LANES, LANES), F32)], 10**9)(
+        own, north, south, w_first, w_second
+    )
     x, a1, s1, s2, small = call(
         forward_kernel,
         [(18 * PITCH + 8, LANES), (N1 + 8, LANES), (N3, LANES), (N2 + 8, LANES), (2, LANES)],
-        [((NX + 8, LANES), F32), ((N1, LANES), F32)] + pair(NX),
+        [((NX + 8, LANES), F32), ((N1, LANES), F32)] + pair(N1) + pair(NX, 2 * LANES),
         10**9,
-        (0,),
-    )(weights, centre, west, east, w1, b_first[None], w2, b_second[None])
+    )(consts, centre, west, east, w1, w2)
 
     share2 = 9 * ch // n_pl
     (part,) = call(second_kernel, [(n_pl, share2 + 2, ch)], pair(20 * PITCH) + [((9 * ch, LANES), F32)], 10**9)(a1, s2, small)
 
-    part = jnp.sum(swap(part, PLANE), axis=0)
     bit2 = -(-share2 // n_z)
-    mine = fill(part[:share2], bit2 * n_z).reshape(n_z, bit2, ch)
-    mine = jnp.concatenate([jnp.broadcast_to(part[None, share2:], (n_z, 2, ch)), mine], axis=1)
+    (mine,) = call(share_kernel, [(n_z, bit2 + 2, ch)], [], 10**6)(swap(part, PLANE))
     mine = swap(mine, RING)
-    piece2 = jnp.sum(mine[:, 2:], axis=0)
 
     share1 = -(-(9 * cin + 1) // n_pl)
-    cot = cotangent.reshape(-1, LANES)
     g1rows, g1 = call(
         backward_kernel,
         [(n_pl, share1, ch), (N3 + 8, LANES)],
-        [weight, ((n_pl * share1, LANES), F32)] + pair(N2),
+        [weight, ((n_pl * share1, LANES), F32)] + pair(N2) + pair(18 * PITCH, 2 * LANES),
         10**9,
-    )(mine, modes, cot, s1, s2, x, w_second)
-
-    part = jnp.sum(swap(g1rows, PLANE), axis=0)
+    )(mine, modes, consts, s1, s2, x, w_second)
+
+    part = swap(g1rows, PLANE)
     grad_field, d_modes, spread_d, bias2 = call(
         lambda *r: field_kernel(float(nlat * nlon), *r),
         [(rows, cols, cin), modes.shape, (LANES, LANES), (1, LANES)],
         [weight, pad] + pair(N3),
         10**9,
-    )(g1, w_first, mine, modes, cot)
+    )(g1, w_first, mine, modes, consts)
     part, grad_field = lax.optimization_barrier((part, grad_field))
-
-    both = to_all(jnp.concatenate([part, piece2]), RING)
-    part = jnp.sum(both[:, :share1], axis=0)
-    piece2 = both[:, share1:].reshape(n_z * bit2, ch)[:share2]
-    whole = to_all(jnp.concatenate([piece2, part]), CHIPS)
+    (both,) = call(ring_kernel, [(n_z, share1 + bit2, ch)], [], 10**6)(part, mine)
+    (whole,) = call(
+        lambda *r: plane_kernel(share2, *r), [(n_pl // 2, share2 + share1, ch)], [((share2, LANES), F32)], 10**6
+    )(swap(both, RING))
+    whole = swap(whole, CHIPS)
     other = lax.ppermute(whole, "c", [(0, 1), (1, 0)])
     core = lax.axis_index("c").astype(jnp.int32).reshape(1)
     grad_w_second, grad_w_first, grad_b_first = call(

time: 139 us -> 133 us (0.957)
  local copies, waits for them, and re-layouts: 6.17 us -> 3.67 us
  Pallas kernels: 14.9 us -> 12.8 us
    unnamed x20 -> x10, local copies, waits for them, and re-layouts: 4.26 us -> 1.08 us
    pallas_call x6 -> x9, Pallas kernels: 14.9 us -> 12.8 us  [run(): pl.pallas_call(kernel, out_shape=[jax.ShapeDtypeStruct(s, d) for s, d in...]
  transfers between devices with their start and end apart: 6 -> 6, of which waited for: 3 -> 2; matrix products, arithmetic and copies ran while one was open for 1% -> 1% of each run, Pallas kernels for 2% -> 2%
where the time goes in v4:
time: 133 us
  blocking collectives  71.7 us (54%)
  starting transfers between devices  34.5 us (26%)
  Pallas kernels  12.8 us (10%)
  waiting for transfers between devices  9.17 us (7%)
  local copies, waits for them, and re-layouts  3.67 us (3%)
    all_to_all x4, blocking collectives, swap(): return lax.all_to_all(pieces, axes, 0, 0, tiled=True)  71.7 us
    ppermute x2, starting transfers between devices, edges(): lax.ppermute(head, axes, [((i + 1) % count, i) for i in range(ends)])  18.1 us
    pallas_call x9, Pallas kernels, run(): pl.pallas_call(kernel, out_shape=[jax.ShapeDtypeStruct(s, d) for s, d in...  12.8 us
    all_to_all x1, waiting for transfers between devices, swap(): return lax.all_to_all(pieces, axes, 0, 0, tiled=True)  7.7 us
    ppermute x1, starting transfers between devices, body(): other = lax.ppermute(whole, 'c', [(0, 1), (1, 0)])  7.13 us
    all_to_all x1, starting transfers between devices, swap(): return lax.all_to_all(pieces, axes, 0, 0, tiled=True)  5.48 us
    ppermute x2, starting transfers between devices, edges(): lax.ppermute(tail, axes, [(i, (i + 1) % count) for i in range(ends)])  3.84 us
  transfers between devices with their start and end apart: 6, of which 2 were waited for; matrix products, arithmetic and copies ran while one was open for 1% of the time, Pallas kernels for 2%

profile of v4, /device:TPU:1, one launch (start us, length us, event | category | flops | bytes accessed | tf_op | source)
XLA Modules:
  0.0 132.7 jit_solution(4151173075782558410)
XLA Ops:
  0.6 0.0 copy-start
  0.6 0.0 copy-start.3
  0.7 1.0 fusion.1
  1.7 8.8 %collective-permute-start.1 = (f32[4,45,69]{2,1,0:T(8,128)S(1)}, f32[4,45,69]{2,1,0:T(8,128)S(1)}, u32[]{:S(2)}, u32[]{:S(2)}) collective-permute-start(f32[4,45,69]{2,1,0:T(8,128)S(1)} %get-tuple-element.46), channel_id=1, source_target_pairs={{32,0},{64,32},{96,64},{128,96},{160,128},{192,160},{224,192},{256... | collective-permute-start | bytes 149048 | tf_op jit(solution)/shard_map/ppermute | solution.py:312
  10.5 1.9 %collective-permute-start = (f32[4,45,69]{2,1,0:T(8,128)S(1)}, f32[4,45,69]{2,1,0:T(8,128)S(1)}, u32[]{:S(2)}, u32[]{:S(2)}) collective-permute-start(f32[4,45,69]{2,1,0:T(8,128)S(1)} %get-tuple-element.47), channel_id=1, source_target_pairs={{0,32},{32,64},{64,96},{96,128},{128,160},{160,192},{192,224},{224... | collective-permute-start | bytes 149048 | tf_op jit(solution)/shard_map/ppermute | solution.py:311
  12.4 0.0 copy-done
  12.4 0.8 dynamic_slice.3
  13.2 0.8 concatenate.9
  14.0 0.0 collective-permute-done.1.south
  14.0 0.0 collective-permute-done.north
  14.1 1.9 %collective-permute-start.2 = (f32[23,4,69]{2,1,0:T(4,128)S(1)}, f32[23,4,69]{2,1,0:T(4,128)S(1)}, u32[]{:S(2)}, u32[]{:S(2)}) collective-permute-start(f32[23,4,69]{2,1,0:T(4,128)S(1)} %pad_maximum_fusion), channel_id=1, source_target_pairs={{0,1},{1,2},{2,3},{3,4},{4,5},{5,6},{6,7},{7,8},{8,9},{9,10},{10,1... | collective-permute-start | bytes 76184 | tf_op jit(solution)/shard_map/ppermute | solution.py:311
  16.0 9.3 %collective-permute-start.3 = (f32[23,4,69]{2,1,0:T(4,128)S(1)}, f32[23,4,69]{2,1,0:T(4,128)S(1)}, u32[]{:S(2)}, u32[]{:S(2)}) collective-permute-start(f32[23,4,69]{2,1,0:T(4,128)S(1)} %pad_maximum_fusion.1), channel_id=1, source_target_pairs={{1,0},{2,1},{3,2},{4,3},{5,4},{6,5},{7,6},{8,7},{9,8},{10,9},{11,1... | collective-permute-start | bytes 76184 | tf_op jit(solution)/shard_map/ppermute | solution.py:312
  25.3 0.0 copy-done.3
  25.3 0.0 copy-start.1
  25.3 1.1 copy-done.1
  26.4 0.4 shard_map.127
  26.7 0.0 collective-permute-done.2.west
  26.7 0.0 collective-permute-done.3.east
  26.8 3.3 %shard_map.128 = (f32[1160,128]{1,0:T(8,128)S(1)}, f32[1352,128]{1,0:T(8,128)S(1)}, f32[1088,128]{1,0:T(8,128)S(1)}, f32[1224,128]{1,0:T(8,128)S(1)}, f32[2,128]{1,0:T(2,128)S(1)}) custom-call(f32[7,128]{1,0:T(8,128)S(1)} %bitcast.11, f32[1480,128]{1,0:T(8,128)S(1)} %get-tuple-element.25.centre, f32[23,4,69]{2,1,0:T(4,128)S(1)} %collective-permute-done.2.west, ...), custom_call_target="tpu_custom_call" | custom-call | flops 1000000000 | bytes 4194304 | tf_op jit(solution)/shard_map/pallas_call | solution.py:293
  30.0 1.6 %shard_map.129 = f32[32,38,128]{2,1,0:T(8,128)S(1)} custom-call(f32[1352,128]{1,0:T(8,128)S(1)} %get-tuple-element.28.a1, f32[1224,128]{1,0:T(8,128)S(1)} %get-tuple-element.29.s2, f32[2,128]{1,0:T(2,128)S(1)} %get-tuple-element.30.small), custom_call_target="tpu_custom_call" | custom-call | flops 1000000000 | bytes 4194304 | tf_op jit(solution)/shard_map/pallas_call | solution.py:293
  31.6 20.6 %all_to_all.25.parts = f32[32,38,128]{2,1,0:T(8,128)S(1)} all-to-all(f32[32,38,128]{2,1,0:T(8,128)S(1)} %shard_map.129), channel_id=1, replica_groups=mesh['y'=4,'xl'=2,'c'=2,'z'=16,'xh'=2] {'y','xl','xh','c'}, dimensions={0} | all-to-all | bytes 1245184 | tf_op jit(solution)/shard_map/all_to_all | solution.py:324
  52.3 0.0 copy-start.2
  52.3 0.0 copy-start.4
  52.3 0.1 shard_map.130
  52.3 23.7 %all_to_all.26.sums.r_2_ = f32[16,5,128]{2,1,0:T(8,128)S(1)} all-to-all(f32[16,5,128]{2,1,0:T(8,128)S(1)} %shard_map.130), channel_id=1, replica_groups=mesh['y'=4,'xl'=2,'c'=2,'z'=16,'xh'=2] {'z'}, dimensions={0} | all-to-all | bytes 81920 | tf_op jit(solution)/shard_map/all_to_all | solution.py:324
  76.0 0.0 copy-done.2
  76.0 0.0 copy-done.4
  76.0 4.0 %shard_map.131 = (f32[32,20,128]{2,1,0:T(8,128)}, f32[1096,128]{1,0:T(8,128)S(1)}) custom-call(f32[16,5,128]{2,1,0:T(8,128)S(1)} %all_to_all.26.sums.r_2_, f32[512,128]{1,0:T(8,128)S(1)} %copy-done.4, f32[7,128]{1,0:T(8,128)S(1)} %bitcast.12, f32[1088,128]{1,0:T(8,128)S(1)} %get-tuple-element.31.s1, f32[1224,128]{1,0:T(8,128)S(1)} %get-tuple-element.29.s2, ...), custom_call_target="tpu_custom_call" | custom-call | flops 1000000000 | bytes 4194304 | tf_op jit(solution)/shard_map/pallas_call | solution.py:293
  80.0 5.5 %all-to-all-start.2 = ((f32[32,20,128]{2,1,0:T(8,128)}), f32[32,20,128]{2,1,0:T(8,128)S(1)}, u32[]{:S(2)}, u32[]{:S(2)}) async-start(f32[32,20,128]{2,1,0:T(8,128)} %get-tuple-element.33), calls=%async_computation.2 | async-start | bytes 786432 | tf_op jit(solution)/shard_map/all_to_all | solution.py:324
  85.5 2.3 %shard_map.132 = (f32[15,45,69]{2,1,0:T(8,128)}, f32[512,128]{1,0:T(8,128)}, f32[128,128]{1,0:T(8,128)S(1)}, f32[1,128]{1,0:T(1,128)}) custom-call(f32[1096,128]{1,0:T(8,128)S(1)} %get-tuple-element.34.r_0_, f32[9,69,128]{2,1,0:T(8,128)S(1)} %bitcast.15, f32[16,5,128]{2,1,0:T(8,128)S(1)} %all_to_all.26.sums.r_2_, f32[512,128]{1,0:T(8,128)S(1)} %copy-done.4, ...), custom_call_target="tpu_custom_call" | custom-call | flops 1000000000 | bytes 4194304 | tf_op jit(solution)/shard_map/pallas_call | solution.py:293
  87.9 7.7 %all-to-all-done.2.parts = f32[32,20,128]{2,1,0:T(8,128)S(1)} async-done(((f32[32,20,128]{2,1,0:T(8,128)}), f32[32,20,128]{2,1,0:T(8,128)S(1)}, u32[]{:S(2)}, u32[]{:S(2)}) %all-to-all-start.2) | async-done | bytes 327712 | tf_op jit(solution)/shard_map/all_to_all | solution.py:324
  95.6 0.1 shard_map.133
  95.6 15.8 %all_to_all.27.r_0_ = f32[16,23,128]{2,1,0:T(8,128)S(1)} all-to-all(f32[16,23,128]{2,1,0:T(8,128)S(1)} %shard_map.133), channel_id=1, replica_groups=mesh['y'=4,'xl'=2,'c'=2,'z'=16,'xh'=2] {'z'}, dimensions={0} | all-to-all | bytes 376832 | tf_op jit(solution)/shard_map/all_to_all | solution.py:324
  111.4 11.6 %all_to_all.28.mine = f32[16,56,128]{2,1,0:T(8,128)S(1)} all-to-all(f32[16,56,128]{2,1,0:T(8,128)S(1)} %shard_map.134), channel_id=1, replica_groups=mesh['y'=4,'xl'=2,'c'=2,'z'=16,'xh'=2] {'y','xl','xh'}, dimensions={0} | all-to-all | bytes 917504 | tf_op jit(solution)/shard_map/all_to_all | solution.py:324
  123.1 7.1 %collective-permute-start.4 = (f32[16,56,128]{2,1,0:T(8,128)S(1)}, f32[16,56,128]{2,1,0:T(8,128)S(1)}, u32[]{:S(2)}, u32[]{:S(2)}) collective-permute-start(f32[16,56,128]{2,1,0:T(8,128)S(1)} %all_to_all.28.mine), channel_id=1, source_target_pairs={{0,32},{32,0},{1,33},{33,1},{2,34},{34,2},{3,35},{35,3},{4,36},{36... | collective-permute-start | bytes 1376264 | tf_op jit(solution)/shard_map/ppermute | solution.py:384
  130.2 1.4 %collective-permute-done.4.other = f32[16,56,128]{2,1,0:T(8,128)S(1)} collective-permute-done((f32[16,56,128]{2,1,0:T(8,128)S(1)}, f32[16,56,128]{2,1,0:T(8,128)S(1)}, u32[]{:S(2)}, u32[]{:S(2)}) %collective-permute-start.4) | collective-permute-done | bytes 458784 | tf_op jit(solution)/shard_map/ppermute | solution.py:384
  131.6 1.0 shard_map.135
  (7 shorter events, 0.1 us)
Async XLA Ops:
  0.6 11.8 %copy-start = (f32[69,15,45]{0,2,1:T(8,128)S(1)}, f32[69,15,45]{0,2,1:T(8,128)}, u32[]{:S(2)}) copy-start(f32[69,15,45]{0,2,1:T(8,128)} %param.8) | copy-start | bytes 558904
  0.6 24.6 %copy-start.3 = (f32[9,128,69]{1,2,0:T(8,128)S(1)}, f32[9,128,69]{1,2,0:T(8,128)}, u32[]{:S(2)}) copy-start(f32[9,128,69]{1,2,0:T(8,128)} %param.9) | copy-start | bytes 953860
  1.7 12.3 %collective-permute-start.1 = (f32[4,45,69]{2,1,0:T(8,128)S(1)}, f32[4,45,69]{2,1,0:T(8,128)S(1)}, u32[]{:S(2)}, u32[]{:S(2)}) collective-permute-start(f32[4,45,69]{2,1,0:T(8,128)S(1)} %get-tuple-element.46), channel_id=1, source_target_pairs={{32,0},{64,32},{96,64},{128,96},{160,128},{192,160},{224,192},{256... | collective-permute-start | bytes 149048 | tf_op jit(solution)/shard_map/ppermute | solution.py:312
  10.5 3.5 %collective-permute-start = (f32[4,45,69]{2,1,0:T(8,128)S(1)}, f32[4,45,69]{2,1,0:T(8,128)S(1)}, u32[]{:S(2)}, u32[]{:S(2)}) collective-permute-start(f32[4,45,69]{2,1,0:T(8,128)S(1)} %get-tuple-element.47), channel_id=1, source_target_pairs={{0,32},{32,64},{64,96},{96,128},{128,160},{160,192},{192,224},{224... | collective-permute-start | bytes 149048 | tf_op jit(solution)/shard_map/ppermute | solution.py:311
  14.1 12.7 %collective-permute-start.2 = (f32[23,4,69]{2,1,0:T(4,128)S(1)}, f32[23,4,69]{2,1,0:T(4,128)S(1)}, u32[]{:S(2)}, u32[]{:S(2)}) collective-permute-start(f32[23,4,69]{2,1,0:T(4,128)S(1)} %pad_maximum_fusion), channel_id=1, source_target_pairs={{0,1},{1,2},{2,3},{3,4},{4,5},{5,6},{6,7},{7,8},{8,9},{9,10},{10,1... | collective-permute-start | bytes 76184 | tf_op jit(solution)/shard_map/ppermute | solution.py:311
  16.0 10.8 %collective-permute-start.3 = (f32[23,4,69]{2,1,0:T(4,128)S(1)}, f32[23,4,69]{2,1,0:T(4,128)S(1)}, u32[]{:S(2)}, u32[]{:S(2)}) collective-permute-start(f32[23,4,69]{2,1,0:T(4,128)S(1)} %pad_maximum_fusion.1), channel_id=1, source_target_pairs={{1,0},{2,1},{3,2},{4,3},{5,4},{6,5},{7,6},{8,7},{9,8},{10,9},{11,1... | collective-permute-start | bytes 76184 | tf_op jit(solution)/shard_map/ppermute | solution.py:312
  25.3 1.1 copy-start.1
  52.3 23.7 %copy-start.2 = (f32[9,128,128]{2,1,0:T(8,128)S(1)}, f32[9,128,128]{2,1,0:T(8,128)}, u32[]{:S(2)}) copy-start(f32[9,128,128]{2,1,0:T(8,128)} %w_second.3) | copy-start | bytes 1769476
  52.3 23.7 %copy-start.4 = (f32[512,128]{1,0:T(8,128)S(1)}, f32[512,128]{1,0:T(8,128)}, u32[]{:S(2)}) copy-start(f32[512,128]{1,0:T(8,128)} %r_3_.1) | copy-start | bytes 786436
  80.0 15.5 %all-to-all-start.2 = ((f32[32,20,128]{2,1,0:T(8,128)}), f32[32,20,128]{2,1,0:T(8,128)S(1)}, u32[]{:S(2)}, u32[]{:S(2)}) async-start(f32[32,20,128]{2,1,0:T(8,128)} %get-tuple-element.33), calls=%async_computation.2 | async-start | bytes 786432 | tf_op jit(solution)/shard_map/all_to_all | solution.py:324
  123.1 8.6 %collective-permute-start.4 = (f32[16,56,128]{2,1,0:T(8,128)S(1)}, f32[16,56,128]{2,1,0:T(8,128)S(1)}, u32[]{:S(2)}, u32[]{:S(2)}) collective-permute-start(f32[16,56,128]{2,1,0:T(8,128)S(1)} %all_to_all.28.mine), channel_id=1, source_target_pairs={{0,32},{32,0},{1,33},{33,1},{2,34},{34,2},{3,35},{35,3},{4,36},{36... | collective-permute-start | bytes 1376264 | tf_op jit(solution)/shard_map/ppermute | solution.py:384

commit v5 on v4

--- a/solution.py
+++ b/solution.py
@@ -62,16 +62,35 @@
     return both[:, :LANES] + both[:, LANES:] + dot(taps(low), w[:, :LANES])
 
 
-def correlate(grad, high, low, start):
+def correlate(grad, high, low, start, spans):
     hi, lo = split(grad.T)
     both = jnp.concatenate([hi, lo], axis=0)
     blocks = []
-    for a in range(3):
-        r = start + a * PITCH
-        x = high[r : r + WINDOW, :]
-        out = dot(both, x)
-        blocks.append(out[:LANES] + out[LANES:] + dot(hi, low[r : r + WINDOW, :]))
+    for a, first, last in spans:
+        r = slice(start + a * PITCH, start + a * PITCH + WINDOW)
+        out = dot(both, high[r, first:last])
+        blocks.append(out[:LANES] + out[LANES:] + dot(hi, low[r, first:last]))
     return blocks
+
+
+HALVES = (((0, 0, 3 * LANES), (1, 0, 2 * LANES)), ((1, LANES, 3 * LANES), (2, 0, 3 * LANES)))
+HALF = 9 * LANES // 2
+
+
+def correlate_half(core, s2, high, low, start, out):
+    mask = column_mask(6, (PITCH, LANES))
+    own = [s2[(i + 2) * PITCH : (i + 3) * PITCH, :] * mask for i in range(ROWS)]
+    grad = jnp.concatenate(own + [jnp.zeros((PITCH, LANES), F32)], axis=0)
+    for half in range(2):
+
+        @pl.when(core == half)
+        def _():
+            r = -half * (LANES // 2)
+            for block in correlate(grad, high, low, start, HALVES[half]):
+                for k in range(0, block.shape[1], LANES):
+                    first, last = max(r, 0), min(r + LANES, HALF)
+                    out[first:last, :] = block[first - r : last - r, k : k + LANES]
+                    r += LANES
 
 
 def chunks(rows, parts):
@@ -96,11 +115,17 @@
     weight[a, b * LANES : (b + 1) * LANES, LANES:] = lo
 
 
-def prepare_kernel(own, north, south, w_first, w_second, x, w1, w2, pad):
+def prepare_kernel(core, own, inner, outer, w_first, w_second, x, w1, w2, pad):
+    first = core[0] == 0
     x[...] = jnp.zeros_like(x)
     for i in range(ROWS + 8):
         r = i * PITCH
-        row = north[i] if i < 4 else own[i - 4] if i < ROWS + 4 else south[i - ROWS - 4]
+        if i < 4:
+            row = jnp.where(first, outer[i], inner[i])
+        elif i < ROWS + 4:
+            row = own[i - 4]
+        else:
+            row = jnp.where(first, inner[i - ROWS - 4], outer[i - ROWS - 4])
         x[r + 8 : r + 8 + COLS, :CIN] = row
     pad[...] = jnp.zeros_like(pad)
     for a in range(3):
@@ -113,14 +138,15 @@
         store_weight(w2, t, w_second[t].T)
 
 
-def forward_kernel(consts, centre, west, east, w1, w2, cells, a1, s1, s2, small, x, slopes, high, low, high1, low1):
+def forward_kernel(core, half, consts, centre, outer, inner, w1, w2, cells, a1, s1, s2, small, send, x, slopes, high, low, high1, low1):
+    first = half[0] == 0
     b1, b2 = consts[0:1, :], consts[1:2, :]
     weights = [consts[6:7, i : i + 1] for i in range(ROWS + 6)]
     x[...] = centre[...]
     for i in range(ROWS + 8):
         r = i * PITCH
-        x[r + 4 : r + 8, :CIN] = west[i]
-        x[r + 8 + COLS : r + 12 + COLS, :CIN] = east[i]
+        x[r + 4 : r + 8, :CIN] = jnp.where(first, outer[i], inner[i])
+        x[r + 8 + COLS : r + 12 + COLS, :CIN] = jnp.where(first, inner[i], outer[i])
     cells[...] = x[3 * PITCH : 21 * PITCH + 8, :]
     spread_packed(x, high1, low1, 0, NX)
     for first, rows in chunks(ROWS + 6, 2):
@@ -154,27 +180,29 @@
     s2[N2:, :] = jnp.zeros((8, LANES), F32)
     small[0:1, :] = jnp.sum(pooled * mask, axis=0, keepdims=True)
     small[1:2, :] = jnp.sum(bias * mask, axis=0, keepdims=True)
-
-
-def write_pieces(out, rows, extra=None):
-    count, size = out.shape[0], out.shape[1] - (0 if extra is None else extra.shape[0])
+    correlate_half(1 - core[0], s2, high, low, 2 * PITCH, send)
+    send[HALF : HALF + 2, :] = small[...]
+
+
+def write_pieces(out, rows):
+    count, size = out.shape[0], out.shape[1]
     for p in range(count):
         q = (p % 2) * (count // 2) + p // 2
-        out[p, :size] = rows[q * size : (q + 1) * size, :]
-        if extra is not None:
-            out[p, size:] = extra[...]
-
-
-def second_kernel(a1, s2, small, out, high, low, rows):
-    spread(a1, high, low, 2 * PITCH, 20 * PITCH)
-    mask = column_mask(6, (PITCH, LANES))
-    own = [s2[(i + 2) * PITCH : (i + 3) * PITCH, :] * mask for i in range(ROWS)]
-    grad = jnp.concatenate(own + [jnp.zeros((PITCH, LANES), F32)], axis=0)
-    for a, block in enumerate(correlate(grad, high, low, 2 * PITCH)):
-        for b in range(3):
-            t = 3 * a + b
-            rows[t * LANES : (t + 1) * LANES, :] = block[:, b * LANES : (b + 1) * LANES]
-    write_pieces(out, rows, small)
+        out[p] = rows[q * size : (q + 1) * size, :]
+
+
+def second_kernel(core, a1, s2, out, high, low):
+    spread(a1.at[2 * PITCH :], high, low, 0, 18 * PITCH)
+    correlate_half(core[0], s2, high, low, 0, out)
+
+
+def pair_kernel(own, other, small, out):
+    size = out.shape[1] - 2
+    sums = small[...] + other[HALF : HALF + 2, :]
+    for p in range(out.shape[0]):
+        r = slice(p * size, (p + 1) * size)
+        out[p, :size] = own[r, :] + other[r, :]
+        out[p, size:] = sums
 
 
 def mode_gradients(sums, modes, consts):
@@ -243,7 +271,7 @@
         bias1 = bias1 + row
     grad = jnp.concatenate(own + [jnp.zeros((PITCH, LANES), F32)], axis=0)
     spread_packed(x, high1, low1, 0, 18 * PITCH)
-    for a, block in enumerate(correlate(grad, high1, low1, 0)):
+    for a, block in enumerate(correlate(grad, high1, low1, 0, [(a, 0, 2 * LANES) for a in range(3)])):
         rows[3 * a * CIN : 3 * (a + 1) * CIN, :] = block.T[: 3 * CIN]
     rows[9 * CIN : 9 * CIN + 1, :] = jnp.sum(bias1, axis=0, keepdims=True)
     rows[9 * CIN + 1 :, :] = jnp.zeros((rows.shape[0] - 9 * CIN - 1, LANES), F32)
@@ -267,7 +295,7 @@
 
 def finish_kernel(core, mine, other, spread_d, w_second, w_first, b_first, rows):
     chips = mine.shape[0]
-    size = 9 * LANES // (2 * chips)
+    size = HALF // chips
     rest = mine.shape[1] - size
     even = core[0] == 0
 
@@ -303,14 +331,14 @@
     return run
 
 
-def edges(cells, axes, dim, width, closed):
-    count = lax.axis_size(axes)
-    ends = count if closed else count - 1
-    head = lax.slice_in_dim(cells, 0, width, axis=dim)
-    tail = lax.slice_in_dim(cells, cells.shape[dim] - width, cells.shape[dim], axis=dim)
-    before = lax.ppermute(tail, axes, [(i, (i + 1) % count) for i in range(ends)])
-    after = lax.ppermute(head, axes, [((i + 1) % count, i) for i in range(ends)])
-    return before, after
+def far_pairs(count, closed):
+    pairs = [(i, (i + 1) % count) for i in range(1, count if closed else count - 1, 2)]
+    return pairs + [(j, i) for i, j in pairs]
+
+
+def near_pairs(count):
+    pairs = [(i, i + 1) for i in range(0, count, 2)]
+    return pairs + [(j, i) for i, j in pairs]
 
 
 def row_weights(first, count, nlat, nlon):
@@ -334,30 +362,39 @@
     consts = jnp.concatenate([b_first, b_second, cotangent, weights, jnp.zeros(LANES - rows - 6, F32)]).reshape(-1, LANES)
 
     own = field.transpose(1, 2, 0)
-    north, south = edges(own, LAT, 0, 4, False)
-    left = jnp.concatenate([north[:, :4], own[:, :4], south[:, :4]], axis=0)
-    right = jnp.concatenate([north[:, cols - 4 :], own[:, cols - 4 :], south[:, cols - 4 :]], axis=0)
-    west, east = edges(jnp.concatenate([left, right], axis=1), LON, 1, 4, True)
+    core, half = lax.axis_index("c"), lax.axis_index("xh")
+    inner = lax.ppermute(lax.dynamic_slice_in_dim(own, (1 - core) * (rows - 4), 4, 0), LAT, near_pairs(n_lat))
+    outer = lax.ppermute(lax.dynamic_slice_in_dim(own, core * (rows - 4), 4, 0), LAT, far_pairs(n_lat, False))
+    strips = []
+    for start in (half * (cols - 4), (1 - half) * (cols - 4)):
+        a, b, c = [lax.dynamic_slice_in_dim(v, start, 4, 1) for v in (outer, own, inner)]
+        strips.append(jnp.concatenate([jnp.where(core == 0, a, c), b, jnp.where(core == 0, c, a)], axis=0))
+    outer_strip = lax.ppermute(strips[0], LON, far_pairs(n_lon, True))
+    inner_strip = lax.ppermute(strips[1], LON, near_pairs(n_lon))
+    core, half = core.astype(jnp.int32).reshape(1), half.astype(jnp.int32).reshape(1)
     w_first = w_first.transpose(0, 2, 1)
     weight = ((3, 3 * LANES, 2 * LANES), BF16)
     packed = ((3, 2 * LANES, 2 * LANES), BF16)
     pad = ((LANES, LANES), F32)
     pair = lambda n, width=3 * LANES: [((n, width), BF16), ((n, width), BF16)]
-    centre, w1, w2 = call(prepare_kernel, [(NX + 8, LANES), packed, weight], [((2 * LANES, LANES), F32)], 10**9)(
-        own, north, south, w_first, w_second
+    centre, w1, w2 = call(prepare_kernel, [(NX + 8, LANES), packed, weight], [((2 * LANES, LANES), F32)], 10**9, smem=(0,))(
+        core, own, inner, outer, w_first, w_second
     )
-    x, a1, s1, s2, small = call(
+    swap_cores = lambda v: lax.ppermute(v, "c", [(0, 1), (1, 0)])
+    x, a1, s1, s2, small, send = call(
         forward_kernel,
-        [(18 * PITCH + 8, LANES), (N1 + 8, LANES), (N3, LANES), (N2 + 8, LANES), (2, LANES)],
+        [(18 * PITCH + 8, LANES), (N1 + 8, LANES), (N3, LANES), (N2 + 8, LANES), (2, LANES), (HALF + 8, LANES)],
         [((NX + 8, LANES), F32), ((N1, LANES), F32)] + pair(N1) + pair(NX, 2 * LANES),
         10**9,
-    )(consts, centre, west, east, w1, w2)
-
-    share2 = 9 * ch // n_pl
-    (part,) = call(second_kernel, [(n_pl, share2 + 2, ch)], pair(20 * PITCH) + [((9 * ch, LANES), F32)], 10**9)(a1, s2, small)
-
+        smem=(0, 1),
+    )(core, half, consts, centre, outer_strip, inner_strip, w1, w2)
+
+    other = swap_cores(send)
+    (half,) = call(second_kernel, [(HALF, LANES)], pair(18 * PITCH), 10**9, smem=(0,))(core, a1, s2)
+    share2 = HALF * 2 // n_pl
+    (part,) = call(pair_kernel, [(n_pl // 2, share2 + 2, ch)], [], 10**6)(half, other, small)
     bit2 = -(-share2 // n_z)
-    (mine,) = call(share_kernel, [(n_z, bit2 + 2, ch)], [], 10**6)(swap(part, PLANE))
+    (mine,) = call(share_kernel, [(n_z, bit2 + 2, ch)], [], 10**6)(swap(part, CHIPS))
     mine = swap(mine, RING)
 
     share1 = -(-(9 * cin + 1) // n_pl)
@@ -381,12 +418,11 @@
         lambda *r: plane_kernel(share2, *r), [(n_pl // 2, share2 + share1, ch)], [((share2, LANES), F32)], 10**6
     )(swap(both, RING))
     whole = swap(whole, CHIPS)
-    other = lax.ppermute(whole, "c", [(0, 1), (1, 0)])
-    core = lax.axis_index("c").astype(jnp.int32).reshape(1)
+    other = swap_cores(whole)
     grad_w_second, grad_w_first, grad_b_first = call(
         finish_kernel,
         [(9, ch, ch), (9, cin, ch), (1, ch)],
-        [((9 * ch, LANES), F32)],
+        [((2 * HALF, LANES), F32)],
         10**6,
         (0,),
     )(core, whole, other, spread_d)

time: 133 us -> 128 us (0.962)
  blocking collectives: 71.7 us -> 59.3 us
  starting transfers between devices: 34.5 us -> 39.1 us
  waiting for transfers between devices: 9.17 us -> 12 us
    all_to_all x4, blocking collectives: 71.7 us -> 59.3 us  [swap(): return lax.all_to_all(pieces, axes, 0, 0, tiled=True)]
    ppermute x5 -> x6, waiting for transfers between devices: 1.48 us -> 4.38 us  [the longest x1 2.92 us: body(): inner_strip = lax.ppermute(strips[1], LON, near_pairs(n_lon))]
    ppermute x5 -> x6, starting transfers between devices: 29 us -> 31.8 us  [the longest x1 10.6 us: body(): outer_strip = lax.ppermute(strips[0], LON, far_pairs(n_lon, True))]
    all_to_all x1, starting transfers between devices: 5.48 us -> 7.32 us  [swap(): return lax.all_to_all(pieces, axes, 0, 0, tiled=True)]
    pallas_call x9 -> x10, Pallas kernels: 12.8 us -> 13.2 us  [run(): pl.pallas_call(kernel, out_shape=[jax.ShapeDtypeStruct(s, d) for s, d in...]
  transfers between devices with their start and end apart: 6 -> 7, of which waited for: 2 -> 3; matrix products, arithmetic and copies ran while one was open for 1% -> 1% of each run, Pallas kernels for 2% -> 3%
where the time goes in v5:
time: 128 us
  blocking collectives  59.3 us (46%)
  starting transfers between devices  39.1 us (31%)
  Pallas kernels  13.2 us (10%)
  waiting for transfers between devices  12 us (9%)
  local copies, waits for them, and re-layouts  2.98 us (2%)
    all_to_all x4, blocking collectives, swap(): return lax.all_to_all(pieces, axes, 0, 0, tiled=True)  59.3 us
    pallas_call x10, Pallas kernels, run(): pl.pallas_call(kernel, out_shape=[jax.ShapeDtypeStruct(s, d) for s, d in...  13.2 us
    ppermute x1, starting transfers between devices, body(): outer_strip = lax.ppermute(strips[0], LON, far_pairs(n_lon, True))  10.6 us
    ppermute x2, starting transfers between devices, body(): swap_cores = lambda v: lax.ppermute(v, 'c', [(0, 1), (1, 0)])  9.83 us
    all_to_all x1, waiting for transfers between devices, swap(): return lax.all_to_all(pieces, axes, 0, 0, tiled=True)  7.65 us
    all_to_all x1, starting transfers between devices, swap(): return lax.all_to_all(pieces, axes, 0, 0, tiled=True)  7.32 us
    ppermute x1, starting transfers between devices, body(): lax.ppermute(lax.dynamic_slice_in_dim(own, (1 - core) * (rows - 4), 4, 0)...  4.94 us
    ppermute x1, starting transfers between devices, body(): lax.ppermute(lax.dynamic_slice_in_dim(own, core * (rows - 4), 4, 0), LAT,...  4.51 us
  transfers between devices with their start and end apart: 7, of which 3 were waited for; matrix products, arithmetic and copies ran while one was open for 1% of the time, Pallas kernels for 3%

profile of v5, /device:TPU:1, one launch (start us, length us, event | category | flops | bytes accessed | tf_op | source)
XLA Modules:
  0.0 127.6 jit_solution(10551385750157035141)
XLA Ops:
  0.6 0.0 copy-start
  0.7 0.0 copy-start.5
  0.7 0.0 copy-start.6
  0.7 0.0 copy-start.7
  0.7 0.0 copy-start.3
  0.7 1.0 dynamic-slice_bitcast_fusion
  1.7 4.5 %collective-permute-start.1 = (f32[4,45,69]{2,1,0:T(8,128)S(1)}, f32[4,45,69]{2,1,0:T(8,128)S(1)}, u32[]{:S(2)}, u32[]{:S(2)}) collective-permute-start(f32[4,45,69]{2,1,0:T(8,128)S(1)} %get-tuple-element.48), channel_id=1, source_target_pairs={{32,64},{96,128},{160,192},{224,256},{288,320},{352,384},{416,448}... | collective-permute-start | bytes 149048 | tf_op jit(solution)/shard_map/ppermute | solution.py:367
  6.2 4.9 %collective-permute-start = (f32[4,45,69]{2,1,0:T(8,128)S(1)}, f32[4,45,69]{2,1,0:T(8,128)S(1)}, u32[]{:S(2)}, u32[]{:S(2)}) collective-permute-start(f32[4,45,69]{2,1,0:T(8,128)S(1)} %get-tuple-element.49), channel_id=1, source_target_pairs={{0,32},{64,96},{128,160},{192,224},{256,288},{320,352},{384,416},{... | collective-permute-start | bytes 149048 | tf_op jit(solution)/shard_map/ppermute | solution.py:366
  11.2 0.0 copy-done
  11.2 0.8 dynamic_slice.27
  12.0 0.0 copy-done.5
  12.0 0.0 copy-done.6
  12.0 0.0 copy-done.7
  12.0 0.1 concatenate.9
  12.1 0.0 collective-permute-done.1.outer
  12.1 0.0 collective-permute-done.inner
  12.2 10.6 %collective-permute-start.2 = (f32[23,4,69]{2,1,0:T(4,128)S(1)}, f32[23,4,69]{2,1,0:T(4,128)S(1)}, u32[]{:S(2)}, u32[]{:S(2)}) collective-permute-start(f32[23,4,69]{2,1,0:T(4,128)S(1)} %pad_maximum_fusion), channel_id=1, source_target_pairs={{1,2},{3,4},{5,6},{7,8},{9,10},{11,12},{13,14},{15,16},{17,18},{19... | collective-permute-start | bytes 76184 | tf_op jit(solution)/shard_map/ppermute | solution.py:372
  22.8 1.9 %collective-permute-start.3 = (f32[23,4,69]{2,1,0:T(4,128)S(1)}, f32[23,4,69]{2,1,0:T(4,128)S(1)}, u32[]{:S(2)}, u32[]{:S(2)}) collective-permute-start(f32[23,4,69]{2,1,0:T(4,128)S(1)} %pad_maximum_fusion.1), channel_id=1, source_target_pairs={{0,1},{2,3},{4,5},{6,7},{8,9},{10,11},{12,13},{14,15},{16,17},{18,... | collective-permute-start | bytes 76184 | tf_op jit(solution)/shard_map/ppermute | solution.py:373
  24.7 0.0 copy-done.3
  24.7 0.0 copy-start.1
  24.7 1.1 copy-done.1
  25.8 0.4 shard_map.127
  26.2 0.0 collective-permute-done.2.outer
  26.2 2.9 %collective-permute-done.3.inner = f32[23,4,69]{2,1,0:T(4,128)S(1)} collective-permute-done((f32[23,4,69]{2,1,0:T(4,128)S(1)}, f32[23,4,69]{2,1,0:T(4,128)S(1)}, u32[]{:S(2)}, u32[]{:S(2)}) %collective-permute-start.3) | collective-permute-done | bytes 25424 | tf_op jit(solution)/shard_map/ppermute | solution.py:373
  29.1 4.1 %shard_map.128 = (f32[1160,128]{1,0:T(8,128)S(1)}, f32[1352,128]{1,0:T(8,128)S(1)}, f32[1088,128]{1,0:T(8,128)S(1)}, f32[1224,128]{1,0:T(8,128)S(1)}, f32[2,128]{1,0:T(2,128)S(1)}, /*index=5*/f32[584,128]{1,0:T(8,128)S(1)}) custom-call(s32[1]{0:T(128)} %bitcast.core, s32[1]{0:T(128)} %bitcast.1.half, f32[7,128]{1,0:T(8,128)S(1)} %bitcast.18, ...), custom_call_target="tpu_custom_call" | custom-call | flops 1000000000 | bytes 4194304 | tf_op jit(solution)/shard_map/pallas_call | solution.py:321
  33.2 3.5 %collective-permute-start.4 = (f32[584,128]{1,0:T(8,128)S(1)}, f32[584,128]{1,0:T(8,128)S(1)}, u32[]{:S(2)}, u32[]{:S(2)}) collective-permute-start(f32[584,128]{1,0:T(8,128)S(1)} %get-tuple-element.31), channel_id=1, source_target_pairs={{0,32},{32,0},{1,33},{33,1},{2,34},{34,2},{3,35},{35,3},{4,36},{36... | collective-permute-start | bytes 897032 | tf_op jit(solution)/shard_map/ppermute | solution.py:383
  36.7 1.1 shard_map.129.own
  37.9 0.0 collective-permute-done.4.other
  37.9 0.0 copy-start.2
  37.9 12.9 %all_to_all.25.parts = f32[16,38,128]{2,1,0:T(8,128)S(1)} all-to-all(f32[16,38,128]{2,1,0:T(8,128)S(1)} %shard_map.130), channel_id=1, replica_groups=mesh['y'=4,'xl'=2,'c'=2,'z'=16,'xh'=2] {'y','xl','xh'}, dimensions={0} | all-to-all | bytes 622592 | tf_op jit(solution)/shard_map/all_to_all | solution.py:352
  50.8 0.0 copy-start.4
  50.9 18.5 %all_to_all.26.sums.r_2_ = f32[16,5,128]{2,1,0:T(8,128)S(1)} all-to-all(f32[16,5,128]{2,1,0:T(8,128)S(1)} %shard_map.131), channel_id=1, replica_groups=mesh['y'=4,'xl'=2,'c'=2,'z'=16,'xh'=2] {'z'}, dimensions={0} | all-to-all | bytes 81920 | tf_op jit(solution)/shard_map/all_to_all | solution.py:352
  69.4 0.0 copy-done.2
  69.4 0.0 copy-done.4
  69.4 4.1 %shard_map.132 = (f32[32,20,128]{2,1,0:T(8,128)}, f32[1096,128]{1,0:T(8,128)S(1)}) custom-call(f32[16,5,128]{2,1,0:T(8,128)S(1)} %all_to_all.26.sums.r_2_, f32[512,128]{1,0:T(8,128)S(1)} %copy-done.4, f32[7,128]{1,0:T(8,128)S(1)} %bitcast.19, f32[1088,128]{1,0:T(8,128)S(1)} %get-tuple-element.33.s1, f32[1224,128]{1,0:T(8,128)S(1)} %get-tuple-element.30.s2, ...), custom_call_target="tpu_custom_call" | custom-call | flops 1000000000 | bytes 4194304 | tf_op jit(solution)/shard_map/pallas_call | solution.py:321
  73.4 7.3 %all-to-all-start.2 = ((f32[32,20,128]{2,1,0:T(8,128)}), f32[32,20,128]{2,1,0:T(8,128)S(1)}, u32[]{:S(2)}, u32[]{:S(2)}) async-start(f32[32,20,128]{2,1,0:T(8,128)} %get-tuple-element.35), calls=%async_computation.2 | async-start | bytes 786432 | tf_op jit(solution)/shard_map/all_to_all | solution.py:352
  80.8 2.3 %shard_map.133 = (f32[15,45,69]{2,1,0:T(8,128)}, f32[512,128]{1,0:T(8,128)}, f32[128,128]{1,0:T(8,128)S(1)}, f32[1,128]{1,0:T(1,128)}) custom-call(f32[1096,128]{1,0:T(8,128)S(1)} %get-tuple-element.36.r_0_, f32[9,69,128]{2,1,0:T(8,128)S(1)} %bitcast.22, f32[16,5,128]{2,1,0:T(8,128)S(1)} %all_to_all.26.sums.r_2_, f32[512,128]{1,0:T(8,128)S(1)} %copy-done.4, ...), custom_call_target="tpu_custom_call" | custom-call | flops 1000000000 | bytes 4194304 | tf_op jit(solution)/shard_map/pallas_call | solution.py:321
  83.1 7.7 %all-to-all-done.2.parts = f32[32,20,128]{2,1,0:T(8,128)S(1)} async-done(((f32[32,20,128]{2,1,0:T(8,128)}), f32[32,20,128]{2,1,0:T(8,128)S(1)}, u32[]{:S(2)}, u32[]{:S(2)}) %all-to-all-start.2) | async-done | bytes 327712 | tf_op jit(solution)/shard_map/all_to_all | solution.py:352
  90.8 0.1 shard_map.134
  90.8 15.8 %all_to_all.27.r_0_ = f32[16,23,128]{2,1,0:T(8,128)S(1)} all-to-all(f32[16,23,128]{2,1,0:T(8,128)S(1)} %shard_map.134), channel_id=1, replica_groups=mesh['y'=4,'xl'=2,'c'=2,'z'=16,'xh'=2] {'z'}, dimensions={0} | all-to-all | bytes 376832 | tf_op jit(solution)/shard_map/all_to_all | solution.py:352
  106.6 12.1 %all_to_all.28.mine = f32[16,56,128]{2,1,0:T(8,128)S(1)} all-to-all(f32[16,56,128]{2,1,0:T(8,128)S(1)} %shard_map.135), channel_id=1, replica_groups=mesh['y'=4,'xl'=2,'c'=2,'z'=16,'xh'=2] {'y','xl','xh'}, dimensions={0} | all-to-all | bytes 917504 | tf_op jit(solution)/shard_map/all_to_all | solution.py:352
  118.8 6.3 %collective-permute-start.5 = (f32[16,56,128]{2,1,0:T(8,128)S(1)}, f32[16,56,128]{2,1,0:T(8,128)S(1)}, u32[]{:S(2)}, u32[]{:S(2)}) collective-permute-start(f32[16,56,128]{2,1,0:T(8,128)S(1)} %all_to_all.28.mine), channel_id=1, source_target_pairs={{0,32},{32,0},{1,33},{33,1},{2,34},{34,2},{3,35},{35,3},{4,36},{36... | collective-permute-start | bytes 1376264 | tf_op jit(solution)/shard_map/ppermute | solution.py:383
  125.1 1.4 %collective-permute-done.5.other = f32[16,56,128]{2,1,0:T(8,128)S(1)} collective-permute-done((f32[16,56,128]{2,1,0:T(8,128)S(1)}, f32[16,56,128]{2,1,0:T(8,128)S(1)}, u32[]{:S(2)}, u32[]{:S(2)}) %collective-permute-start.5) | collective-permute-done | bytes 458784 | tf_op jit(solution)/shard_map/ppermute | solution.py:383
  126.6 1.0 shard_map.136
  (8 shorter events, 0.2 us)
Async XLA Ops:
  0.6 10.6 %copy-start = (f32[69,15,45]{0,2,1:T(8,128)S(1)}, f32[69,15,45]{0,2,1:T(8,128)}, u32[]{:S(2)}) copy-start(f32[69,15,45]{0,2,1:T(8,128)} %param.8) | copy-start | bytes 558904
  0.7 11.4 %copy-start.5 = (f32[512]{0:T(512)S(1)}, f32[512]{0:T(512)}, u32[]{:S(2)}) copy-start(f32[512]{0:T(512)} %param.14) | copy-start | bytes 6148
  0.7 11.4 %copy-start.6 = (f32[128]{0:T(128)S(1)}, f32[128]{0:T(128)}, u32[]{:S(2)}) copy-start(f32[128]{0:T(128)} %param.10) | copy-start | bytes 1540
  0.7 11.3 %copy-start.7 = (f32[128]{0:T(128)S(1)}, f32[128]{0:T(128)}, u32[]{:S(2)}) copy-start(f32[128]{0:T(128)} %param.12) | copy-start | bytes 1540
  0.7 24.0 %copy-start.3 = (f32[9,128,69]{1,2,0:T(8,128)S(1)}, f32[9,128,69]{1,2,0:T(8,128)}, u32[]{:S(2)}) copy-start(f32[9,128,69]{1,2,0:T(8,128)} %param.9) | copy-start | bytes 953860
  1.7 10.4 %collective-permute-start.1 = (f32[4,45,69]{2,1,0:T(8,128)S(1)}, f32[4,45,69]{2,1,0:T(8,128)S(1)}, u32[]{:S(2)}, u32[]{:S(2)}) collective-permute-start(f32[4,45,69]{2,1,0:T(8,128)S(1)} %get-tuple-element.48), channel_id=1, source_target_pairs={{32,64},{96,128},{160,192},{224,256},{288,320},{352,384},{416,448}... | collective-permute-start | bytes 149048 | tf_op jit(solution)/shard_map/ppermute | solution.py:367
  6.2 5.9 %collective-permute-start = (f32[4,45,69]{2,1,0:T(8,128)S(1)}, f32[4,45,69]{2,1,0:T(8,128)S(1)}, u32[]{:S(2)}, u32[]{:S(2)}) collective-permute-start(f32[4,45,69]{2,1,0:T(8,128)S(1)} %get-tuple-element.49), channel_id=1, source_target_pairs={{0,32},{64,96},{128,160},{192,224},{256,288},{320,352},{384,416},{... | collective-permute-start | bytes 149048 | tf_op jit(solution)/shard_map/ppermute | solution.py:366
  12.2 14.0 %collective-permute-start.2 = (f32[23,4,69]{2,1,0:T(4,128)S(1)}, f32[23,4,69]{2,1,0:T(4,128)S(1)}, u32[]{:S(2)}, u32[]{:S(2)}) collective-permute-start(f32[23,4,69]{2,1,0:T(4,128)S(1)} %pad_maximum_fusion), channel_id=1, source_target_pairs={{1,2},{3,4},{5,6},{7,8},{9,10},{11,12},{13,14},{15,16},{17,18},{19... | collective-permute-start | bytes 76184 | tf_op jit(solution)/shard_map/ppermute | solution.py:372
  22.8 6.3 %collective-permute-start.3 = (f32[23,4,69]{2,1,0:T(4,128)S(1)}, f32[23,4,69]{2,1,0:T(4,128)S(1)}, u32[]{:S(2)}, u32[]{:S(2)}) collective-permute-start(f32[23,4,69]{2,1,0:T(4,128)S(1)} %pad_maximum_fusion.1), channel_id=1, source_target_pairs={{0,1},{2,3},{4,5},{6,7},{8,9},{10,11},{12,13},{14,15},{16,17},{18,... | collective-permute-start | bytes 76184 | tf_op jit(solution)/shard_map/ppermute | solution.py:373
  24.7 1.1 copy-start.1
  33.2 4.7 %collective-permute-start.4 = (f32[584,128]{1,0:T(8,128)S(1)}, f32[584,128]{1,0:T(8,128)S(1)}, u32[]{:S(2)}, u32[]{:S(2)}) collective-permute-start(f32[584,128]{1,0:T(8,128)S(1)} %get-tuple-element.31), channel_id=1, source_target_pairs={{0,32},{32,0},{1,33},{33,1},{2,34},{34,2},{3,35},{35,3},{4,36},{36... | collective-permute-start | bytes 897032 | tf_op jit(solution)/shard_map/ppermute | solution.py:383
  37.9 31.5 %copy-start.2 = (f32[9,128,128]{2,1,0:T(8,128)S(1)}, f32[9,128,128]{2,1,0:T(8,128)}, u32[]{:S(2)}) copy-start(f32[9,128,128]{2,1,0:T(8,128)} %w_second.3) | copy-start | bytes 1769476
  50.8 18.6 %copy-start.4 = (f32[512,128]{1,0:T(8,128)S(1)}, f32[512,128]{1,0:T(8,128)}, u32[]{:S(2)}) copy-start(f32[512,128]{1,0:T(8,128)} %r_3_.1) | copy-start | bytes 786436
  73.4 17.3 %all-to-all-start.2 = ((f32[32,20,128]{2,1,0:T(8,128)}), f32[32,20,128]{2,1,0:T(8,128)S(1)}, u32[]{:S(2)}, u32[]{:S(2)}) async-start(f32[32,20,128]{2,1,0:T(8,128)} %get-tuple-element.35), calls=%async_computation.2 | async-start | bytes 786432 | tf_op jit(solution)/shard_map/all_to_all | solution.py:352
  118.8 7.8 %collective-permute-start.5 = (f32[16,56,128]{2,1,0:T(8,128)S(1)}, f32[16,56,128]{2,1,0:T(8,128)S(1)}, u32[]{:S(2)}, u32[]{:S(2)}) collective-permute-start(f32[16,56,128]{2,1,0:T(8,128)S(1)} %all_to_all.28.mine), channel_id=1, source_target_pairs={{0,32},{32,0},{1,33},{33,1},{2,34},{34,2},{3,35},{35,3},{4,36},{36... | collective-permute-start | bytes 1376264 | tf_op jit(solution)/shard_map/ppermute | solution.py:383

commit v6 on v5

--- a/solution.py
+++ b/solution.py
@@ -19,8 +19,10 @@
 PITCH = 64
 LANES = 128
 ROWS, COLS, CIN = 15, 45, 69
-WINDOW = 16 * PITCH
-NX, N1, N2, N3 = 23 * PITCH, 21 * PITCH, 19 * PITCH, 17 * PITCH
+SHORT = 48
+NARROW = 16
+WINDOW = 16 * SHORT
+NX, N1, N2, N3 = 23 * PITCH, 21 * PITCH, 19 * PITCH, 17 * SHORT
 
 
 def split(x):
@@ -28,46 +30,48 @@
     return hi, (x - hi.astype(F32)).astype(BF16)
 
 
-def spread(src, high, low, start, stop):
-    for r in range(start, stop, PITCH):
+def spread(src, high, low, rows, first=0, col=0, width=PITCH, pitch=PITCH):
+    for i in range(rows):
         for b in range(3):
-            hi, lo = split(src[r + b : r + b + PITCH, :])
-            high[r : r + PITCH, b * LANES : (b + 1) * LANES] = hi
-            low[r : r + PITCH, b * LANES : (b + 1) * LANES] = lo
-
-
-def spread_packed(src, high, low, start, stop):
-    lane = lax.broadcasted_iota(jnp.int32, (PITCH, LANES), 1)
-    for r in range(start, stop, PITCH):
-        second = pltpu.roll(src[r + 1 : r + 1 + PITCH, :], CIN, 1)
-        third = pltpu.roll(src[r + 2 : r + 2 + PITCH, :], 2 * CIN - LANES, 1)
+            r = (first + i) * pitch + col + b
+            hi, lo = split(src[r : r + width, :])
+            high[i * width : (i + 1) * width, b * LANES : (b + 1) * LANES] = hi
+            low[i * width : (i + 1) * width, b * LANES : (b + 1) * LANES] = lo
+
+
+def spread_packed(src, high, low, rows, col=0, width=PITCH, pitch=PITCH):
+    lane = lax.broadcasted_iota(jnp.int32, (width, LANES), 1)
+    for i in range(rows):
+        r = i * pitch + col
+        second = pltpu.roll(src[r + 1 : r + 1 + width, :], CIN, 1)
+        third = pltpu.roll(src[r + 2 : r + 2 + width, :], 2 * CIN - LANES, 1)
         for k, x in enumerate(
-            (jnp.where(lane < CIN, src[r : r + PITCH, :], second), jnp.where(lane < 2 * CIN - LANES, second, third))
+            (jnp.where(lane < CIN, src[r : r + width, :], second), jnp.where(lane < 2 * CIN - LANES, second, third))
         ):
             hi, lo = split(x)
-            high[r : r + PITCH, k * LANES : (k + 1) * LANES] = hi
-            low[r : r + PITCH, k * LANES : (k + 1) * LANES] = lo
+            high[i * width : (i + 1) * width, k * LANES : (k + 1) * LANES] = hi
+            low[i * width : (i + 1) * width, k * LANES : (k + 1) * LANES] = lo
 
 
 def dot(a, b):
     return jnp.dot(a, b, preferred_element_type=F32)
 
 
-def convolve(high, low, weight, start, count):
+def convolve(high, low, weight, first, rows, pitch=PITCH):
     def taps(src):
-        return jnp.concatenate([src[start + a * PITCH : start + a * PITCH + count, :] for a in range(3)], axis=1)
+        return jnp.concatenate([src[(first + a) * pitch : (first + a + rows) * pitch, :] for a in range(3)], axis=1)
 
     w = jnp.concatenate([weight[a] for a in range(3)], axis=0)
     both = dot(taps(high), w)
     return both[:, :LANES] + both[:, LANES:] + dot(taps(low), w[:, :LANES])
 
 
-def correlate(grad, high, low, start, spans):
+def correlate(grad, high, low, spans):
     hi, lo = split(grad.T)
     both = jnp.concatenate([hi, lo], axis=0)
     blocks = []
     for a, first, last in spans:
-        r = slice(start + a * PITCH, start + a * PITCH + WINDOW)
+        r = slice(a * SHORT, a * SHORT + WINDOW)
         out = dot(both, high[r, first:last])
         blocks.append(out[:LANES] + out[LANES:] + dot(hi, low[r, first:last]))
     return blocks
@@ -77,16 +81,17 @@
 HALF = 9 * LANES // 2
 
 
-def correlate_half(core, s2, high, low, start, out):
-    mask = column_mask(6, (PITCH, LANES))
-    own = [s2[(i + 2) * PITCH : (i + 3) * PITCH, :] * mask for i in range(ROWS)]
-    grad = jnp.concatenate(own + [jnp.zeros((PITCH, LANES), F32)], axis=0)
+def correlate_half(core, a1, s2, high, low, out):
+    spread(a1, high, low, 18, first=2, col=6, width=SHORT)
+    mask = column_mask(0, (SHORT, LANES))
+    own = [s2[(i + 2) * PITCH + 6 : (i + 2) * PITCH + 6 + SHORT, :] * mask for i in range(ROWS)]
+    grad = jnp.concatenate(own + [jnp.zeros((SHORT, LANES), F32)], axis=0)
     for half in range(2):
 
         @pl.when(core == half)
         def _():
             r = -half * (LANES // 2)
-            for block in correlate(grad, high, low, start, HALVES[half]):
+            for block in correlate(grad, high, low, HALVES[half]):
                 for k in range(0, block.shape[1], LANES):
                     first, last = max(r, 0), min(r + LANES, HALF)
                     out[first:last, :] = block[first - r : last - r, k : k + LANES]
@@ -115,17 +120,22 @@
     weight[a, b * LANES : (b + 1) * LANES, LANES:] = lo
 
 
-def prepare_kernel(core, own, inner, outer, w_first, w_second, x, w1, w2, pad):
-    first = core[0] == 0
+def activate(h, inside):
+    sigma = jax.nn.sigmoid(h)
+    return h * sigma * inside, sigma * (1.0 + h * (1.0 - sigma)) * inside
+
+
+def prepare_kernel(core, consts, own, inner, outer, w_first, w_second, x, a1, slopes, w1, w2, pad, high, low):
+    upper = core[0] == 0
     x[...] = jnp.zeros_like(x)
     for i in range(ROWS + 8):
         r = i * PITCH
         if i < 4:
-            row = jnp.where(first, outer[i], inner[i])
+            row = jnp.where(upper, outer[i], inner[i])
         elif i < ROWS + 4:
             row = own[i - 4]
         else:
-            row = jnp.where(first, inner[i - ROWS - 4], outer[i - ROWS - 4])
+            row = jnp.where(upper, inner[i - ROWS - 4], outer[i - ROWS - 4])
         x[r + 8 : r + 8 + COLS, :CIN] = row
     pad[...] = jnp.zeros_like(pad)
     for a in range(3):
@@ -134,38 +144,53 @@
         hi, lo = split(pad[...])
         w1[a, :, :LANES] = hi
         w1[a, :, LANES:] = lo
+    spread_packed(x, high, low, ROWS + 8)
+    for first, rows in chunks(ROWS + 6, 2):
+        acc = convolve(high, low, w1, first, rows)
+        for k in range(rows):
+            i = first + k
+            inside = jnp.where(consts[6:7, i : i + 1] > 0.0, 1.0, 0.0)
+            r = slice(i * PITCH, (i + 1) * PITCH)
+            a1[r, :], slopes[r, :] = activate(acc[k * PITCH : (k + 1) * PITCH] + consts[0:1, :], inside)
+    a1[N1:, :] = jnp.zeros((8, LANES), F32)
     for t in range(9):
         store_weight(w2, t, w_second[t].T)
 
 
-def forward_kernel(core, half, consts, centre, outer, inner, w1, w2, cells, a1, s1, s2, small, send, x, slopes, high, low, high1, low1):
-    first = half[0] == 0
+def forward_kernel(core, half, consts, centre, a1_part, slopes_part, outer, inner, w1, w2, cells, a1, s1, s2, small, send, x, slopes, edge, high, low, high1, low1, high2, low2):
+    west = half[0] == 0
     b1, b2 = consts[0:1, :], consts[1:2, :]
     weights = [consts[6:7, i : i + 1] for i in range(ROWS + 6)]
     x[...] = centre[...]
+    a1[...] = a1_part[...]
+    slopes[...] = slopes_part[...]
+    edge[...] = jnp.zeros_like(edge)
     for i in range(ROWS + 8):
+        r, q = i * PITCH, i * NARROW
+        x[r + 4 : r + 8, :CIN] = jnp.where(west, outer[i], inner[i])
+        x[r + 8 + COLS : r + 12 + COLS, :CIN] = jnp.where(west, inner[i], outer[i])
+        edge[q : q + 6, :] = x[r + 4 : r + 10, :]
+        edge[q + 8 : q + 14, :] = x[r + 6 + COLS : r + 12 + COLS, :]
+    cells[...] = x[3 * PITCH : 21 * PITCH + 8, :]
+    spread_packed(edge, high1, low1, ROWS + 8, width=NARROW, pitch=NARROW)
+    acc = convolve(high1, low1, w1, 0, ROWS + 6, NARROW)
+    for i in range(ROWS + 6):
         r = i * PITCH
-        x[r + 4 : r + 8, :CIN] = jnp.where(first, outer[i], inner[i])
-        x[r + 8 + COLS : r + 12 + COLS, :CIN] = jnp.where(first, inner[i], outer[i])
-    cells[...] = x[3 * PITCH : 21 * PITCH + 8, :]
-    spread_packed(x, high1, low1, 0, NX)
-    for first, rows in chunks(ROWS + 6, 2):
-        acc = convolve(high1, low1, w1, first * PITCH, rows * PITCH)
-        for k in range(rows):
-            r = (first + k) * PITCH
-            h = acc[k * PITCH : (k + 1) * PITCH] + b1
-            sigma = jax.nn.sigmoid(h)
-            inside = jnp.where(weights[first + k] > 0.0, 1.0, 0.0)
-            a1[r : r + PITCH, :] = h * sigma * inside
-            slopes[r : r + PITCH, :] = sigma * (1.0 + h * (1.0 - sigma)) * inside
-    a1[N1:, :] = jnp.zeros((8, LANES), F32)
-    s1[...] = slopes[2 * PITCH + 2 : 2 * PITCH + 2 + N3, :]
-    spread(a1, high, low, 0, N1)
+        inside = jnp.where(weights[i] > 0.0, 1.0, 0.0)
+        active, slope = activate(acc[i * NARROW : (i + 1) * NARROW] + b1, inside)
+        a1[r + 4 : r + 8, :] = active[:4]
+        a1[r + 6 + COLS : r + 10 + COLS, :] = active[8:12]
+        slopes[r + 4 : r + 8, :] = slope[:4]
+        slopes[r + 6 + COLS : r + 10 + COLS, :] = slope[8:12]
+    for i in range(ROWS + 2):
+        r = (i + 2) * PITCH + 6
+        s1[i * SHORT : (i + 1) * SHORT, :] = slopes[r : r + SHORT, :]
+    spread(a1, high, low, ROWS + 6)
     mask = column_mask(6, (PITCH, LANES))
     pooled = jnp.zeros((PITCH, LANES), F32)
     bias = jnp.zeros((PITCH, LANES), F32)
     for first, rows in chunks(ROWS + 4, 2):
-        acc = convolve(high, low, w2, first * PITCH, rows * PITCH)
+        acc = convolve(high, low, w2, first, rows)
         for k in range(rows):
             i = first + k
             r = i * PITCH
@@ -180,7 +205,7 @@
     s2[N2:, :] = jnp.zeros((8, LANES), F32)
     small[0:1, :] = jnp.sum(pooled * mask, axis=0, keepdims=True)
     small[1:2, :] = jnp.sum(bias * mask, axis=0, keepdims=True)
-    correlate_half(1 - core[0], s2, high, low, 2 * PITCH, send)
+    correlate_half(1 - core[0], a1, s2, high2, low2, send)
     send[HALF : HALF + 2, :] = small[...]
 
 
@@ -192,8 +217,7 @@
 
 
 def second_kernel(core, a1, s2, out, high, low):
-    spread(a1.at[2 * PITCH :], high, low, 0, 18 * PITCH)
-    correlate_half(core[0], s2, high, low, 0, out)
+    correlate_half(core[0], a1, s2, high, low, out)
 
 
 def pair_kernel(own, other, small, out):
@@ -254,24 +278,24 @@
 
 
 def backward_kernel(sums, modes, consts, s1, s2, x, w_second, out, g1, weight, rows, high, low, high1, low1):
-    spread(s2, high, low, 0, N2)
+    spread(s2, high, low, ROWS + 4, col=4, width=SHORT)
     d_pooled = mode_gradients(sums, modes, consts)[3]
     column = jnp.broadcast_to(d_pooled, (LANES, LANES)).T
     for t in range(9):
         store_weight(weight, t, w_second[8 - t] * column)
-    for first, count in chunks(ROWS + 2, 6):
-        r, n = first * PITCH, count * PITCH
-        g1[r : r + n, :] = convolve(high, low, weight, r, n) * s1[r : r + n, :]
+    for first, count in chunks(ROWS + 2, 3):
+        r = slice(first * SHORT, (first + count) * SHORT)
+        g1[r, :] = convolve(high, low, weight, first, count, SHORT) * s1[r, :]
     g1[N3:, :] = jnp.zeros((8, LANES), F32)
 
-    mask = column_mask(7, (PITCH, LANES))
-    own = [g1[(i + 1) * PITCH - 2 : (i + 2) * PITCH - 2, :] * mask for i in range(ROWS)]
+    mask = column_mask(1, (SHORT, LANES))
+    own = [g1[(i + 1) * SHORT : (i + 2) * SHORT, :] * mask for i in range(ROWS)]
     bias1 = own[0]
     for row in own[1:]:
         bias1 = bias1 + row
-    grad = jnp.concatenate(own + [jnp.zeros((PITCH, LANES), F32)], axis=0)
-    spread_packed(x, high1, low1, 0, 18 * PITCH)
-    for a, block in enumerate(correlate(grad, high1, low1, 0, [(a, 0, 2 * LANES) for a in range(3)])):
+    grad = jnp.concatenate(own + [jnp.zeros((SHORT, LANES), F32)], axis=0)
+    spread_packed(x, high1, low1, 18, col=6, width=SHORT)
+    for a, block in enumerate(correlate(grad, high1, low1, [(a, 0, 2 * LANES) for a in range(3)])):
         rows[3 * a * CIN : 3 * (a + 1) * CIN, :] = block.T[: 3 * CIN]
     rows[9 * CIN : 9 * CIN + 1, :] = jnp.sum(bias1, axis=0, keepdims=True)
     rows[9 * CIN + 1 :, :] = jnp.zeros((rows.shape[0] - 9 * CIN - 1, LANES), F32)
@@ -286,11 +310,11 @@
     pad[...] = jnp.zeros_like(pad)
     for t in range(9):
         store_weight(weight, t, padded_rows(pad, w_first[8 - t]).T)
-    spread(g1, high, low, 0, N3)
+    spread(g1, high, low, ROWS + 2, width=SHORT, pitch=SHORT)
     for first, count in chunks(ROWS, 2):
-        acc = convolve(high, low, weight, first * PITCH, count * PITCH) * scale
+        acc = convolve(high, low, weight, first, count, SHORT) * scale
         for k in range(count):
-            out[first + k] = acc[k * PITCH + 4 : k * PITCH + 4 + COLS, :CIN]
+            out[first + k] = acc[k * SHORT : k * SHORT + COLS, :CIN]
 
 
 def finish_kernel(core, mine, other, spread_d, w_second, w_first, b_first, rows):
@@ -377,20 +401,27 @@
     packed = ((3, 2 * LANES, 2 * LANES), BF16)
     pad = ((LANES, LANES), F32)
     pair = lambda n, width=3 * LANES: [((n, width), BF16), ((n, width), BF16)]
-    centre, w1, w2 = call(prepare_kernel, [(NX + 8, LANES), packed, weight], [((2 * LANES, LANES), F32)], 10**9, smem=(0,))(
-        core, own, inner, outer, w_first, w_second
-    )
+    centre, a1, slopes, w1, w2 = call(
+        prepare_kernel,
+        [(NX + 8, LANES), (N1 + 8, LANES), (N1, LANES), packed, weight],
+        [((2 * LANES, LANES), F32)] + pair(NX, 2 * LANES),
+        10**9,
+        smem=(0,),
+    )(core, consts, own, inner, outer, w_first, w_second)
     swap_cores = lambda v: lax.ppermute(v, "c", [(0, 1), (1, 0)])
     x, a1, s1, s2, small, send = call(
         forward_kernel,
         [(18 * PITCH + 8, LANES), (N1 + 8, LANES), (N3, LANES), (N2 + 8, LANES), (2, LANES), (HALF + 8, LANES)],
-        [((NX + 8, LANES), F32), ((N1, LANES), F32)] + pair(N1) + pair(NX, 2 * LANES),
+        [((NX + 8, LANES), F32), ((N1, LANES), F32), ((23 * NARROW + 8, LANES), F32)]
+        + pair(N1)
+        + pair(23 * NARROW, 2 * LANES)
+        + pair(18 * SHORT),
         10**9,
         smem=(0, 1),
-    )(core, half, consts, centre, outer_strip, inner_strip, w1, w2)
+    )(core, half, consts, centre, a1, slopes, outer_strip, inner_strip, w1, w2)
 
     other = swap_cores(send)
-    (half,) = call(second_kernel, [(HALF, LANES)], pair(18 * PITCH), 10**9, smem=(0,))(core, a1, s2)
+    (half,) = call(second_kernel, [(HALF, LANES)], pair(18 * SHORT), 10**9, smem=(0,))(core, a1, s2)
     share2 = HALF * 2 // n_pl
     (part,) = call(pair_kernel, [(n_pl // 2, share2 + 2, ch)], [], 10**6)(half, other, small)
     bit2 = -(-share2 // n_z)
@@ -401,7 +432,7 @@
     g1rows, g1 = call(
         backward_kernel,
         [(n_pl, share1, ch), (N3 + 8, LANES)],
-        [weight, ((n_pl * share1, LANES), F32)] + pair(N2) + pair(18 * PITCH, 2 * LANES),
+        [weight, ((n_pl * share1, LANES), F32)] + pair(19 * SHORT) + pair(18 * SHORT, 2 * LANES),
         10**9,
     )(mine, modes, consts, s1, s2, x, w_second)
 
@@ -424,7 +455,7 @@
         [(9, ch, ch), (9, cin, ch), (1, ch)],
         [((2 * HALF, LANES), F32)],
         10**6,
-        (0,),
+        smem=(0,),
     )(core, whole, other, spread_d)
     return (grad_field.transpose(2, 0, 1), grad_w_first.transpose(0, 2, 1), grad_b_first[0], grad_w_second, bias2[0], d_modes)
 

time: 128 us -> 127 us (level)
  transfers between devices with their start and end apart: 7 -> 7, of which waited for: 3 -> 4; matrix products, arithmetic and copies ran while one was open for 1% -> 1% of each run, Pallas kernels for 3% -> 4%
where the time goes in v6:
time: 127 us
  blocking collectives  59.3 us (47%)
  starting transfers between devices  39.3 us (31%)
  Pallas kernels  12.9 us (10%)
  waiting for transfers between devices  11.3 us (9%)
  local copies, waits for them, and re-layouts  2.96 us (2%)
    all_to_all x4, blocking collectives, swap(): return lax.all_to_all(pieces, axes, 0, 0, tiled=True)  59.3 us
    pallas_call x10, Pallas kernels, run(): pl.pallas_call(kernel, out_shape=[jax.ShapeDtypeStruct(s, d) for s, d in...  12.9 us
    ppermute x1, starting transfers between devices, body(): outer_strip = lax.ppermute(strips[0], LON, far_pairs(n_lon, True))  10.6 us
    ppermute x2, starting transfers between devices, body(): swap_cores = lambda v: lax.ppermute(v, 'c', [(0, 1), (1, 0)])  9.85 us
    all_to_all x1, waiting for transfers between devices, swap(): return lax.all_to_all(pieces, axes, 0, 0, tiled=True)  7.88 us
    all_to_all x1, starting transfers between devices, swap(): return lax.all_to_all(pieces, axes, 0, 0, tiled=True)  7.32 us
    ppermute x1, starting transfers between devices, body(): lax.ppermute(lax.dynamic_slice_in_dim(own, (1 - core) * (rows - 4), 4, 0)...  4.94 us
    ppermute x1, starting transfers between devices, body(): lax.ppermute(lax.dynamic_slice_in_dim(own, core * (rows - 4), 4, 0), LAT,...  4.64 us
  transfers between devices with their start and end apart: 7, of which 4 were waited for; matrix products, arithmetic and copies ran while one was open for 1% of the time, Pallas kernels for 4%

profile of v6, /device:TPU:1, one launch (start us, length us, event | category | flops | bytes accessed | tf_op | source)
XLA Modules:
  0.0 126.7 jit_solution(15890068495054689338)
XLA Ops:
  0.6 0.0 copy-start
  0.6 0.0 copy-start.5
  0.7 0.0 copy-start.6
  0.7 0.0 copy-start.7
  0.7 1.0 dynamic-slice_bitcast_fusion
  1.7 0.0 copy-start.3
  1.7 4.6 %collective-permute-start.1 = (f32[4,45,69]{2,1,0:T(8,128)S(1)}, f32[4,45,69]{2,1,0:T(8,128)S(1)}, u32[]{:S(2)}, u32[]{:S(2)}) collective-permute-start(f32[4,45,69]{2,1,0:T(8,128)S(1)} %get-tuple-element.52), channel_id=1, source_target_pairs={{32,64},{96,128},{160,192},{224,256},{288,320},{352,384},{416,448}... | collective-permute-start | bytes 149048 | tf_op jit(solution)/shard_map/ppermute | solution.py:391
  6.3 4.9 %collective-permute-start = (f32[4,45,69]{2,1,0:T(8,128)S(1)}, f32[4,45,69]{2,1,0:T(8,128)S(1)}, u32[]{:S(2)}, u32[]{:S(2)}) collective-permute-start(f32[4,45,69]{2,1,0:T(8,128)S(1)} %get-tuple-element.53), channel_id=1, source_target_pairs={{0,32},{64,96},{128,160},{192,224},{256,288},{320,352},{384,416},{... | collective-permute-start | bytes 149048 | tf_op jit(solution)/shard_map/ppermute | solution.py:390
  11.3 0.0 copy-done
  11.4 0.8 dynamic_slice.27
  12.1 0.0 copy-done.5
  12.1 0.0 copy-done.6
  12.1 0.0 copy-done.7
  12.1 0.1 concatenate.9
  12.2 0.0 collective-permute-done.1.outer
  12.2 0.0 collective-permute-done.inner
  12.3 10.6 %collective-permute-start.2 = (f32[23,4,69]{2,1,0:T(4,128)S(1)}, f32[23,4,69]{2,1,0:T(4,128)S(1)}, u32[]{:S(2)}, u32[]{:S(2)}) collective-permute-start(f32[23,4,69]{2,1,0:T(4,128)S(1)} %pad_maximum_fusion), channel_id=1, source_target_pairs={{1,2},{3,4},{5,6},{7,8},{9,10},{11,12},{13,14},{15,16},{17,18},{19... | collective-permute-start | bytes 76184 | tf_op jit(solution)/shard_map/ppermute | solution.py:396
  22.9 1.9 %collective-permute-start.3 = (f32[23,4,69]{2,1,0:T(4,128)S(1)}, f32[23,4,69]{2,1,0:T(4,128)S(1)}, u32[]{:S(2)}, u32[]{:S(2)}) collective-permute-start(f32[23,4,69]{2,1,0:T(4,128)S(1)} %pad_maximum_fusion.1), channel_id=1, source_target_pairs={{0,1},{2,3},{4,5},{6,7},{8,9},{10,11},{12,13},{14,15},{16,17},{18,... | collective-permute-start | bytes 76184 | tf_op jit(solution)/shard_map/ppermute | solution.py:397
  24.8 0.0 copy-done.3
  24.8 0.0 copy-start.1
  24.9 1.1 copy-done.1
  25.9 1.6 %shard_map.127 = (f32[1480,128]{1,0:T(8,128)S(1)}, f32[1352,128]{1,0:T(8,128)S(1)}, f32[1344,128]{1,0:T(8,128)S(1)}, bf16[3,256,256]{2,1,0:T(8,128)(2,1)S(1)}, bf16[3,384,256]{2,1,0:T(8,128)(2,1)S(1)}) custom-call(s32[1]{0:T(128)} %bitcast.core, f32[7,128]{1,0:T(8,128)S(1)} %bitcast.18, f32[15,45,69]{2,1,0:T(8,128)S(1)} %bitcast.17, ...), custom_call_target="tpu_custom_call" | custom-call | flops 1000000000 | bytes 4194304 | tf_op jit(solution)/shard_map/pallas_call | solution.py:345
  27.5 0.0 collective-permute-done.2.outer
  27.5 1.7 %collective-permute-done.3.inner = f32[23,4,69]{2,1,0:T(4,128)S(1)} collective-permute-done((f32[23,4,69]{2,1,0:T(4,128)S(1)}, f32[23,4,69]{2,1,0:T(4,128)S(1)}, u32[]{:S(2)}, u32[]{:S(2)}) %collective-permute-start.3) | collective-permute-done | bytes 25424 | tf_op jit(solution)/shard_map/ppermute | solution.py:397
  29.2 3.5 %shard_map.128 = (f32[1160,128]{1,0:T(8,128)S(1)}, f32[1352,128]{1,0:T(8,128)S(1)}, f32[816,128]{1,0:T(8,128)S(1)}, f32[1224,128]{1,0:T(8,128)S(1)}, f32[2,128]{1,0:T(2,128)S(1)}, /*index=5*/f32[584,128]{1,0:T(8,128)S(1)}) custom-call(s32[1]{0:T(128)} %bitcast.core, s32[1]{0:T(128)} %bitcast.1.half, f32[7,128]{1,0:T(8,128)S(1)} %bitcast.19, ...), custom_call_target="tpu_custom_call" | custom-call | flops 1000000000 | bytes 4194304 | tf_op jit(solution)/shard_map/pallas_call | solution.py:345
  32.8 3.5 %collective-permute-start.4 = (f32[584,128]{1,0:T(8,128)S(1)}, f32[584,128]{1,0:T(8,128)S(1)}, u32[]{:S(2)}, u32[]{:S(2)}) collective-permute-start(f32[584,128]{1,0:T(8,128)S(1)} %get-tuple-element.35), channel_id=1, source_target_pairs={{0,32},{32,0},{1,33},{33,1},{2,34},{34,2},{3,35},{35,3},{4,36},{36... | collective-permute-start | bytes 897032 | tf_op jit(solution)/shard_map/ppermute | solution.py:411
  36.2 0.9 shard_map.129.own
  37.1 0.3 collective-permute-done.4.other
  37.5 0.0 copy-start.2
  37.5 13.0 %all_to_all.25.parts = f32[16,38,128]{2,1,0:T(8,128)S(1)} all-to-all(f32[16,38,128]{2,1,0:T(8,128)S(1)} %shard_map.130), channel_id=1, replica_groups=mesh['y'=4,'xl'=2,'c'=2,'z'=16,'xh'=2] {'y','xl','xh'}, dimensions={0} | all-to-all | bytes 622592 | tf_op jit(solution)/shard_map/all_to_all | solution.py:376
  50.5 0.0 copy-start.4
  50.5 18.4 %all_to_all.26.sums.r_2_ = f32[16,5,128]{2,1,0:T(8,128)S(1)} all-to-all(f32[16,5,128]{2,1,0:T(8,128)S(1)} %shard_map.131), channel_id=1, replica_groups=mesh['y'=4,'xl'=2,'c'=2,'z'=16,'xh'=2] {'z'}, dimensions={0} | all-to-all | bytes 81920 | tf_op jit(solution)/shard_map/all_to_all | solution.py:376
  68.9 0.0 copy-done.2
  68.9 0.0 copy-done.4
  68.9 3.6 %shard_map.132 = (f32[32,20,128]{2,1,0:T(8,128)}, f32[824,128]{1,0:T(8,128)S(1)}) custom-call(f32[16,5,128]{2,1,0:T(8,128)S(1)} %all_to_all.26.sums.r_2_, f32[512,128]{1,0:T(8,128)S(1)} %copy-done.4, f32[7,128]{1,0:T(8,128)S(1)} %bitcast.20, f32[816,128]{1,0:T(8,128)S(1)} %get-tuple-element.37.s1, f32[1224,128]{1,0:T(8,128)S(1)} %get-tuple-element.34.s2, ...), custom_call_target="tpu_custom_call" | custom-call | flops 1000000000 | bytes 4194304 | tf_op jit(solution)/shard_map/pallas_call | solution.py:345
  72.5 7.3 %all-to-all-start.2 = ((f32[32,20,128]{2,1,0:T(8,128)}), f32[32,20,128]{2,1,0:T(8,128)S(1)}, u32[]{:S(2)}, u32[]{:S(2)}) async-start(f32[32,20,128]{2,1,0:T(8,128)} %get-tuple-element.39), calls=%async_computation.2 | async-start | bytes 786432 | tf_op jit(solution)/shard_map/all_to_all | solution.py:376
  79.9 2.1 %shard_map.133 = (f32[15,45,69]{2,1,0:T(8,128)}, f32[512,128]{1,0:T(8,128)}, f32[128,128]{1,0:T(8,128)S(1)}, f32[1,128]{1,0:T(1,128)}) custom-call(f32[824,128]{1,0:T(8,128)S(1)} %get-tuple-element.40.r_0_, f32[9,69,128]{2,1,0:T(8,128)S(1)} %bitcast.23, f32[16,5,128]{2,1,0:T(8,128)S(1)} %all_to_all.26.sums.r_2_, f32[512,128]{1,0:T(8,128)S(1)} %copy-done.4, ...), custom_call_target="tpu_custom_call" | custom-call | flops 1000000000 | bytes 4194304 | tf_op jit(solution)/shard_map/pallas_call | solution.py:345
  82.0 7.9 %all-to-all-done.2.parts = f32[32,20,128]{2,1,0:T(8,128)S(1)} async-done(((f32[32,20,128]{2,1,0:T(8,128)}), f32[32,20,128]{2,1,0:T(8,128)S(1)}, u32[]{:S(2)}, u32[]{:S(2)}) %all-to-all-start.2) | async-done | bytes 327712 | tf_op jit(solution)/shard_map/all_to_all | solution.py:376
  89.8 0.1 shard_map.134
  89.9 15.8 %all_to_all.27.r_0_ = f32[16,23,128]{2,1,0:T(8,128)S(1)} all-to-all(f32[16,23,128]{2,1,0:T(8,128)S(1)} %shard_map.134), channel_id=1, replica_groups=mesh['y'=4,'xl'=2,'c'=2,'z'=16,'xh'=2] {'z'}, dimensions={0} | all-to-all | bytes 376832 | tf_op jit(solution)/shard_map/all_to_all | solution.py:376
  105.7 12.1 %all_to_all.28.mine = f32[16,56,128]{2,1,0:T(8,128)S(1)} all-to-all(f32[16,56,128]{2,1,0:T(8,128)S(1)} %shard_map.135), channel_id=1, replica_groups=mesh['y'=4,'xl'=2,'c'=2,'z'=16,'xh'=2] {'y','xl','xh'}, dimensions={0} | all-to-all | bytes 917504 | tf_op jit(solution)/shard_map/all_to_all | solution.py:376
  117.8 6.4 %collective-permute-start.5 = (f32[16,56,128]{2,1,0:T(8,128)S(1)}, f32[16,56,128]{2,1,0:T(8,128)S(1)}, u32[]{:S(2)}, u32[]{:S(2)}) collective-permute-start(f32[16,56,128]{2,1,0:T(8,128)S(1)} %all_to_all.28.mine), channel_id=1, source_target_pairs={{0,32},{32,0},{1,33},{33,1},{2,34},{34,2},{3,35},{35,3},{4,36},{36... | collective-permute-start | bytes 1376264 | tf_op jit(solution)/shard_map/ppermute | solution.py:411
  124.2 1.4 %collective-permute-done.5.other = f32[16,56,128]{2,1,0:T(8,128)S(1)} collective-permute-done((f32[16,56,128]{2,1,0:T(8,128)S(1)}, f32[16,56,128]{2,1,0:T(8,128)S(1)}, u32[]{:S(2)}, u32[]{:S(2)}) %collective-permute-start.5) | collective-permute-done | bytes 458784 | tf_op jit(solution)/shard_map/ppermute | solution.py:411
  125.6 1.0 shard_map.136
  (8 shorter events, 0.2 us)
Async XLA Ops:
  0.6 10.7 %copy-start = (f32[69,15,45]{0,2,1:T(8,128)S(1)}, f32[69,15,45]{0,2,1:T(8,128)}, u32[]{:S(2)}) copy-start(f32[69,15,45]{0,2,1:T(8,128)} %param.8) | copy-start | bytes 558904
  0.6 11.5 %copy-start.5 = (f32[512]{0:T(512)S(1)}, f32[512]{0:T(512)}, u32[]{:S(2)}) copy-start(f32[512]{0:T(512)} %param.14) | copy-start | bytes 6148
  0.7 11.5 %copy-start.6 = (f32[128]{0:T(128)S(1)}, f32[128]{0:T(128)}, u32[]{:S(2)}) copy-start(f32[128]{0:T(128)} %param.10) | copy-start | bytes 1540
  0.7 11.5 %copy-start.7 = (f32[128]{0:T(128)S(1)}, f32[128]{0:T(128)}, u32[]{:S(2)}) copy-start(f32[128]{0:T(128)} %param.12) | copy-start | bytes 1540
  1.7 23.2 %copy-start.3 = (f32[9,128,69]{1,2,0:T(8,128)S(1)}, f32[9,128,69]{1,2,0:T(8,128)}, u32[]{:S(2)}) copy-start(f32[9,128,69]{1,2,0:T(8,128)} %param.9) | copy-start | bytes 953860
  1.7 10.5 %collective-permute-start.1 = (f32[4,45,69]{2,1,0:T(8,128)S(1)}, f32[4,45,69]{2,1,0:T(8,128)S(1)}, u32[]{:S(2)}, u32[]{:S(2)}) collective-permute-start(f32[4,45,69]{2,1,0:T(8,128)S(1)} %get-tuple-element.52), channel_id=1, source_target_pairs={{32,64},{96,128},{160,192},{224,256},{288,320},{352,384},{416,448}... | collective-permute-start | bytes 149048 | tf_op jit(solution)/shard_map/ppermute | solution.py:391
  6.3 5.9 %collective-permute-start = (f32[4,45,69]{2,1,0:T(8,128)S(1)}, f32[4,45,69]{2,1,0:T(8,128)S(1)}, u32[]{:S(2)}, u32[]{:S(2)}) collective-permute-start(f32[4,45,69]{2,1,0:T(8,128)S(1)} %get-tuple-element.53), channel_id=1, source_target_pairs={{0,32},{64,96},{128,160},{192,224},{256,288},{320,352},{384,416},{... | collective-permute-start | bytes 149048 | tf_op jit(solution)/shard_map/ppermute | solution.py:390
  12.3 15.2 %collective-permute-start.2 = (f32[23,4,69]{2,1,0:T(4,128)S(1)}, f32[23,4,69]{2,1,0:T(4,128)S(1)}, u32[]{:S(2)}, u32[]{:S(2)}) collective-permute-start(f32[23,4,69]{2,1,0:T(4,128)S(1)} %pad_maximum_fusion), channel_id=1, source_target_pairs={{1,2},{3,4},{5,6},{7,8},{9,10},{11,12},{13,14},{15,16},{17,18},{19... | collective-permute-start | bytes 76184 | tf_op jit(solution)/shard_map/ppermute | solution.py:396
  22.9 6.3 %collective-permute-start.3 = (f32[23,4,69]{2,1,0:T(4,128)S(1)}, f32[23,4,69]{2,1,0:T(4,128)S(1)}, u32[]{:S(2)}, u32[]{:S(2)}) collective-permute-start(f32[23,4,69]{2,1,0:T(4,128)S(1)} %pad_maximum_fusion.1), channel_id=1, source_target_pairs={{0,1},{2,3},{4,5},{6,7},{8,9},{10,11},{12,13},{14,15},{16,17},{18,... | collective-permute-start | bytes 76184 | tf_op jit(solution)/shard_map/ppermute | solution.py:397
  24.8 1.1 copy-start.1
  32.8 4.7 %collective-permute-start.4 = (f32[584,128]{1,0:T(8,128)S(1)}, f32[584,128]{1,0:T(8,128)S(1)}, u32[]{:S(2)}, u32[]{:S(2)}) collective-permute-start(f32[584,128]{1,0:T(8,128)S(1)} %get-tuple-element.35), channel_id=1, source_target_pairs={{0,32},{32,0},{1,33},{33,1},{2,34},{34,2},{3,35},{35,3},{4,36},{36... | collective-permute-start | bytes 897032 | tf_op jit(solution)/shard_map/ppermute | solution.py:411
  37.5 31.5 %copy-start.2 = (f32[9,128,128]{2,1,0:T(8,128)S(1)}, f32[9,128,128]{2,1,0:T(8,128)}, u32[]{:S(2)}) copy-start(f32[9,128,128]{2,1,0:T(8,128)} %w_second.3) | copy-start | bytes 1769476
  50.5 18.5 %copy-start.4 = (f32[512,128]{1,0:T(8,128)S(1)}, f32[512,128]{1,0:T(8,128)}, u32[]{:S(2)}) copy-start(f32[512,128]{1,0:T(8,128)} %r_3_.1) | copy-start | bytes 786436
  72.5 17.3 %all-to-all-start.2 = ((f32[32,20,128]{2,1,0:T(8,128)}), f32[32,20,128]{2,1,0:T(8,128)S(1)}, u32[]{:S(2)}, u32[]{:S(2)}) async-start(f32[32,20,128]{2,1,0:T(8,128)} %get-tuple-element.39), calls=%async_computation.2 | async-start | bytes 786432 | tf_op jit(solution)/shard_map/all_to_all | solution.py:376
  117.8 7.8 %collective-permute-start.5 = (f32[16,56,128]{2,1,0:T(8,128)S(1)}, f32[16,56,128]{2,1,0:T(8,128)S(1)}, u32[]{:S(2)}, u32[]{:S(2)}) collective-permute-start(f32[16,56,128]{2,1,0:T(8,128)S(1)} %all_to_all.28.mine), channel_id=1, source_target_pairs={{0,32},{32,0},{1,33},{33,1},{2,34},{34,2},{3,35},{35,3},{4,36},{36... | collective-permute-start | bytes 1376264 | tf_op jit(solution)/shard_map/ppermute | solution.py:411

commit v7 on v6

--- a/solution.py
+++ b/solution.py
@@ -125,7 +125,7 @@
     return h * sigma * inside, sigma * (1.0 + h * (1.0 - sigma)) * inside
 
 
-def prepare_kernel(core, consts, own, inner, outer, w_first, w_second, x, a1, slopes, w1, w2, pad, high, low):
+def prepare_kernel(core, consts, own, inner, outer, w_first, w_second, x, a1, slopes, w1, w2, w1_back, pad, pad_back, high, low):
     upper = core[0] == 0
     x[...] = jnp.zeros_like(x)
     for i in range(ROWS + 8):
@@ -153,25 +153,34 @@
             r = slice(i * PITCH, (i + 1) * PITCH)
             a1[r, :], slopes[r, :] = activate(acc[k * PITCH : (k + 1) * PITCH] + consts[0:1, :], inside)
     a1[N1:, :] = jnp.zeros((8, LANES), F32)
+    pad_back[...] = jnp.zeros_like(pad_back)
     for t in range(9):
         store_weight(w2, t, w_second[t].T)
-
-
-def forward_kernel(core, half, consts, centre, a1_part, slopes_part, outer, inner, w1, w2, cells, a1, s1, s2, small, send, x, slopes, edge, high, low, high1, low1, high2, low2):
+        store_weight(w1_back, t, padded_rows(pad_back, w_first[8 - t]).T)
+
+
+def forward_kernel(core, half, consts, centre, a1_part, slopes_part, outer, inner, w1, w2, cells, a1, s1, s2, small, send, edge, high, low, high1, low1, high2, low2):
     west = half[0] == 0
     b1, b2 = consts[0:1, :], consts[1:2, :]
     weights = [consts[6:7, i : i + 1] for i in range(ROWS + 6)]
-    x[...] = centre[...]
     a1[...] = a1_part[...]
-    slopes[...] = slopes_part[...]
+    for i in range(ROWS + 2):
+        r = (i + 2) * PITCH + 6
+        s1[i * SHORT : (i + 1) * SHORT, :] = slopes_part[r : r + SHORT, :]
+    cells[...] = centre[3 * PITCH : 21 * PITCH + 8, :]
     edge[...] = jnp.zeros_like(edge)
     for i in range(ROWS + 8):
         r, q = i * PITCH, i * NARROW
-        x[r + 4 : r + 8, :CIN] = jnp.where(west, outer[i], inner[i])
-        x[r + 8 + COLS : r + 12 + COLS, :CIN] = jnp.where(west, inner[i], outer[i])
-        edge[q : q + 6, :] = x[r + 4 : r + 10, :]
-        edge[q + 8 : q + 14, :] = x[r + 6 + COLS : r + 12 + COLS, :]
-    cells[...] = x[3 * PITCH : 21 * PITCH + 8, :]
+        before = jnp.where(west, outer[i], inner[i])
+        after = jnp.where(west, inner[i], outer[i])
+        edge[q : q + 4, :CIN] = before
+        edge[q + 4 : q + 6, :] = centre[r + 8 : r + 10, :]
+        edge[q + 8 : q + 10, :] = centre[r + 6 + COLS : r + 8 + COLS, :]
+        edge[q + 10 : q + 14, :CIN] = after
+        if 3 <= i < 21:
+            r = (i - 3) * PITCH
+            cells[r + 4 : r + 8, :CIN] = before
+            cells[r + 8 + COLS : r + 12 + COLS, :CIN] = after
     spread_packed(edge, high1, low1, ROWS + 8, width=NARROW, pitch=NARROW)
     acc = convolve(high1, low1, w1, 0, ROWS + 6, NARROW)
     for i in range(ROWS + 6):
@@ -180,11 +189,10 @@
         active, slope = activate(acc[i * NARROW : (i + 1) * NARROW] + b1, inside)
         a1[r + 4 : r + 8, :] = active[:4]
         a1[r + 6 + COLS : r + 10 + COLS, :] = active[8:12]
-        slopes[r + 4 : r + 8, :] = slope[:4]
-        slopes[r + 6 + COLS : r + 10 + COLS, :] = slope[8:12]
-    for i in range(ROWS + 2):
-        r = (i + 2) * PITCH + 6
-        s1[i * SHORT : (i + 1) * SHORT, :] = slopes[r : r + SHORT, :]
+        if 2 <= i < ROWS + 4:
+            r = (i - 2) * SHORT
+            s1[r : r + 2, :] = slope[2:4]
+            s1[r + COLS : r + COLS + 3, :] = slope[8:11]
     spread(a1, high, low, ROWS + 6)
     mask = column_mask(6, (PITCH, LANES))
     pooled = jnp.zeros((PITCH, LANES), F32)
@@ -302,14 +310,11 @@
     write_pieces(out, rows)
 
 
-def field_kernel(scale, g1, w_first, sums, modes, consts, out, d_modes, spread_d, bias2, weight, pad, high, low):
+def field_kernel(scale, g1, weight, sums, modes, consts, out, d_modes, spread_d, bias2, high, low):
     total, pooled, d_amplitude, d_pooled = mode_gradients(sums, modes, consts)
     d_modes[...] = d_amplitude * pooled
     spread_d[...] = jnp.broadcast_to(d_pooled, (LANES, LANES)).T
     bias2[...] = total[1:2] * d_pooled
-    pad[...] = jnp.zeros_like(pad)
-    for t in range(9):
-        store_weight(weight, t, padded_rows(pad, w_first[8 - t]).T)
     spread(g1, high, low, ROWS + 2, width=SHORT, pitch=SHORT)
     for first, count in chunks(ROWS, 2):
         acc = convolve(high, low, weight, first, count, SHORT) * scale
@@ -367,9 +372,10 @@
 
 def row_weights(first, count, nlat, nlon):
     phi = (np.arange(nlat) + 0.5) * (math.pi / nlat) - math.pi / 2
-    table = np.zeros(nlat + 2 * count, np.float32)
-    table[count : count + nlat] = np.cos(phi) / (np.cos(phi).sum() * nlon)
-    return lax.dynamic_slice(jnp.asarray(table), (first + count,), (count,))
+    total = float(np.cos(phi).sum() * nlon)
+    row = first + jnp.arange(count, dtype=jnp.int32)
+    phi = (row.astype(F32) + 0.5) * (math.pi / nlat) - math.pi / 2
+    return jnp.where((row >= 0) & (row < nlat), jnp.cos(phi), 0.0) / total
 
 
 def swap(pieces, axes):
@@ -382,8 +388,8 @@
     n_lat, n_lon = lax.axis_size(LAT), lax.axis_size(LON)
     n_pl, n_z = lax.axis_size(PLANE), lax.axis_size(RING)
     nlat, nlon = rows * n_lat, cols * n_lon
-    weights = row_weights(lax.axis_index(LAT) * rows - 3, rows + 6, nlat, nlon)
-    consts = jnp.concatenate([b_first, b_second, cotangent, weights, jnp.zeros(LANES - rows - 6, F32)]).reshape(-1, LANES)
+    weights = row_weights(lax.axis_index(LAT) * rows - 3, LANES, nlat, nlon)
+    consts = jnp.concatenate([b_first, b_second, cotangent, weights]).reshape(-1, LANES)
 
     own = field.transpose(1, 2, 0)
     core, half = lax.axis_index("c"), lax.axis_index("xh")
@@ -401,10 +407,10 @@
     packed = ((3, 2 * LANES, 2 * LANES), BF16)
     pad = ((LANES, LANES), F32)
     pair = lambda n, width=3 * LANES: [((n, width), BF16), ((n, width), BF16)]
-    centre, a1, slopes, w1, w2 = call(
+    centre, a1, slopes, w1, w2, w1_back = call(
         prepare_kernel,
-        [(NX + 8, LANES), (N1 + 8, LANES), (N1, LANES), packed, weight],
-        [((2 * LANES, LANES), F32)] + pair(NX, 2 * LANES),
+        [(NX + 8, LANES), (N1 + 8, LANES), (N1, LANES), packed, weight, weight],
+        [((2 * LANES, LANES), F32), pad] + pair(NX, 2 * LANES),
         10**9,
         smem=(0,),
     )(core, consts, own, inner, outer, w_first, w_second)
@@ -412,7 +418,7 @@
     x, a1, s1, s2, small, send = call(
         forward_kernel,
         [(18 * PITCH + 8, LANES), (N1 + 8, LANES), (N3, LANES), (N2 + 8, LANES), (2, LANES), (HALF + 8, LANES)],
-        [((NX + 8, LANES), F32), ((N1, LANES), F32), ((23 * NARROW + 8, LANES), F32)]
+        [((23 * NARROW + 8, LANES), F32)]
         + pair(N1)
         + pair(23 * NARROW, 2 * LANES)
         + pair(18 * SHORT),
@@ -437,19 +443,19 @@
     )(mine, modes, consts, s1, s2, x, w_second)
 
     part = swap(g1rows, PLANE)
-    grad_field, d_modes, spread_d, bias2 = call(
-        lambda *r: field_kernel(float(nlat * nlon), *r),
-        [(rows, cols, cin), modes.shape, (LANES, LANES), (1, LANES)],
-        [weight, pad] + pair(N3),
-        10**9,
-    )(g1, w_first, mine, modes, consts)
-    part, grad_field = lax.optimization_barrier((part, grad_field))
     (both,) = call(ring_kernel, [(n_z, share1 + bit2, ch)], [], 10**6)(part, mine)
     (whole,) = call(
         lambda *r: plane_kernel(share2, *r), [(n_pl // 2, share2 + share1, ch)], [((share2, LANES), F32)], 10**6
     )(swap(both, RING))
     whole = swap(whole, CHIPS)
+    whole, g1 = lax.optimization_barrier((whole, g1))
     other = swap_cores(whole)
+    grad_field, d_modes, spread_d, bias2 = call(
+        lambda *r: field_kernel(float(nlat * nlon), *r),
+        [(rows, cols, cin), modes.shape, (LANES, LANES), (1, LANES)],
+        pair(N3),
+        10**9,
+    )(g1, w1_back, mine, modes, consts)
     grad_w_second, grad_w_first, grad_b_first = call(
         finish_kernel,
         [(9, ch, ch), (9, cin, ch), (1, ch)],

time: 127 us -> 127 us (level)
  blocking collectives: 59.3 us -> 76.2 us
  waiting for transfers between devices: 11.3 us -> 2.75 us
  starting transfers between devices: 39.3 us -> 32 us
    all_to_all x4 -> x5, blocking collectives: 59.3 us -> 76.2 us  [swap(): return lax.all_to_all(pieces, axes, 0, 0, tiled=True)]
    all_to_all x1 -> x0, waiting for transfers between devices: 7.88 us -> none  [swap(): return lax.all_to_all(pieces, axes, 0, 0, tiled=True)]
    all_to_all x1 -> x0, starting transfers between devices: 7.32 us -> none  [swap(): return lax.all_to_all(pieces, axes, 0, 0, tiled=True)]
    ppermute x2, waiting for transfers between devices: 1.7 us -> 0.28 us  [body(): swap_cores = lambda v: lax.ppermute(v, 'c', [(0, 1), (1, 0)])]
  transfers between devices with their start and end apart: 7 -> 6, of which waited for: 4 -> 3; matrix products, arithmetic and copies ran while one was open for 1% -> 0% of each run, Pallas kernels for 4% -> 3%
where the time goes in v7:
time: 127 us; the launch traced here: 126 us
  blocking collectives  76.2 us (60%)
  starting transfers between devices  32 us (25%)
  Pallas kernels  11.9 us (9%)
  waiting for transfers between devices  2.75 us (2%)
  local copies, waits for them, and re-layouts  2.14 us (2%)
    all_to_all x5, blocking collectives, swap(): return lax.all_to_all(pieces, axes, 0, 0, tiled=True)  76.2 us
    pallas_call x10, Pallas kernels, run(): pl.pallas_call(kernel, out_shape=[jax.ShapeDtypeStruct(s, d) for s, d in...  11.9 us
    ppermute x1, starting transfers between devices, body(): outer_strip = lax.ppermute(strips[0], LON, far_pairs(n_lon, True))  10.6 us
    ppermute x2, starting transfers between devices, body(): swap_cores = lambda v: lax.ppermute(v, 'c', [(0, 1), (1, 0)])  10 us
    ppermute x1, starting transfers between devices, body(): lax.ppermute(lax.dynamic_slice_in_dim(own, (1 - core) * (rows - 4), 4, 0)...  4.94 us
    ppermute x1, starting transfers between devices, body(): lax.ppermute(lax.dynamic_slice_in_dim(own, core * (rows - 4), 4, 0), LAT,...  4.51 us
  transfers between devices with their start and end apart: 6, of which 3 were waited for; matrix products, arithmetic and copies ran while one was open for 0% of the time, Pallas kernels for 3%

profile of v7, /device:TPU:1, one launch (start us, length us, event | category | flops | bytes accessed | tf_op | source)
XLA Modules:
  0.0 126.0 jit_solution(7089631422624423742)
XLA Ops:
  0.6 0.0 copy-start
  0.7 0.0 copy-start.5
  0.7 0.0 copy-start.6
  0.7 0.0 copy-start.7
  0.7 0.0 copy-start.3
  0.7 1.0 dynamic-slice_bitcast_fusion
  1.7 4.5 %collective-permute-start.1 = (f32[4,45,69]{2,1,0:T(8,128)S(1)}, f32[4,45,69]{2,1,0:T(8,128)S(1)}, u32[]{:S(2)}, u32[]{:S(2)}) collective-permute-start(f32[4,45,69]{2,1,0:T(8,128)S(1)} %get-tuple-element.54), channel_id=1, source_target_pairs={{32,64},{96,128},{160,192},{224,256},{288,320},{352,384},{416,448}... | collective-permute-start | bytes 149048 | tf_op jit(solution)/shard_map/ppermute | solution.py:397
  6.2 4.9 %collective-permute-start = (f32[4,45,69]{2,1,0:T(8,128)S(1)}, f32[4,45,69]{2,1,0:T(8,128)S(1)}, u32[]{:S(2)}, u32[]{:S(2)}) collective-permute-start(f32[4,45,69]{2,1,0:T(8,128)S(1)} %get-tuple-element.55), channel_id=1, source_target_pairs={{0,32},{64,96},{128,160},{192,224},{256,288},{320,352},{384,416},{... | collective-permute-start | bytes 149048 | tf_op jit(solution)/shard_map/ppermute | solution.py:396
  11.2 0.0 copy-done
  11.3 0.0 copy-done.5
  11.3 0.0 copy-done.6
  11.3 0.0 copy-done.7
  11.3 0.0 collective-permute-done.1.outer
  11.4 0.7 collective-permute-done.inner
  12.1 10.6 %collective-permute-start.2 = (f32[23,4,69]{2,1,0:T(4,128)S(1)}, f32[23,4,69]{2,1,0:T(4,128)S(1)}, u32[]{:S(2)}, u32[]{:S(2)}) collective-permute-start(f32[23,4,69]{2,1,0:T(4,128)S(1)} %pad_maximum_fusion), channel_id=1, source_target_pairs={{1,2},{3,4},{5,6},{7,8},{9,10},{11,12},{13,14},{15,16},{17,18},{19... | collective-permute-start | bytes 76184 | tf_op jit(solution)/shard_map/ppermute | solution.py:402
  22.8 1.9 %collective-permute-start.3 = (f32[23,4,69]{2,1,0:T(4,128)S(1)}, f32[23,4,69]{2,1,0:T(4,128)S(1)}, u32[]{:S(2)}, u32[]{:S(2)}) collective-permute-start(f32[23,4,69]{2,1,0:T(4,128)S(1)} %pad_maximum_fusion.1), channel_id=1, source_target_pairs={{0,1},{2,3},{4,5},{6,7},{8,9},{10,11},{12,13},{14,15},{16,17},{18,... | collective-permute-start | bytes 76184 | tf_op jit(solution)/shard_map/ppermute | solution.py:403
  24.7 0.0 copy-done.3
  24.7 0.0 copy-start.1
  24.7 1.1 copy-done.1
  25.8 1.6 %shard_map.118 = (f32[1480,128]{1,0:T(8,128)S(1)}, f32[1352,128]{1,0:T(8,128)S(1)}, f32[1344,128]{1,0:T(8,128)S(1)}, bf16[3,256,256]{2,1,0:T(8,128)(2,1)S(1)}, b...) custom-call(s32[1]{0:T(128)} %bitcast.core, f32[7,128]{1,0:T(8,128)S(1)} %maximum_bitcast_fusion.consts.r_4_, ...), custom_call_target="tpu_custom_call" | custom-call | flops 1000000000 | bytes 4194304 | tf_op jit(solution)/shard_map/pallas_call | solution.py:350
  27.4 0.0 collective-permute-done.2.outer
  27.4 1.7 %collective-permute-done.3.inner = f32[23,4,69]{2,1,0:T(4,128)S(1)} collective-permute-done((f32[23,4,69]{2,1,0:T(4,128)S(1)}, f32[23,4,69]{2,1,0:T(4,128)S(1)}, u32[]{:S(2)}, u32[]{:S(2)}) %collective-permute-start.3) | collective-permute-done | bytes 25424 | tf_op jit(solution)/shard_map/ppermute | solution.py:403
  29.1 3.4 %shard_map.119 = (f32[1160,128]{1,0:T(8,128)S(1)}, f32[1352,128]{1,0:T(8,128)S(1)}, f32[816,128]{1,0:T(8,128)S(1)}, f32[1224,128]{1,0:T(8,128)S(1)}, f32[2,128]{1,0:T(2,128)S(1)}, /*index=5*/f32[584,128]{1,0:T(8,128)S(1)}) custom-call(s32[1]{0:T(128)} %bitcast.core, s32[1]{0:T(128)} %bitcast.1.half, f32[7,128]{1,0:T(8,128)S(1)} %maximum_bitcast_fusion.consts.r_4_, ...), custom_call_target="tpu_custom_call" | custom-call | flops 1000000000 | bytes 4194304 | tf_op jit(solution)/shard_map/pallas_call | solution.py:350
  32.6 3.5 %collective-permute-start.4 = (f32[584,128]{1,0:T(8,128)S(1)}, f32[584,128]{1,0:T(8,128)S(1)}, u32[]{:S(2)}, u32[]{:S(2)}) collective-permute-start(f32[584,128]{1,0:T(8,128)S(1)} %get-tuple-element.36), channel_id=1, source_target_pairs={{0,32},{32,0},{1,33},{33,1},{2,34},{34,2},{3,35},{35,3},{4,36},{36... | collective-permute-start | bytes 897032 | tf_op jit(solution)/shard_map/ppermute | solution.py:417
  36.0 0.9 shard_map.120.own
  37.0 0.3 collective-permute-done.4.other
  37.3 0.0 copy-start.2
  37.3 13.0 %all_to_all.25.parts = f32[16,38,128]{2,1,0:T(8,128)S(1)} all-to-all(f32[16,38,128]{2,1,0:T(8,128)S(1)} %shard_map.121), channel_id=1, replica_groups=mesh['y'=4,'xl'=2,'c'=2,'z'=16,'xh'=2] {'y','xl','xh'}, dimensions={0} | all-to-all | bytes 622592 | tf_op jit(solution)/shard_map/all_to_all | solution.py:382
  50.3 0.0 copy-start.4
  50.3 18.4 %all_to_all.26.sums.r_2_ = f32[16,5,128]{2,1,0:T(8,128)S(1)} all-to-all(f32[16,5,128]{2,1,0:T(8,128)S(1)} %shard_map.122), channel_id=1, replica_groups=mesh['y'=4,'xl'=2,'c'=2,'z'=16,'xh'=2] {'z'}, dimensions={0} | all-to-all | bytes 81920 | tf_op jit(solution)/shard_map/all_to_all | solution.py:382
  68.7 0.0 copy-done.2
  68.7 0.0 copy-done.4
  68.7 2.9 %shard_map.123 = (f32[32,20,128]{2,1,0:T(8,128)S(1)}, f32[824,128]{1,0:T(8,128)S(1)}) custom-call(f32[16,5,128]{2,1,0:T(8,128)S(1)} %all_to_all.26.sums.r_2_, f32[512,128]{1,0:T(8,128)S(1)} %copy-done.4, f32[7,128]{1,0:T(8,128)S(1)} %maximum_bitcast_fusion.consts.r_4_, f32[816,128]{1,0:T(8,128)S(1)} %get-tuple-element.38.s1, ...), custom_call_target="tpu_custom_call" | custom-call | flops 1000000000 | bytes 4194304 | tf_op jit(solution)/shard_map/pallas_call | solution.py:350
  71.6 17.0 %all_to_all.27.parts = f32[32,20,128]{2,1,0:T(8,128)S(1)} all-to-all(f32[32,20,128]{2,1,0:T(8,128)S(1)} %get-tuple-element.40), channel_id=1, replica_groups=mesh['y'=4,'xl'=2,'c'=2,'z'=16,'xh'=2] {'y','xl','xh','c'}, dimensions={0} | all-to-all | bytes 655360 | tf_op jit(solution)/shard_map/all_to_all | solution.py:382
  88.6 0.1 shard_map.124
  88.7 15.7 %all_to_all.28.r_0_ = f32[16,23,128]{2,1,0:T(8,128)S(1)} all-to-all(f32[16,23,128]{2,1,0:T(8,128)S(1)} %shard_map.124), channel_id=1, replica_groups=mesh['y'=4,'xl'=2,'c'=2,'z'=16,'xh'=2] {'z'}, dimensions={0} | all-to-all | bytes 376832 | tf_op jit(solution)/shard_map/all_to_all | solution.py:382
  104.4 12.1 %all_to_all.29.mine = f32[16,56,128]{2,1,0:T(8,128)S(1)} all-to-all(f32[16,56,128]{2,1,0:T(8,128)S(1)} %shard_map.125), channel_id=1, replica_groups=mesh['y'=4,'xl'=2,'c'=2,'z'=16,'xh'=2] {'y','xl','xh'}, dimensions={0} | all-to-all | bytes 917504 | tf_op jit(solution)/shard_map/all_to_all | solution.py:382
  116.5 6.5 %collective-permute-start.5 = (f32[16,56,128]{2,1,0:T(8,128)S(1)}, f32[16,56,128]{2,1,0:T(8,128)S(1)}, u32[]{:S(2)}, u32[]{:S(2)}) collective-permute-start(f32[16,56,128]{2,1,0:T(8,128)S(1)} %all_to_all.29.mine), channel_id=1, source_target_pairs={{0,32},{32,0},{1,33},{33,1},{2,34},{34,2},{3,35},{35,3},{4,36},{36... | collective-permute-start | bytes 1376264 | tf_op jit(solution)/shard_map/ppermute | solution.py:417
  123.1 1.9 %shard_map.126 = (f32[15,45,69]{2,1,0:T(8,128)}, f32[512,128]{1,0:T(8,128)}, f32[128,128]{1,0:T(8,128)S(1)}, f32[1,128]{1,0:T(1,128)}) custom-call(f32[824,128]{1,0:T(8,128)S(1)} %get-tuple-element.42.r_0_, bf16[3,384,256]{2,1,0:T(8,128)(2,1)S(1)} %get-tuple-element.43.r_1_, f32[16,5,128]{2,1,0:T(8,128)S(1)} %all_to_all.26.sums.r_2_, ...), custom_call_target="tpu_custom_call" | custom-call | flops 1000000000 | bytes 4194304 | tf_op jit(solution)/shard_map/pallas_call | solution.py:350
  125.0 0.0 collective-permute-done.5.other
  125.0 1.0 shard_map.127
  (9 shorter events, 0.2 us)
Async XLA Ops:
  0.6 10.6 %copy-start = (f32[69,15,45]{0,2,1:T(8,128)S(1)}, f32[69,15,45]{0,2,1:T(8,128)}, u32[]{:S(2)}) copy-start(f32[69,15,45]{0,2,1:T(8,128)} %param.7) | copy-start | bytes 558904
  0.7 10.6 %copy-start.5 = (f32[512]{0:T(512)S(1)}, f32[512]{0:T(512)}, u32[]{:S(2)}) copy-start(f32[512]{0:T(512)} %param.13) | copy-start | bytes 6148
  0.7 10.6 %copy-start.6 = (f32[128]{0:T(128)S(1)}, f32[128]{0:T(128)}, u32[]{:S(2)}) copy-start(f32[128]{0:T(128)} %param.11) | copy-start | bytes 1540
  0.7 10.6 %copy-start.7 = (f32[128]{0:T(128)S(1)}, f32[128]{0:T(128)}, u32[]{:S(2)}) copy-start(f32[128]{0:T(128)} %param.9) | copy-start | bytes 1540
  0.7 24.0 %copy-start.3 = (f32[9,128,69]{1,2,0:T(8,128)S(1)}, f32[9,128,69]{1,2,0:T(8,128)}, u32[]{:S(2)}) copy-start(f32[9,128,69]{1,2,0:T(8,128)} %param.8) | copy-start | bytes 953860
  1.7 9.6 %collective-permute-start.1 = (f32[4,45,69]{2,1,0:T(8,128)S(1)}, f32[4,45,69]{2,1,0:T(8,128)S(1)}, u32[]{:S(2)}, u32[]{:S(2)}) collective-permute-start(f32[4,45,69]{2,1,0:T(8,128)S(1)} %get-tuple-element.54), channel_id=1, source_target_pairs={{32,64},{96,128},{160,192},{224,256},{288,320},{352,384},{416,448}... | collective-permute-start | bytes 149048 | tf_op jit(solution)/shard_map/ppermute | solution.py:397
  6.2 5.9 %collective-permute-start = (f32[4,45,69]{2,1,0:T(8,128)S(1)}, f32[4,45,69]{2,1,0:T(8,128)S(1)}, u32[]{:S(2)}, u32[]{:S(2)}) collective-permute-start(f32[4,45,69]{2,1,0:T(8,128)S(1)} %get-tuple-element.55), channel_id=1, source_target_pairs={{0,32},{64,96},{128,160},{192,224},{256,288},{320,352},{384,416},{... | collective-permute-start | bytes 149048 | tf_op jit(solution)/shard_map/ppermute | solution.py:396
  12.1 15.2 %collective-permute-start.2 = (f32[23,4,69]{2,1,0:T(4,128)S(1)}, f32[23,4,69]{2,1,0:T(4,128)S(1)}, u32[]{:S(2)}, u32[]{:S(2)}) collective-permute-start(f32[23,4,69]{2,1,0:T(4,128)S(1)} %pad_maximum_fusion), channel_id=1, source_target_pairs={{1,2},{3,4},{5,6},{7,8},{9,10},{11,12},{13,14},{15,16},{17,18},{19... | collective-permute-start | bytes 76184 | tf_op jit(solution)/shard_map/ppermute | solution.py:402
  22.8 6.3 %collective-permute-start.3 = (f32[23,4,69]{2,1,0:T(4,128)S(1)}, f32[23,4,69]{2,1,0:T(4,128)S(1)}, u32[]{:S(2)}, u32[]{:S(2)}) collective-permute-start(f32[23,4,69]{2,1,0:T(4,128)S(1)} %pad_maximum_fusion.1), channel_id=1, source_target_pairs={{0,1},{2,3},{4,5},{6,7},{8,9},{10,11},{12,13},{14,15},{16,17},{18,... | collective-permute-start | bytes 76184 | tf_op jit(solution)/shard_map/ppermute | solution.py:403
  24.7 1.1 copy-start.1
  32.6 4.7 %collective-permute-start.4 = (f32[584,128]{1,0:T(8,128)S(1)}, f32[584,128]{1,0:T(8,128)S(1)}, u32[]{:S(2)}, u32[]{:S(2)}) collective-permute-start(f32[584,128]{1,0:T(8,128)S(1)} %get-tuple-element.36), channel_id=1, source_target_pairs={{0,32},{32,0},{1,33},{33,1},{2,34},{34,2},{3,35},{35,3},{4,36},{36... | collective-permute-start | bytes 897032 | tf_op jit(solution)/shard_map/ppermute | solution.py:417
  37.3 31.4 %copy-start.2 = (f32[9,128,128]{2,1,0:T(8,128)S(1)}, f32[9,128,128]{2,1,0:T(8,128)}, u32[]{:S(2)}) copy-start(f32[9,128,128]{2,1,0:T(8,128)} %w_second.3) | copy-start | bytes 1769476
  50.3 18.4 %copy-start.4 = (f32[512,128]{1,0:T(8,128)S(1)}, f32[512,128]{1,0:T(8,128)}, u32[]{:S(2)}) copy-start(f32[512,128]{1,0:T(8,128)} %r_3_.1) | copy-start | bytes 786436
  116.5 8.4 %collective-permute-start.5 = (f32[16,56,128]{2,1,0:T(8,128)S(1)}, f32[16,56,128]{2,1,0:T(8,128)S(1)}, u32[]{:S(2)}, u32[]{:S(2)}) collective-permute-start(f32[16,56,128]{2,1,0:T(8,128)S(1)} %all_to_all.29.mine), channel_id=1, source_target_pairs={{0,32},{32,0},{1,33},{33,1},{2,34},{34,2},{3,35},{35,3},{4,36},{36... | collective-permute-start | bytes 1376264 | tf_op jit(solution)/shard_map/ppermute | solution.py:417

commit v8 on v7

--- a/solution.py
+++ b/solution.py
@@ -21,6 +21,7 @@
 ROWS, COLS, CIN = 15, 45, 69
 SHORT = 48
 NARROW = 16
+PAIRS = 46
 WINDOW = 16 * SHORT
 NX, N1, N2, N3 = 23 * PITCH, 21 * PITCH, 19 * PITCH, 17 * SHORT
 
@@ -118,6 +119,36 @@
     hi, lo = split(block)
     weight[a, b * LANES : (b + 1) * LANES, :LANES] = hi
     weight[a, b * LANES : (b + 1) * LANES, LANES:] = lo
+
+
+def pack_kernel(core, half, own, outer, inner, far, near, strip):
+    upper, west = core[0] == 0, half[0] == 0
+    lane = lax.broadcasted_iota(jnp.int32, (PAIRS, LANES), 1)
+    strip[...] = jnp.zeros_like(strip)
+    for out, first in ((far, True), (near, False)):
+        for i in range(ROWS + 8):
+            left, right = slice(0, 4), slice(COLS - 4, COLS)
+            if not first:
+                left, right = right, left
+            if 4 <= i < ROWS + 4:
+                cells = jnp.where(west, own[i - 4, left], own[i - 4, right])
+            else:
+                k = i if i < 4 else i - ROWS - 4
+                a, b = (outer, inner) if i < 4 else (inner, outer)
+                cells = jnp.where(upper, jnp.where(west, a[k, left], a[k, right]), jnp.where(west, b[k, left], b[k, right]))
+            strip[4 * i : 4 * i + 4, :CIN] = cells
+        moved = pltpu.roll(strip[...], LANES // 2, 1)
+        out[:PAIRS, :] = jnp.where(lane < LANES // 2, strip[:PAIRS, :], moved[PAIRS : 2 * PAIRS])
+        out[PAIRS : PAIRS + 2, :] = jnp.zeros((2, LANES), F32)
+        out[PAIRS + 2 :, :] = moved.T[:8]
+
+
+def unpack(packed, block):
+    block[:8, :] = packed[PAIRS + 2 :, :]
+    last = pltpu.roll(block[...].T, LANES // 2, 1)[: 2 * PAIRS]
+    most = jnp.concatenate([packed[:PAIRS, :], pltpu.roll(packed[:PAIRS, :], LANES // 2, 1)], axis=0)
+    lane = lax.broadcasted_iota(jnp.int32, (2 * PAIRS, LANES), 1)
+    return jnp.where(lane < LANES // 2, most, last)
 
 
 def activate(h, inside):
@@ -159,7 +190,7 @@
         store_weight(w1_back, t, padded_rows(pad_back, w_first[8 - t]).T)
 
 
-def forward_kernel(core, half, consts, centre, a1_part, slopes_part, outer, inner, w1, w2, cells, a1, s1, s2, small, send, edge, high, low, high1, low1, high2, low2):
+def forward_kernel(core, half, consts, centre, a1_part, slopes_part, outer, inner, w1, w2, cells, a1, s1, s2, small, send, edge, block, strip, high, low, high1, low1, high2, low2):
     west = half[0] == 0
     b1, b2 = consts[0:1, :], consts[1:2, :]
     weights = [consts[6:7, i : i + 1] for i in range(ROWS + 6)]
@@ -169,18 +200,22 @@
         s1[i * SHORT : (i + 1) * SHORT, :] = slopes_part[r : r + SHORT, :]
     cells[...] = centre[3 * PITCH : 21 * PITCH + 8, :]
     edge[...] = jnp.zeros_like(edge)
+    block[...] = jnp.zeros_like(block)
+    far = unpack(outer, block)
+    near = unpack(inner, block)
+    strip[0] = jnp.where(west, far, near)
+    strip[1] = jnp.where(west, near, far)
     for i in range(ROWS + 8):
         r, q = i * PITCH, i * NARROW
-        before = jnp.where(west, outer[i], inner[i])
-        after = jnp.where(west, inner[i], outer[i])
-        edge[q : q + 4, :CIN] = before
+        before, after = strip[0, 4 * i : 4 * i + 4], strip[1, 4 * i : 4 * i + 4]
+        edge[q : q + 4, :] = before
         edge[q + 4 : q + 6, :] = centre[r + 8 : r + 10, :]
         edge[q + 8 : q + 10, :] = centre[r + 6 + COLS : r + 8 + COLS, :]
-        edge[q + 10 : q + 14, :CIN] = after
+        edge[q + 10 : q + 14, :] = after
         if 3 <= i < 21:
             r = (i - 3) * PITCH
-            cells[r + 4 : r + 8, :CIN] = before
-            cells[r + 8 + COLS : r + 12 + COLS, :CIN] = after
+            cells[r + 4 : r + 8, :] = before
+            cells[r + 8 + COLS : r + 12 + COLS, :] = after
     spread_packed(edge, high1, low1, ROWS + 8, width=NARROW, pitch=NARROW)
     acc = convolve(high1, low1, w1, 0, ROWS + 6, NARROW)
     for i in range(ROWS + 6):
@@ -395,13 +430,12 @@
     core, half = lax.axis_index("c"), lax.axis_index("xh")
     inner = lax.ppermute(lax.dynamic_slice_in_dim(own, (1 - core) * (rows - 4), 4, 0), LAT, near_pairs(n_lat))
     outer = lax.ppermute(lax.dynamic_slice_in_dim(own, core * (rows - 4), 4, 0), LAT, far_pairs(n_lat, False))
-    strips = []
-    for start in (half * (cols - 4), (1 - half) * (cols - 4)):
-        a, b, c = [lax.dynamic_slice_in_dim(v, start, 4, 1) for v in (outer, own, inner)]
-        strips.append(jnp.concatenate([jnp.where(core == 0, a, c), b, jnp.where(core == 0, c, a)], axis=0))
+    core, half = core.astype(jnp.int32).reshape(1), half.astype(jnp.int32).reshape(1)
+    strips = call(pack_kernel, [(PAIRS + 10, LANES)] * 2, [((LANES, LANES), F32)], 10**6, smem=(0, 1))(
+        core, half, own, outer, inner
+    )
     outer_strip = lax.ppermute(strips[0], LON, far_pairs(n_lon, True))
     inner_strip = lax.ppermute(strips[1], LON, near_pairs(n_lon))
-    core, half = core.astype(jnp.int32).reshape(1), half.astype(jnp.int32).reshape(1)
     w_first = w_first.transpose(0, 2, 1)
     weight = ((3, 3 * LANES, 2 * LANES), BF16)
     packed = ((3, 2 * LANES, 2 * LANES), BF16)
@@ -418,7 +452,7 @@
     x, a1, s1, s2, small, send = call(
         forward_kernel,
         [(18 * PITCH + 8, LANES), (N1 + 8, LANES), (N3, LANES), (N2 + 8, LANES), (2, LANES), (HALF + 8, LANES)],
-        [((23 * NARROW + 8, LANES), F32)]
+        [((23 * NARROW + 8, LANES), F32), ((LANES, LANES), F32), ((2, 2 * PAIRS, LANES), F32)]
         + pair(N1)
         + pair(23 * NARROW, 2 * LANES)
         + pair(18 * SHORT),

time: 127 us -> 127 us (level)
    pallas_call x10 -> x11, Pallas kernels: 11.9 us -> 12.2 us  [run(): pl.pallas_call(kernel, out_shape=[jax.ShapeDtypeStruct(s, d) for s, d in...]
  transfers between devices with their start and end apart: 6 -> 6, of which waited for: 3 -> 3; matrix products, arithmetic and copies ran while one was open for 0% -> 1% of each run, Pallas kernels for 3% -> 3%
where the time goes in v8:
time: 127 us; the launch traced here: 126 us
  blocking collectives  76.1 us (60%)
  starting transfers between devices  32 us (25%)
  Pallas kernels  12.2 us (10%)
  waiting for transfers between devices  2.05 us (2%)
  local copies, waits for them, and re-layouts  2.02 us (2%)
    all_to_all x5, blocking collectives, swap(): return lax.all_to_all(pieces, axes, 0, 0, tiled=True)  76.1 us
    pallas_call x11, Pallas kernels, run(): pl.pallas_call(kernel, out_shape=[jax.ShapeDtypeStruct(s, d) for s, d in...  12.2 us
    ppermute x1, starting transfers between devices, body(): outer_strip = lax.ppermute(strips[0], LON, far_pairs(n_lon, True))  10.6 us
    ppermute x2, starting transfers between devices, body(): swap_cores = lambda v: lax.ppermute(v, 'c', [(0, 1), (1, 0)])  9.99 us
    ppermute x1, starting transfers between devices, body(): lax.ppermute(lax.dynamic_slice_in_dim(own, (1 - core) * (rows - 4), 4, 0)...  4.94 us
    ppermute x1, starting transfers between devices, body(): lax.ppermute(lax.dynamic_slice_in_dim(own, core * (rows - 4), 4, 0), LAT,...  4.51 us
  transfers between devices with their start and end apart: 6, of which 3 were waited for; matrix products, arithmetic and copies ran while one was open for 1% of the time, Pallas kernels for 3%

profile of v8, /device:TPU:1, one launch (start us, length us, event | category | flops | bytes accessed | tf_op | source)
XLA Modules:
  0.0 125.9 jit_solution(6315049532067672869)
XLA Ops:
  0.6 0.0 copy-start
  0.6 0.0 copy-start.1
  0.7 1.0 dynamic-slice_bitcast_fusion
  1.7 4.5 %collective-permute-start.1 = (f32[4,45,69]{2,1,0:T(8,128)S(1)}, f32[4,45,69]{2,1,0:T(8,128)S(1)}, u32[]{:S(2)}, u32[]{:S(2)}) collective-permute-start(f32[4,45,69]{2,1,0:T(8,128)S(1)} %get-tuple-element.56), channel_id=1, source_target_pairs={{32,64},{96,128},{160,192},{224,256},{288,320},{352,384},{416,448}... | collective-permute-start | bytes 149048 | tf_op jit(solution)/shard_map/ppermute | solution.py:432
  6.2 4.9 %collective-permute-start = (f32[4,45,69]{2,1,0:T(8,128)S(1)}, f32[4,45,69]{2,1,0:T(8,128)S(1)}, u32[]{:S(2)}, u32[]{:S(2)}) collective-permute-start(f32[4,45,69]{2,1,0:T(8,128)S(1)} %get-tuple-element.57), channel_id=1, source_target_pairs={{0,32},{64,96},{128,160},{192,224},{256,288},{320,352},{384,416},{... | collective-permute-start | bytes 149048 | tf_op jit(solution)/shard_map/ppermute | solution.py:431
  11.2 0.7 maximum_bitcast_fusion.consts.r_4_
  11.9 0.0 collective-permute-done.1.outer
  11.9 0.1 collective-permute-done.inner
  12.1 0.0 copy-done
  12.1 0.2 shard_map.119
  12.3 10.6 %collective-permute-start.2 = (f32[56,128]{1,0:T(8,128)S(1)}, f32[56,128]{1,0:T(8,128)S(1)}, u32[]{:S(2)}, u32[]{:S(2)}) collective-permute-start(f32[56,128]{1,0:T(8,128)S(1)} %get-tuple-element.34), channel_id=1, source_target_pairs={{1,2},{3,4},{5,6},{7,8},{9,10},{11,12},{13,14},{15,16},{17,18},{19... | collective-permute-start | bytes 86024 | tf_op jit(solution)/shard_map/ppermute | solution.py:437
  22.9 1.9 %collective-permute-start.3 = (f32[56,128]{1,0:T(8,128)S(1)}, f32[56,128]{1,0:T(8,128)S(1)}, u32[]{:S(2)}, u32[]{:S(2)}) collective-permute-start(f32[56,128]{1,0:T(8,128)S(1)} %get-tuple-element.35), channel_id=1, source_target_pairs={{0,1},{2,3},{4,5},{6,7},{8,9},{10,11},{12,13},{14,15},{16,17},{18,... | collective-permute-start | bytes 86024 | tf_op jit(solution)/shard_map/ppermute | solution.py:438
  24.8 0.0 copy-done.1
  24.8 0.0 copy-start.2
  24.8 1.0 copy-done.2
  25.8 1.6 %shard_map.118 = (f32[1480,128]{1,0:T(8,128)S(1)}, f32[1352,128]{1,0:T(8,128)S(1)}, f32[1344,128]{1,0:T(8,128)S(1)}, bf16[3,256,256]{2,1,0:T(8,128)(2,1)S(1)}, b...) custom-call(s32[1]{0:T(128)} %bitcast.core, f32[7,128]{1,0:T(8,128)S(1)} %maximum_bitcast_fusion.consts.r_4_, ...), custom_call_target="tpu_custom_call" | custom-call | flops 1000000000 | bytes 4194304 | tf_op jit(solution)/shard_map/pallas_call | solution.py:385
  27.4 0.0 collective-permute-done.2.outer
  27.4 1.6 %collective-permute-done.3.inner = f32[56,128]{1,0:T(8,128)S(1)} collective-permute-done((f32[56,128]{1,0:T(8,128)S(1)}, f32[56,128]{1,0:T(8,128)S(1)}, u32[]{:S(2)}, u32[]{:S(2)}) %collective-permute-start.3) | collective-permute-done | bytes 28704 | tf_op jit(solution)/shard_map/ppermute | solution.py:438
  29.0 3.6 %shard_map.120 = (f32[1160,128]{1,0:T(8,128)S(1)}, f32[1352,128]{1,0:T(8,128)S(1)}, f32[816,128]{1,0:T(8,128)S(1)}, f32[1224,128]{1,0:T(8,128)S(1)}, f32[2,128]{1,0:T(2,128)S(1)}, /*index=5*/f32[584,128]{1,0:T(8,128)S(1)}) custom-call(s32[1]{0:T(128)} %bitcast.core, s32[1]{0:T(128)} %bitcast.1.half, f32[7,128]{1,0:T(8,128)S(1)} %maximum_bitcast_fusion.consts.r_4_, ...), custom_call_target="tpu_custom_call" | custom-call | flops 1000000000 | bytes 4194304 | tf_op jit(solution)/shard_map/pallas_call | solution.py:385
  32.6 3.5 %collective-permute-start.4 = (f32[584,128]{1,0:T(8,128)S(1)}, f32[584,128]{1,0:T(8,128)S(1)}, u32[]{:S(2)}, u32[]{:S(2)}) collective-permute-start(f32[584,128]{1,0:T(8,128)S(1)} %get-tuple-element.40), channel_id=1, source_target_pairs={{0,32},{32,0},{1,33},{33,1},{2,34},{34,2},{3,35},{35,3},{4,36},{36... | collective-permute-start | bytes 897032 | tf_op jit(solution)/shard_map/ppermute | solution.py:451
  36.1 0.9 shard_map.121.own
  37.0 0.3 collective-permute-done.4.other
  37.3 13.0 %all_to_all.25.parts = f32[16,38,128]{2,1,0:T(8,128)S(1)} all-to-all(f32[16,38,128]{2,1,0:T(8,128)S(1)} %shard_map.122), channel_id=1, replica_groups=mesh['y'=4,'xl'=2,'c'=2,'z'=16,'xh'=2] {'y','xl','xh'}, dimensions={0} | all-to-all | bytes 622592 | tf_op jit(solution)/shard_map/all_to_all | solution.py:417
  50.2 0.0 copy-start.3
  50.3 18.3 %all_to_all.26.sums.r_2_ = f32[16,5,128]{2,1,0:T(8,128)S(1)} all-to-all(f32[16,5,128]{2,1,0:T(8,128)S(1)} %shard_map.123), channel_id=1, replica_groups=mesh['y'=4,'xl'=2,'c'=2,'z'=16,'xh'=2] {'z'}, dimensions={0} | all-to-all | bytes 81920 | tf_op jit(solution)/shard_map/all_to_all | solution.py:417
  68.6 0.0 copy-done.3
  68.6 2.9 %shard_map.124 = (f32[32,20,128]{2,1,0:T(8,128)S(1)}, f32[824,128]{1,0:T(8,128)S(1)}) custom-call(f32[16,5,128]{2,1,0:T(8,128)S(1)} %all_to_all.26.sums.r_2_, f32[512,128]{1,0:T(8,128)S(1)} %copy-done.3, f32[7,128]{1,0:T(8,128)S(1)} %maximum_bitcast_fusion.consts.r_4_, f32[816,128]{1,0:T(8,128)S(1)} %get-tuple-element.42.s1, ...), custom_call_target="tpu_custom_call" | custom-call | flops 1000000000 | bytes 4194304 | tf_op jit(solution)/shard_map/pallas_call | solution.py:385
  71.5 17.0 %all_to_all.27.parts = f32[32,20,128]{2,1,0:T(8,128)S(1)} all-to-all(f32[32,20,128]{2,1,0:T(8,128)S(1)} %get-tuple-element.44), channel_id=1, replica_groups=mesh['y'=4,'xl'=2,'c'=2,'z'=16,'xh'=2] {'y','xl','xh','c'}, dimensions={0} | all-to-all | bytes 655360 | tf_op jit(solution)/shard_map/all_to_all | solution.py:417
  88.5 0.1 shard_map.125
  88.6 15.7 %all_to_all.28.r_0_ = f32[16,23,128]{2,1,0:T(8,128)S(1)} all-to-all(f32[16,23,128]{2,1,0:T(8,128)S(1)} %shard_map.125), channel_id=1, replica_groups=mesh['y'=4,'xl'=2,'c'=2,'z'=16,'xh'=2] {'z'}, dimensions={0} | all-to-all | bytes 376832 | tf_op jit(solution)/shard_map/all_to_all | solution.py:417
  104.3 12.1 %all_to_all.29.mine = f32[16,56,128]{2,1,0:T(8,128)S(1)} all-to-all(f32[16,56,128]{2,1,0:T(8,128)S(1)} %shard_map.126), channel_id=1, replica_groups=mesh['y'=4,'xl'=2,'c'=2,'z'=16,'xh'=2] {'y','xl','xh'}, dimensions={0} | all-to-all | bytes 917504 | tf_op jit(solution)/shard_map/all_to_all | solution.py:417
  116.4 6.5 %collective-permute-start.5 = (f32[16,56,128]{2,1,0:T(8,128)S(1)}, f32[16,56,128]{2,1,0:T(8,128)S(1)}, u32[]{:S(2)}, u32[]{:S(2)}) collective-permute-start(f32[16,56,128]{2,1,0:T(8,128)S(1)} %all_to_all.29.mine), channel_id=1, source_target_pairs={{0,32},{32,0},{1,33},{33,1},{2,34},{34,2},{3,35},{35,3},{4,36},{36... | collective-permute-start | bytes 1376264 | tf_op jit(solution)/shard_map/ppermute | solution.py:451
  122.9 1.9 %shard_map.127 = (f32[15,45,69]{2,1,0:T(8,128)}, f32[512,128]{1,0:T(8,128)}, f32[128,128]{1,0:T(8,128)S(1)}, f32[1,128]{1,0:T(1,128)}) custom-call(f32[824,128]{1,0:T(8,128)S(1)} %get-tuple-element.46.r_0_, bf16[3,384,256]{2,1,0:T(8,128)(2,1)S(1)} %get-tuple-element.47.r_1_, f32[16,5,128]{2,1,0:T(8,128)S(1)} %all_to_all.26.sums.r_2_, ...), custom_call_target="tpu_custom_call" | custom-call | flops 1000000000 | bytes 4194304 | tf_op jit(solution)/shard_map/pallas_call | solution.py:385
  124.9 0.0 collective-permute-done.5.other
  124.9 1.0 shard_map.128
  (4 shorter events, 0.2 us)
Async XLA Ops:
  0.6 11.5 %copy-start = (f32[69,15,45]{0,2,1:T(8,128)S(1)}, f32[69,15,45]{0,2,1:T(8,128)}, u32[]{:S(2)}) copy-start(f32[69,15,45]{0,2,1:T(8,128)} %param.7) | copy-start | bytes 558904
  0.6 24.2 %copy-start.1 = (f32[9,128,128]{2,1,0:T(8,128)S(1)}, f32[9,128,128]{2,1,0:T(8,128)}, u32[]{:S(2)}) copy-start(f32[9,128,128]{2,1,0:T(8,128)} %w_second.3) | copy-start | bytes 1769476
  1.7 10.2 %collective-permute-start.1 = (f32[4,45,69]{2,1,0:T(8,128)S(1)}, f32[4,45,69]{2,1,0:T(8,128)S(1)}, u32[]{:S(2)}, u32[]{:S(2)}) collective-permute-start(f32[4,45,69]{2,1,0:T(8,128)S(1)} %get-tuple-element.56), channel_id=1, source_target_pairs={{32,64},{96,128},{160,192},{224,256},{288,320},{352,384},{416,448}... | collective-permute-start | bytes 149048 | tf_op jit(solution)/shard_map/ppermute | solution.py:432
  6.2 5.9 %collective-permute-start = (f32[4,45,69]{2,1,0:T(8,128)S(1)}, f32[4,45,69]{2,1,0:T(8,128)S(1)}, u32[]{:S(2)}, u32[]{:S(2)}) collective-permute-start(f32[4,45,69]{2,1,0:T(8,128)S(1)} %get-tuple-element.57), channel_id=1, source_target_pairs={{0,32},{64,96},{128,160},{192,224},{256,288},{320,352},{384,416},{... | collective-permute-start | bytes 149048 | tf_op jit(solution)/shard_map/ppermute | solution.py:431
  12.3 15.1 %collective-permute-start.2 = (f32[56,128]{1,0:T(8,128)S(1)}, f32[56,128]{1,0:T(8,128)S(1)}, u32[]{:S(2)}, u32[]{:S(2)}) collective-permute-start(f32[56,128]{1,0:T(8,128)S(1)} %get-tuple-element.34), channel_id=1, source_target_pairs={{1,2},{3,4},{5,6},{7,8},{9,10},{11,12},{13,14},{15,16},{17,18},{19... | collective-permute-start | bytes 86024 | tf_op jit(solution)/shard_map/ppermute | solution.py:437
  22.9 6.1 %collective-permute-start.3 = (f32[56,128]{1,0:T(8,128)S(1)}, f32[56,128]{1,0:T(8,128)S(1)}, u32[]{:S(2)}, u32[]{:S(2)}) collective-permute-start(f32[56,128]{1,0:T(8,128)S(1)} %get-tuple-element.35), channel_id=1, source_target_pairs={{0,1},{2,3},{4,5},{6,7},{8,9},{10,11},{12,13},{14,15},{16,17},{18,... | collective-permute-start | bytes 86024 | tf_op jit(solution)/shard_map/ppermute | solution.py:438
  24.8 1.0 copy-start.2
  32.6 4.7 %collective-permute-start.4 = (f32[584,128]{1,0:T(8,128)S(1)}, f32[584,128]{1,0:T(8,128)S(1)}, u32[]{:S(2)}, u32[]{:S(2)}) collective-permute-start(f32[584,128]{1,0:T(8,128)S(1)} %get-tuple-element.40), channel_id=1, source_target_pairs={{0,32},{32,0},{1,33},{33,1},{2,34},{34,2},{3,35},{35,3},{4,36},{36... | collective-permute-start | bytes 897032 | tf_op jit(solution)/shard_map/ppermute | solution.py:451
  50.2 18.3 %copy-start.3 = (f32[512,128]{1,0:T(8,128)S(1)}, f32[512,128]{1,0:T(8,128)}, u32[]{:S(2)}) copy-start(f32[512,128]{1,0:T(8,128)} %r_3_.1) | copy-start | bytes 786436
  116.4 8.4 %collective-permute-start.5 = (f32[16,56,128]{2,1,0:T(8,128)S(1)}, f32[16,56,128]{2,1,0:T(8,128)S(1)}, u32[]{:S(2)}, u32[]{:S(2)}) collective-permute-start(f32[16,56,128]{2,1,0:T(8,128)S(1)} %all_to_all.29.mine), channel_id=1, source_target_pairs={{0,32},{32,0},{1,33},{33,1},{2,34},{34,2},{3,35},{35,3},{4,36},{36... | collective-permute-start | bytes 1376264 | tf_op jit(solution)/shard_map/ppermute | solution.py:451
